TPU v7x, 32 devices: a whole 2x2x4 slice. The times are simulated.
32 devices in a mesh: rad: 8 (over z, x), src: 4 (over y, core).
Axes of the slice: x: 2, y: 2, z: 4, core: 2. Of those that a mesh axis runs over, the one named last changes fastest.
Arguments:
- slab: bfloat16 [1024, 256, 512], P('rad', 'src'), may hold values from -6 to 6
- radius_factor: bfloat16 [1024, 256], P('rad'), may hold values from -2.5 to 2.5
- height_factor: bfloat16 [512, 256], P('src'), may hold values from -2.5 to 2.5
- source_factor: bfloat16 [256, 256], P('src'), may hold values from -2.5 to 2.5
Outputs:
- grad_radius: float32 [1024, 256], P('rad')
- grad_height: float32 [512, 256], P('src')
- grad_source: float32 [256, 256], P('src')
All inputs are finite; a program needn't handle non-finite values.
Results may differ from a plain program's by a relative error of at most 0.00046.
Values may be sent and summed in bfloat16 or wider, within the bound.
No kernel may reach another device: no remote copies, remote signals or barrier semaphores. Data moves between devices by JAX's collectives and lax.ppermute only.
A program may use at most 128 MiB of HBM per device.

v0:
```python
import jax
import jax.numpy as jnp
from jax import lax
from jax.sharding import PartitionSpec as P


def per_device(slab, radius_factor, height_factor, source_factor):
    heights = lax.all_gather(height_factor, "src", axis=0, tiled=True)
    r_rows, s_rows, width = slab.shape
    rank = heights.shape[1]
    n_rad = lax.axis_size("rad")
    n_src = lax.axis_size("src")
    total_r = r_rows * n_rad
    total_s = s_rows * n_src
    src_f = source_factor.astype(jnp.float32)
    a_f = radius_factor.astype(jnp.float32)
    kr_bc = (
        (src_f[:, None, :] * heights.astype(jnp.float32)[None, :, :])
        .astype(jnp.bfloat16)
        .reshape(s_rows * width, rank)
    )
    flat = slab.reshape(r_rows, s_rows * width)
    rebuilt = lax.dot_general(
        radius_factor, kr_bc, (((1,), (1,)), ((), ())), preferred_element_type=jnp.float32
    )
    residual = (rebuilt - flat.astype(jnp.float32)).astype(jnp.bfloat16)
    err_rows = residual.reshape(r_rows * s_rows, width)
    projected = jnp.dot(err_rows, heights, preferred_element_type=jnp.float32).reshape(
        r_rows, s_rows, rank
    )
    part_a = jnp.einsum("rsk,sk->rk", projected, src_f, precision=lax.Precision.HIGHEST)
    part_c = jnp.einsum("rsk,rk->sk", projected, a_f, precision=lax.Precision.HIGHEST)
    grad_radius = lax.psum(part_a, "src") / jnp.sqrt(jnp.float32(total_s * width))
    grad_source = lax.psum(part_c, "rad") / jnp.sqrt(jnp.float32(total_r * width))
    kr_ac = (
        (a_f[:, None, :] * src_f[None, :, :]).astype(jnp.bfloat16).reshape(r_rows * s_rows, rank)
    )
    share = lax.psum_scatter(
        lax.dot_general(
            err_rows, kr_ac, (((0,), (0,)), ((), ())), preferred_element_type=jnp.float32
        ),
        "src",
        scatter_dimension=0,
        tiled=True,
    )
    own_rows = lax.psum(share, "rad")
    grad_height = own_rows / jnp.sqrt(jnp.float32(total_r * total_s))
    return (grad_radius, grad_height, grad_source)


def solution(mesh):
    return jax.shard_map(
        per_device,
        mesh=mesh,
        in_specs=(P("rad", "src", None), P("rad", None), P("src", None), P("src", None)),
        out_specs=(P("rad", None), P("src", None), P("src", None)),
        check_vma=False,
    )
```

profile of v0, /device:TPU:0, one launch (start us, length us, event | category | flops | bytes accessed | tf_op | source)
XLA Modules:
  0.0 227.9 jit_solution(6111362316032763185)
XLA Ops:
  7.2 0.0 reduce-scatter.2.cloned.1.call-start
  7.2 0.8 bitcast_convert_fusion.1
  8.1 0.0 copy-start.1
  8.1 0.0 copy-start
  8.1 14.7 %copy.9 = f32[128,64,512]{0,2,1:T(8,128)} copy(bf16[128,64,512]{2,1,0:T(8,128)(2,1)} %param.4) | data formatting | bytes 25165824 | tf_op jit(solution)/shard_map/convert_element_type | solution.py:26
  22.8 0.0 copy-done.1
  22.8 7.2 %all_gather.3 = bf16[512,256]{1,0:T(8,128)(2,1)S(1)} all-gather(bf16[128,256]{1,0:T(8,128)(2,1)S(1)} %copy-done.1), channel_id=1, replica_groups=mesh['rad'=8,'src'=4] {'src'}, dimensions={0}, use_global_device_ids=true | all-gather | bytes 327680 | tf_op jit(solution)/shard_map/all_gather | solution.py:8
  30.1 0.0 copy-done
  30.1 6.5 %multiply_convert_fusion = bf16[64,512,256]{2,1,0:T(8,128)(2,1)} fusion(f32[512,256]{1,0:T(8,128)S(1)} %convert_element_type.39, f32[64,256]{1,0:T(8,128)S(1)} %get-tuple-element.8), kind=kLoop, calls=%fused_computation.3 | loop fusion | flops 16777216 | bytes 17367040 | tf_op jit(solution)/shard_map/convert_element_type | solution.py:19
  36.6 16.4 %fusion.1 = bf16[128,32768]{0,1:T(8,128)(2,1)} fusion(f32[128,32768]{0,1:T(8,128)} %bitcast.31, bf16[32768,256]{1,0:T(8,128)(2,1)} %bitcast.32, bf16[128,256]{1,0:T(8,128)(2,1)S(1)} %copy-done), kind=kOutput, calls=%fused_computation.2 | convolution fusion | flops 2155872256 | bytes 42008576 | tf_op jit(solution)/shard_map/dot_general | solution.py:23
  52.9 11.9 %copy.11 = bf16[128,32768]{1,0:T(8,128)(2,1)} copy(bf16[128,32768]{0,1:T(8,128)(2,1)} %fusion.1) | data formatting | bytes 16777216 | tf_op jit(solution)/shard_map/convert_element_type | solution.py:26
  64.8 13.5 %reshape.37 = bf16[8192,512]{1,0:T(8,128)(2,1)} reshape(bf16[128,32768]{1,0:T(8,128)(2,1)} %copy.11) | data formatting | bytes 16777216 | tf_op jit(solution)/shard_map/reshape | solution.py:27
  78.3 1.6 multiply_convert_fusion.1
  79.9 6.6 %fusion.4 = f32[512,256]{1,0:T(8,128)} fusion(bf16[8192,512]{1,0:T(8,128)(2,1)} %reshape.37, bf16[8192,256]{1,0:T(8,128)(2,1)S(1)} %bitcast.33), kind=kOutput, calls=%fused_computation.14 | convolution fusion | flops 2147483648 | bytes 13107200 | tf_op jit(solution)/shard_map/dot_general | solution.py:39
  86.5 0.0 reduce-scatter.2.cloned.1.call-update
  86.6 0.0 all-reduce.4.cloned.1.call-start
  86.6 9.6 %multiply_reduce_fusion.1 = (f32[256,128]{0,1:T(8,128)}, f32[128,64,256]{2,0,1:T(8,128)}) fusion(f32[256,64]{0,1:T(8,128)S(1)} %get-tuple-element.7, bf16[128,64,512]{0,2,1:T(8,128)(2,1)} %bitcast.30, bf16[512,256]{1,0:T(8,128)(2,1)S(1)} %all_gather.3), kind=kOutput, calls=%fused_computation.5 | convolution fusion | flops 2151645184 | bytes 17235968 | tf_op jit(solution)/shard_map/dot_general | solution.py:28
  96.3 0.0 all-reduce.4.cloned.1.call-update
  96.3 0.0 all-reduce.6.cloned.1.call-start
  96.3 5.2 %multiply_reduce_fusion = f32[256,64]{0,1:T(8,128)} fusion(f32[128,64,256]{2,0,1:T(8,128)} %get-tuple-element.10, f32[256,128]{0,1:T(8,128)S(1)} %get-tuple-element.5), kind=kLoop, calls=%fused_computation.4 | loop fusion | flops 4177920 | bytes 8585216 | tf_op jit(solution)/shard_map/rsk,rk->sk/dot_general | solution.py:32
  101.6 8.1 %reduce-scatter.2.cloned.1.call-done = f32[128,256]{1,0:T(8,128)} async-done(((f32[512,256]{1,0:T(8,128)}), f32[128,256]{1,0:T(8,128)}) %reduce-scatter.2.cloned.1.call-update) | async-done | bytes 131088 | tf_op jit(solution)/shard_map/reduce_scatter | solution.py:38
  109.7 0.0 all-reduce.6.cloned.1.call-update
  109.7 34.4 %all-reduce.4.cloned.1.call-done = f32[128,256]{1,0:T(8,128)} async-done(((f32[128,256]{1,0:T(8,128)}), f32[128,256]{1,0:T(8,128)}) %all-reduce.4.cloned.1.call-update) | async-done | bytes 131088 | tf_op jit(solution)/shard_map/psum | solution.py:33
  144.1 1.6 broadcast_multiply_fusion.1
  145.7 72.7 %all-reduce.6.cloned.1.call-done = (f32[128,256]{1,0:T(8,128)}, f32[64,256]{1,0:T(8,128)}) async-done(((f32[128,256]{1,0:T(8,128)}, f32[64,256]{1,0:T(8,128)}), (f32[128,256]{1,0:T(8,128)}, f32[64,256]{1,0:T(8,128)})) %all-reduce.6.cloned.1.call-update) | async-done | bytes 196624 | tf_op jit(solution)/shard_map/psum | solution.py:46
  218.4 1.6 broadcast_multiply_fusion
  219.9 1.5 broadcast_multiply_fusion.2
  (2 shorter events, 0.1 us)
Async XLA Ops:
  7.2 102.5 %reduce-scatter.2.cloned.1.call-start = ((), (), s32[]{:S(2)}) async-start(), calls=%async_computation.2 | async-start | bytes 655360 | tf_op jit(solution)/shard_map/reduce_scatter | solution.py:38
  8.1 14.8 %copy-start.1 = (bf16[128,256]{1,0:T(8,128)(2,1)S(1)}, bf16[128,256]{1,0:T(8,128)(2,1)}, u32[]{:S(2)}) copy-start(bf16[128,256]{1,0:T(8,128)(2,1)} %param.6) | copy-start | bytes 196612
  8.1 22.0 %copy-start = (bf16[128,256]{1,0:T(8,128)(2,1)S(1)}, bf16[128,256]{1,0:T(8,128)(2,1)}, u32[]{:S(2)}) copy-start(bf16[128,256]{1,0:T(8,128)(2,1)} %param.5) | copy-start | bytes 196612
  86.6 57.5 %all-reduce.4.cloned.1.call-start = ((), (), s32[]{:S(2)}) async-start(), calls=%async_computation.1 | async-start | bytes 262144 | tf_op jit(solution)/shard_map/psum | solution.py:33
  96.3 122.1 %all-reduce.6.cloned.1.call-start = ((), (), s32[]{:S(2)}) async-start(), calls=%async_computation.3 | async-start | bytes 393216 | tf_op jit(solution)/shard_map/psum | solution.py:46
Sparse Core Ops, SparseCore 0:
  86.7 22.9 reduce-scatter.1
  112.7 31.4 all-reduce.3
  148.1 70.2 all-reduce.5
where the time goes:
time: 229 us; the launch traced here: 228 us
  waiting for transfers between devices  115 us (50%)
  local copies, waits for them, and re-layouts  40.1 us (18%)
  matrix products  32.6 us (14%)
  other arithmetic  18.8 us (8%)
  between operations  13.8 us (6%)
  blocking collectives  7.21 us (3%)
    psum x1, waiting for transfers between devices, per_device(): own_rows = lax.psum(share, 'rad')  72.7 us
    psum x1, waiting for transfers between devices, per_device(): lax.psum(part_a, 'src') / jnp.sqrt(jnp.float32(total_s * width))  34.4 us
    convert_element_type x2, local copies, waits for them, and re-layouts, per_device(): residual = (rebuilt - flat.astype(jnp.float32)).astype(jnp.bfloat16)  26.6 us
    dot_general x1, matrix products, per_device(): lax.dot_general(radius_factor, kr_bc, (((1,), (1,)), ((), ())), preferred...  16.4 us
    reshape x1, local copies, waits for them, and re-layouts, per_device(): err_rows = residual.reshape(r_rows * s_rows, width)  13.5 us
    dot_general x1, matrix products, per_device(): jnp.dot(err_rows, heights, preferred_element_type=jnp.float32)  9.65 us
    reduce_scatter x1, waiting for transfers between devices, per_device(): lax.psum_scatter(lax.dot_general(err_rows, kr_ac, (((0,), (0,)), ((), ())...  8.09 us
    all_gather x1, blocking collectives, per_device(): heights = lax.all_gather(height_factor, 'src', axis=0, tiled=True)  7.21 us
  transfers between devices with their start and end apart: 3, of which 3 were waited for; matrix products, arithmetic and copies ran while one was open for 7% of the time, Pallas kernels for 0%

commit v1 on v0

v1 whole, which is shorter than its diff:
```python
import functools

import jax
import jax.numpy as jnp
from jax import lax
from jax.experimental import pallas as pl
from jax.experimental.pallas import tpu as pltpu
from jax.sharding import PartitionSpec as P

F32 = jnp.float32
BF16 = jnp.bfloat16
F16 = jnp.float16
VMEM_LIMIT = 32 * 1024 * 1024
LANES = 128
TAIL = 16
TOP = 13.0
WHOLE = pl.BlockSpec(memory_space=pltpu.VMEM)


def inside(x):
    return pltpu.with_memory_space_constraint(x, pltpu.VMEM)


def after(x, *others):
    return lax.optimization_barrier((x, *others))[0]


def swap(x, axis, bit):
    return lax.ppermute(x, axis, [(i, i ^ bit) for i in range(lax.axis_size(axis))])


def call(body, outs, args, flops, resident=True, scratch=()):
    return pl.pallas_call(
        body,
        in_specs=[WHOLE] * len(args),
        out_specs=[WHOLE] * len(outs),
        out_shape=[pltpu.VMEM(shape, dtype) for shape, dtype in outs],
        scratch_shapes=scratch,
        compiler_params=pltpu.CompilerParams(vmem_limit_bytes=VMEM_LIMIT),
        cost_estimate=pl.CostEstimate(flops=flops, bytes_accessed=0, transcendentals=0),
    )(*[inside(a) if resident else a for a in args])


def gram(x):
    return lax.dot_general(x, x, (((0,), (0,)), ((), ())), preferred_element_type=F32)


def times(x, m):
    hi = m.astype(BF16)
    lo = (m - hi.astype(F32)).astype(BF16)
    return jnp.dot(x, hi, preferred_element_type=F32) + jnp.dot(x, lo, preferred_element_type=F32)


def prepare(a_ref, b_ref, c_ref, a_out, b_out, cb_out, ga_out):
    h_own = c_ref.shape[0]
    cb_out[0:h_own] = c_ref[...]
    cb_out[h_own:] = b_ref[...]
    a_out[...] = a_ref[...]
    b_out[...] = b_ref[...]
    ga_out[...] = gram(a_ref[...])


def height_terms(offsets, x_ref, a_ref, b_ref, g_ref):
    s_rows, rank = b_ref.shape
    r_rows = a_ref.shape[0]
    rows = r_rows * s_rows
    kr = (a_ref[...][:, None, :] * b_ref[...][None]).reshape(rows, rank)
    if offsets is None:
        x = x_ref[...]
    else:
        width = g_ref.shape[0] // len(offsets)
        me = lax.axis_index("src")
        x = jnp.concatenate(
            [x_ref[:, :, pl.ds(pl.multiple_of((me ^ o) * width, width), width)] for o in offsets], axis=2
        )
    g_ref[...] = lax.dot_general(
        x.reshape(rows, x.shape[2]), kr, (((0,), (0,)), ((), ())), preferred_element_type=F32
    )


def project(scales, n_src, x_ref, a_ref, b_ref, ga_ref, *refs):
    blocks, (pa_ref, ps_ref, ph_ref, heights) = refs[:n_src], refs[n_src:]
    s_rows, rank = b_ref.shape
    r_rows = a_ref.shape[0]
    h_own = blocks[0].shape[0] - s_rows
    me = lax.axis_index("src")
    for o, ref in enumerate(blocks):
        heights[pl.ds(pl.multiple_of((me ^ o) * h_own, h_own), h_own)] = ref[0:h_own]
    x = x_ref[...].reshape(r_rows * s_rows, x_ref.shape[2])
    proj = jnp.dot(x, heights[...], preferred_element_type=F32).reshape(r_rows, s_rows, rank)
    pa = (proj * b_ref[...].astype(F32)[None]).sum(1)
    ps = (proj * a_ref[...].astype(F32)[:, None, :]).sum(0)
    gb_own = gram(b_ref[...])
    gb = gb_own
    for ref in blocks[1:]:
        gb = gb + gram(ref[h_own:])
    gc = gram(heights[...])
    ga = ga_ref[...]
    to_radius, to_height, to_source = scales
    pa_ref[...] = (times(a_ref[...], gb_own * gc) - pa) * to_radius
    ps_ref[...] = (times(b_ref[...], ga * gc) - ps) * to_source
    ph_ref[...] = times(blocks[0][0:h_own], ga * gb) * to_height


def split(v_ref, h_ref, s_ref):
    h_own = h_ref.shape[0]
    h_ref[...] = v_ref[0:h_own]
    s_ref[...] = v_ref[h_own : h_own + s_ref.shape[0]]


def pack(v, e):
    rows = lax.broadcasted_iota(jnp.int32, v.shape, 0)
    return jnp.where(rows < v.shape[0] - TAIL, v * jnp.exp2(TOP - e), e).astype(F16)


def unpack(m):
    e = m[-1:].astype(F32)
    return m.astype(F32) * jnp.exp2(e - TOP), e


def per_device(slab, radius_factor, height_factor, source_factor):
    n_rad, n_src = lax.axis_size("rad"), lax.axis_size("src")
    r_rows, s_rows, width = slab.shape
    h_own, rank = height_factor.shape
    total_r, total_s = r_rows * n_rad, s_rows * n_src
    scales = (
        (total_s * width) ** -0.5,
        (total_r * total_s) ** -0.5,
        (total_r * width) ** -0.5,
    )
    work = 2 * r_rows * s_rows * width * rank
    src_bits = [1 << i for i in range(n_src.bit_length() - 1)]
    rad_bits = [1 << i for i in range(n_rad.bit_length() - 1)]

    a, b, cb, ga = call(
        prepare,
        [((r_rows, rank), BF16), ((s_rows, rank), BF16), ((h_own + s_rows, rank), BF16), ((rank, rank), F32)],
        (radius_factor, source_factor, height_factor),
        work // 2,
        resident=False,
    )
    blocks = {0: cb}
    for bit in reversed(src_bits):
        blocks[bit] = swap(cb, "src", bit)
    if h_own % LANES == 0:
        offsets = list(range(n_src))
        (g_away,) = call(
            functools.partial(height_terms, offsets[1::2]), [((width // 2, rank), F32)], (slab, a, b), work // 2
        )
        g_in = swap(g_away, "src", 1)
        ready = after(a, g_away, *[blocks[bit] for bit in src_bits])
        (g_keep,) = call(
            functools.partial(height_terms, offsets[0::2]), [((width // 2, rank), F32)], (slab, ready, b), work // 2
        )
    else:
        (g,) = call(functools.partial(height_terms, None), [((width, rank), F32)], (slab, a, b), work)
        me = lax.axis_index("src")
        g = jnp.take(g.reshape(n_src, h_own, rank), me ^ jnp.arange(n_src), axis=0)
        g_away, g_keep = (g[i::2].reshape(width // 2, rank) for i in (1, 0))
        g_in = swap(g_away, "src", 1)
    for o in range(1, n_src):
        if o not in blocks:
            low = o & -o
            blocks[o] = swap(after(blocks[o ^ low], g_away), "src", low)
    g = g_keep + g_in
    for bit in src_bits[1:-1]:
        g = g.reshape(-1, 2, h_own, rank)
        g = (g[:, 0] + swap(g[:, 1], "src", bit)).reshape(-1, rank)
    share_in = swap(g[h_own:], "src", src_bits[-1])
    pa, ps, ph = call(
        functools.partial(project, scales, n_src),
        [((r_rows, rank), F32), ((s_rows, rank), F32), ((h_own, rank), F32)],
        (slab, a, b, ga, *[blocks[o] for o in range(n_src)]),
        work,
        scratch=[pltpu.VMEM((width, rank), BF16)],
    )
    ph = ph - (g[:h_own] + share_in) * scales[1]
    v = jnp.concatenate([ph, ps, jnp.zeros((TAIL, rank), F32)], axis=0)
    top = jnp.max(jnp.abs(v), axis=0, keepdims=True)
    e = jnp.clip(jnp.ceil(jnp.log2(jnp.maximum(top, 1e-30))), -100.0, 100.0)
    bits = list(src_bits)
    for i, bit in enumerate(rad_bits):
        m = pack(v, e)
        if bits:
            pa, m = lax.optimization_barrier((pa, m))
            pa = pa + swap(pa, "src", bits.pop(0))
        other, e_other = unpack(swap(m, "rad", bit))
        v, e = unpack(m)
        v = v + other
        e = jnp.maximum(e, e_other) + 1.0
    for bit in bits:
        pa = pa + swap(pa, "src", bit)
    grad_height, grad_source = pl.pallas_call(
        split,
        in_specs=[WHOLE],
        out_specs=[WHOLE] * 2,
        out_shape=[jax.ShapeDtypeStruct((h_own, rank), F32), jax.ShapeDtypeStruct((s_rows, rank), F32)],
    )(inside(v))
    return pa, grad_height, grad_source


def solution(mesh):
    return jax.shard_map(
        per_device,
        mesh=mesh,
        in_specs=(P("rad", "src", None), P("rad", None), P("src", None), P("src", None)),
        out_specs=(P("rad", None), P("src", None), P("src", None)),
        check_vma=False,
    )
```

time: 229 us -> 38.7 us (0.17)
  waiting for transfers between devices: 115 us -> 10.9 us
  local copies, waits for them, and re-layouts: 40.1 us -> 5.9 us
  matrix products: 32.6 us -> 0 us
  other arithmetic: 18.8 us -> 1.32 us
  between operations: 13.8 us -> 0.77 us
  starting transfers between devices: 0.12 us -> 13.1 us
  blocking collectives: 7.21 us -> 0 us
  Pallas kernels: 0 us -> 6.39 us
    psum x2 -> x0, waiting for transfers between devices: 107 us -> none  [the longest x1 72.7 us: per_device(): own_rows = lax.psum(share, 'rad')]
    dot_general x3 -> x0, matrix products: 32.6 us -> none  [the longest x1 16.4 us: per_device(): lax.dot_general(radius_factor, kr_bc, (((1,), (1,)), ((), ())), preferred...]
    convert_element_type x2 -> x0, local copies, waits for them, and re-layouts: 26.6 us -> none  [per_device(): residual = (rebuilt - flat.astype(jnp.float32)).astype(jnp.bfloat16)]
    reshape x1 -> x0, local copies, waits for them, and re-layouts: 13.5 us -> none  [per_device(): err_rows = residual.reshape(r_rows * s_rows, width)]
    ppermute x0 -> x10, starting transfers between devices: none -> 13.1 us  [swap(): lax.ppermute(x, axis, [(i, i ^ bit) for i in range(lax.axis_size(axis))])]
    ppermute x0 -> x10, waiting for transfers between devices: none -> 10.9 us  [swap(): lax.ppermute(x, axis, [(i, i ^ bit) for i in range(lax.axis_size(axis))])]
    reduce_scatter x1 -> x0, waiting for transfers between devices: 8.09 us -> none  [per_device(): lax.psum_scatter(lax.dot_general(err_rows, kr_ac, (((0,), (0,)), ((), ())...]
    convert_element_type x3, other arithmetic: 8.14 us -> 0.34 us  [pack(): jnp.where(rows < v.shape[0] - TAIL, v * jnp.exp2(TOP - e), e).astype(F16)]
  transfers between devices with their start and end apart: 3 -> 10, of which waited for: 3 -> 5; matrix products, arithmetic and copies ran while one was open for 7% -> 3% of each run, Pallas kernels for 0% -> 11%
where the time goes in v1:
time: 38.7 us; the launch traced here: 38.4 us
  starting transfers between devices  13.1 us (34%)
  waiting for transfers between devices  10.9 us (28%)
  Pallas kernels  6.39 us (17%)
  local copies, waits for them, and re-layouts  5.9 us (15%)
  other arithmetic  1.32 us (3%)
  between operations  0.77 us (2%)
    ppermute x10, starting transfers between devices, swap(): lax.ppermute(x, axis, [(i, i ^ bit) for i in range(lax.axis_size(axis))])  13.1 us
    ppermute x10, waiting for transfers between devices, swap(): lax.ppermute(x, axis, [(i, i ^ bit) for i in range(lax.axis_size(axis))])  10.9 us
    unnamed x12, local copies, waits for them, and re-layouts  5.81 us
    pallas_call x4, Pallas kernels, call(): pl.pallas_call(body, in_specs=[WHOLE] * len(args), out_specs=[WHOLE] * le...  5.71 us
  transfers between devices with their start and end apart: 10, of which 5 were waited for; matrix products, arithmetic and copies ran while one was open for 3% of the time, Pallas kernels for 11%

profile of v1, /device:TPU:0, one launch (start us, length us, event | category | flops | bytes accessed | tf_op | source)
XLA Modules:
  0.0 38.4 jit_solution(6496013353596383789)
XLA Ops:
  0.6 0.8 %copy-done.1 = bf16[128,256]{1,0:T(8,128)(2,1)S(1)} copy-done((bf16[128,256]{1,0:T(8,128)(2,1)S(1)}, bf16[128,256]{1,0:T(8,128)(2,1)}, u32[]{:S(2)}) %copy-start.1) | copy-done | bytes 65560
  1.5 0.8 %copy-done.2 = bf16[128,256]{1,0:T(8,128)(2,1)S(1)} copy-done((bf16[128,256]{1,0:T(8,128)(2,1)S(1)}, bf16[128,256]{1,0:T(8,128)(2,1)}, u32[]{:S(2)}) %copy-start.2) | copy-done | bytes 65560
  2.3 0.8 %copy-done.3 = bf16[64,256]{1,0:T(8,128)(2,1)S(1)} copy-done((bf16[64,256]{1,0:T(8,128)(2,1)S(1)}, bf16[64,256]{1,0:T(8,128)(2,1)}, u32[]{:S(2)}) %copy-start.3) | copy-done | bytes 32792
  3.1 0.2 shard_map.67
  3.3 0.0 copy-start
  3.3 3.4 %copy-done = bf16[128,64,512]{2,1,0:T(8,128)(2,1)S(1)} copy-done((bf16[128,64,512]{2,1,0:T(8,128)(2,1)S(1)}, bf16[128,64,512]{2,1,0:T(8,128)(2,1)}, u32[]{:S(2)}) %copy-start) | copy-done | bytes 8388632
  6.7 1.3 %shard_map.68 = f32[256,256]{1,0:T(8,128)S(1)} custom-call(bf16[128,64,512]{2,1,0:T(8,128)(2,1)S(1)} %copy-done, bf16[128,256]{1,0:T(8,128)(2,1)S(1)} %get-tuple-element.25.a_ref, bf16[64,256]{1,0:T(8,128)(2,1)S(1)} %get-tuple-element.19.b_ref), custom_call_target="tpu_custom_call" | custom-call | flops 1073741824 | tf_op jit(solution)/shard_map/pallas_call | solution.py:33
  8.0 0.5 %collective-permute-start.3 = (f32[256,256]{1,0:T(8,128)S(1)}, f32[256,256]{1,0:T(8,128)S(1)}, u32[]{:S(2)}, u32[]{:S(2)}) collective-permute-start(f32[256,256]{1,0:T(8,128)S(1)} %shard_map.68), channel_id=1, source_target_pairs={{0,1},{1,0},{2,3},{3,2},{4,5},{5,4},{6,7},{7,6},{8,9},{9,8},{10,11... | collective-permute-start | bytes 786440 | tf_op jit(solution)/shard_map/ppermute | solution.py:29
  8.5 2.6 %collective-permute-start.1 = (bf16[192,256]{1,0:T(8,128)(2,1)S(1)}, bf16[192,256]{1,0:T(8,128)(2,1)S(1)}, u32[]{:S(2)}, u32[]{:S(2)}) collective-permute-start(bf16[192,256]{1,0:T(8,128)(2,1)S(1)} %get-tuple-element.21.refs_0_), channel_id=1, source_target_pairs={{0,2},{1,3},{2,0},{3,1},{4,6},{5,7},{6,4},{7,5},{8,10},{9,11},{10,... | collective-permute-start | bytes 294920 | tf_op jit(solution)/shard_map/ppermute | solution.py:29
  11.1 0.2 collective-permute-start
  11.3 0.1 pad.2.clone
  11.4 3.1 %collective-permute-done.1.refs_2_ = bf16[192,256]{1,0:T(8,128)(2,1)S(1)} collective-permute-done((bf16[192,256]{1,0:T(8,128)(2,1)S(1)}, bf16[192,256]{1,0:T(8,128)(2,1)S(1)}, u32[]{:S(2)}, u32[]{:S(2)}) %collective-permute-start.1) | collective-permute-done | bytes 98336 | tf_op jit(solution)/shard_map/ppermute | solution.py:29
  14.5 0.0 collective-permute-start.2
  14.5 0.0 collective-permute-done.refs_1_
  14.5 1.3 %shard_map.70 = f32[256,256]{1,0:T(8,128)S(1)} custom-call(bf16[128,64,512]{2,1,0:T(8,128)(2,1)S(1)} %copy-done, bf16[128,256]{1,0:T(8,128)(2,1)S(1)} %get-tuple-element.25.a_ref, bf16[64,256]{1,0:T(8,128)(2,1)S(1)} %get-tuple-element.19.b_ref), custom_call_target="tpu_custom_call" | custom-call | flops 1073741824 | tf_op jit(solution)/shard_map/pallas_call | solution.py:33
  15.8 0.0 collective-permute-done.3
  15.9 1.8 %collective-permute-start.4 = (f32[128,256]{1,0:T(8,128)S(1)}, f32[128,256]{1,0:T(8,128)S(1)}, u32[]{:S(2)}, u32[]{:S(2)}) collective-permute-start(f32[128,256]{1,0:T(8,128)S(1)} %slice.33), channel_id=1, source_target_pairs={{0,2},{1,3},{2,0},{3,1},{4,6},{5,7},{6,4},{7,5},{8,10},{9,11},{10,... | collective-permute-start | bytes 393224 | tf_op jit(solution)/shard_map/ppermute | solution.py:29
  17.7 2.9 %shard_map.69 = (f32[128,256]{1,0:T(8,128)S(1)}, f32[64,256]{1,0:T(8,128)S(1)}, f32[128,256]{1,0:T(8,128)S(1)}) custom-call(bf16[128,64,512]{2,1,0:T(8,128)(2,1)S(1)} %bitcast.11, bf16[128,256]{1,0:T(8,128)(2,1)S(1)} %get-tuple-element.25.a_ref, bf16[64,256]{1,0:T(8,128)(2,1)S(1)} %get-tuple-element.19.b_ref, f32[256,256]{1,0:T(8,128)S(1)} %get-tuple-element.20.ga_ref, ...), custom_call_target="tpu_custom_call" | custom-call | flops 2147483648 | tf_op jit(solution)/shard_map/pallas_call | solution.py:33
  20.6 1.3 %collective-permute-done.4 = f32[128,256]{1,0:T(8,128)S(1)} collective-permute-done((f32[128,256]{1,0:T(8,128)S(1)}, f32[128,256]{1,0:T(8,128)S(1)}, u32[]{:S(2)}, u32[]{:S(2)}) %collective-permute-start.4) | collective-permute-done | bytes 131104 | tf_op jit(solution)/shard_map/ppermute | solution.py:29
  21.9 0.1 abs_reduce_fusion
  22.0 0.1 select_convert_fusion.2
  22.2 1.8 %collective-permute-start.6 = (f16[208,256]{1,0:T(8,128)(2,1)S(1)}, f16[208,256]{1,0:T(8,128)(2,1)S(1)}, u32[]{:S(2)}, u32[]{:S(2)}) collective-permute-start(f16[208,256]{1,0:T(8,128)(2,1)S(1)} %select_convert_fusion.2), channel_id=1, source_target_pairs={{0,4},{4,0},{8,12},{12,8},{16,20},{20,16},{24,28},{28,24},{1,5},{5... | collective-permute-start | bytes 319496 | tf_op jit(solution)/shard_map/ppermute | solution.py:29
  24.0 3.0 %collective-permute-done.6 = f16[208,256]{1,0:T(8,128)(2,1)S(1)} collective-permute-done((f16[208,256]{1,0:T(8,128)(2,1)S(1)}, f16[208,256]{1,0:T(8,128)(2,1)S(1)}, u32[]{:S(2)}, u32[]{:S(2)}) %collective-permute-start.6) | collective-permute-done | bytes 106528 | tf_op jit(solution)/shard_map/ppermute | solution.py:29
  27.0 0.1 select_convert_fusion.1
  27.1 1.9 %collective-permute-start.8 = (f16[208,256]{1,0:T(8,128)(2,1)S(1)}, f16[208,256]{1,0:T(8,128)(2,1)S(1)}, u32[]{:S(2)}, u32[]{:S(2)}) collective-permute-start(f16[208,256]{1,0:T(8,128)(2,1)S(1)} %select_convert_fusion.1), channel_id=1, source_target_pairs={{0,8},{4,12},{8,0},{12,4},{16,24},{20,28},{24,16},{28,20},{1,9},{5... | collective-permute-start | bytes 319496 | tf_op jit(solution)/shard_map/ppermute | solution.py:29
  29.0 1.5 %collective-permute-start.7 = (f32[128,256]{1,0:T(8,128)S(1)}, f32[128,256]{1,0:T(8,128)S(1)}, u32[]{:S(2)}, u32[]{:S(2)}) collective-permute-start(f32[128,256]{1,0:T(8,128)S(1)} %add.35), channel_id=1, source_target_pairs={{0,2},{1,3},{2,0},{3,1},{4,6},{5,7},{6,4},{7,5},{8,10},{9,11},{10,... | collective-permute-start | bytes 393224 | tf_op jit(solution)/shard_map/ppermute | solution.py:29
  30.5 1.4 %collective-permute-done.8 = f16[208,256]{1,0:T(8,128)(2,1)S(1)} collective-permute-done((f16[208,256]{1,0:T(8,128)(2,1)S(1)}, f16[208,256]{1,0:T(8,128)(2,1)S(1)}, u32[]{:S(2)}, u32[]{:S(2)}) %collective-permute-start.8) | collective-permute-done | bytes 106528 | tf_op jit(solution)/shard_map/ppermute | solution.py:29
  31.9 0.1 select_convert_fusion
  32.0 2.9 %collective-permute-start.9 = (f16[208,256]{1,0:T(8,128)(2,1)S(1)}, f16[208,256]{1,0:T(8,128)(2,1)S(1)}, u32[]{:S(2)}, u32[]{:S(2)}) collective-permute-start(f16[208,256]{1,0:T(8,128)(2,1)S(1)} %select_convert_fusion), channel_id=1, source_target_pairs={{0,16},{4,20},{8,24},{12,28},{16,0},{20,4},{24,8},{28,12},{1,17},{... | collective-permute-start | bytes 319496 | tf_op jit(solution)/shard_map/ppermute | solution.py:29
  34.9 0.7 %add.38 = f32[128,256]{1,0:T(8,128)} add(f32[128,256]{1,0:T(8,128)S(1)} %add.35, f32[128,256]{1,0:T(8,128)S(1)} %collective-permute-done.7) | non-fusion elementwise | flops 32768 | bytes 393216 | tf_op jit(solution)/shard_map/add | solution.py:186
  35.6 2.1 %collective-permute-done.9 = f16[208,256]{1,0:T(8,128)(2,1)S(1)} collective-permute-done((f16[208,256]{1,0:T(8,128)(2,1)S(1)}, f16[208,256]{1,0:T(8,128)(2,1)S(1)}, u32[]{:S(2)}, u32[]{:S(2)}) %collective-permute-start.9) | collective-permute-done | bytes 106528 | tf_op jit(solution)/shard_map/ppermute | solution.py:29
  37.7 0.7 %shard_map.71 = (f32[128,256]{1,0:T(8,128)}, f32[64,256]{1,0:T(8,128)}) custom-call(f32[208,256]{1,0:T(8,128)S(1)} %multiply_add_fusion.v_ref), custom_call_target="tpu_custom_call" | custom-call | tf_op jit(solution)/shard_map/pallas_call | solution.py:193
  (24 shorter events, 0.2 us)
Async XLA Ops:
  0.6 0.8 %copy-start.1 = (bf16[128,256]{1,0:T(8,128)(2,1)S(1)}, bf16[128,256]{1,0:T(8,128)(2,1)}, u32[]{:S(2)}) copy-start(bf16[128,256]{1,0:T(8,128)(2,1)} %a_ref.1) | copy-start | bytes 196612
  1.5 0.8 %copy-start.2 = (bf16[128,256]{1,0:T(8,128)(2,1)S(1)}, bf16[128,256]{1,0:T(8,128)(2,1)}, u32[]{:S(2)}) copy-start(bf16[128,256]{1,0:T(8,128)(2,1)} %c_ref.1) | copy-start | bytes 196612
  2.3 0.8 %copy-start.3 = (bf16[64,256]{1,0:T(8,128)(2,1)S(1)}, bf16[64,256]{1,0:T(8,128)(2,1)}, u32[]{:S(2)}) copy-start(bf16[64,256]{1,0:T(8,128)(2,1)} %b_ref.1) | copy-start | bytes 98308
  3.3 3.4 %copy-start = (bf16[128,64,512]{2,1,0:T(8,128)(2,1)S(1)}, bf16[128,64,512]{2,1,0:T(8,128)(2,1)}, u32[]{:S(2)}) copy-start(bf16[128,64,512]{2,1,0:T(8,128)(2,1)} %x_ref.5) | copy-start | bytes 25165828
  6.7 11.0 %slice-start = ((s8[8388608]{0:T(1024)(128)(4,1)}), s8[4194304]{0:T(1024)(128)(4,1)S(1)}, s32[]{:S(2)}) async-start(s8[8388608]{0:T(1024)(128)(4,1)} %bitcast.10), calls=%async_computation | async-start | bytes 8388608
  8.0 7.8 %collective-permute-start.3 = (f32[256,256]{1,0:T(8,128)S(1)}, f32[256,256]{1,0:T(8,128)S(1)}, u32[]{:S(2)}, u32[]{:S(2)}) collective-permute-start(f32[256,256]{1,0:T(8,128)S(1)} %shard_map.68), channel_id=1, source_target_pairs={{0,1},{1,0},{2,3},{3,2},{4,5},{5,4},{6,7},{7,6},{8,9},{9,8},{10,11... | collective-permute-start | bytes 786440 | tf_op jit(solution)/shard_map/ppermute | solution.py:29
  8.5 6.0 %collective-permute-start.1 = (bf16[192,256]{1,0:T(8,128)(2,1)S(1)}, bf16[192,256]{1,0:T(8,128)(2,1)S(1)}, u32[]{:S(2)}, u32[]{:S(2)}) collective-permute-start(bf16[192,256]{1,0:T(8,128)(2,1)S(1)} %get-tuple-element.21.refs_0_), channel_id=1, source_target_pairs={{0,2},{1,3},{2,0},{3,1},{4,6},{5,7},{6,4},{7,5},{8,10},{9,11},{10,... | collective-permute-start | bytes 294920 | tf_op jit(solution)/shard_map/ppermute | solution.py:29
  11.1 3.4 %collective-permute-start = (bf16[192,256]{1,0:T(8,128)(2,1)S(1)}, bf16[192,256]{1,0:T(8,128)(2,1)S(1)}, u32[]{:S(2)}, u32[]{:S(2)}) collective-permute-start(bf16[192,256]{1,0:T(8,128)(2,1)S(1)} %get-tuple-element.21.refs_0_), channel_id=1, source_target_pairs={{0,1},{1,0},{2,3},{3,2},{4,5},{5,4},{6,7},{7,6},{8,9},{9,8},{10,11... | collective-permute-start | bytes 294920 | tf_op jit(solution)/shard_map/ppermute | solution.py:29
  11.3 6.4 %slice-start.1 = ((s8[8388608]{0:T(1024)(128)(4,1)}), s8[4194304]{0:T(1024)(128)(4,1)S(1)}, s32[]{:S(2)}) async-start(s8[8388608]{0:T(1024)(128)(4,1)} %bitcast.10), calls=%async_computation.1 | async-start | bytes 8388608
  14.5 3.2 %collective-permute-start.2 = (bf16[192,256]{1,0:T(8,128)(2,1)S(1)}, bf16[192,256]{1,0:T(8,128)(2,1)S(1)}, u32[]{:S(2)}, u32[]{:S(2)}) collective-permute-start(bf16[192,256]{1,0:T(8,128)(2,1)S(1)} %collective-permute-done.1.refs_2_), channel_id=1, source_target_pairs={{0,1},{1,0},{2,3},{3,2},{4,5},{5,4},{6,7},{7,6},{8,9},{9,8},{10,11... | collective-permute-start | bytes 294920 | tf_op jit(solution)/shard_map/ppermute | solution.py:29
  15.9 6.0 %collective-permute-start.4 = (f32[128,256]{1,0:T(8,128)S(1)}, f32[128,256]{1,0:T(8,128)S(1)}, u32[]{:S(2)}, u32[]{:S(2)}) collective-permute-start(f32[128,256]{1,0:T(8,128)S(1)} %slice.33), channel_id=1, source_target_pairs={{0,2},{1,3},{2,0},{3,1},{4,6},{5,7},{6,4},{7,5},{8,10},{9,11},{10,... | collective-permute-start | bytes 393224 | tf_op jit(solution)/shard_map/ppermute | solution.py:29
  22.2 4.8 %collective-permute-start.6 = (f16[208,256]{1,0:T(8,128)(2,1)S(1)}, f16[208,256]{1,0:T(8,128)(2,1)S(1)}, u32[]{:S(2)}, u32[]{:S(2)}) collective-permute-start(f16[208,256]{1,0:T(8,128)(2,1)S(1)} %select_convert_fusion.2), channel_id=1, source_target_pairs={{0,4},{4,0},{8,12},{12,8},{16,20},{20,16},{24,28},{28,24},{1,5},{5... | collective-permute-start | bytes 319496 | tf_op jit(solution)/shard_map/ppermute | solution.py:29
  24.0 3.1 %collective-permute-start.5 = (f32[128,256]{1,0:T(8,128)S(1)}, f32[128,256]{1,0:T(8,128)S(1)}, u32[]{:S(2)}, u32[]{:S(2)}) collective-permute-start(f32[128,256]{1,0:T(8,128)S(1)} %get-tuple-element.27), channel_id=1, source_target_pairs={{0,1},{1,0},{2,3},{3,2},{4,5},{5,4},{6,7},{7,6},{8,9},{9,8},{10,11... | collective-permute-start | bytes 393224 | tf_op jit(solution)/shard_map/ppermute | solution.py:29
  27.1 4.8 %collective-permute-start.8 = (f16[208,256]{1,0:T(8,128)(2,1)S(1)}, f16[208,256]{1,0:T(8,128)(2,1)S(1)}, u32[]{:S(2)}, u32[]{:S(2)}) collective-permute-start(f16[208,256]{1,0:T(8,128)(2,1)S(1)} %select_convert_fusion.1), channel_id=1, source_target_pairs={{0,8},{4,12},{8,0},{12,4},{16,24},{20,28},{24,16},{28,20},{1,9},{5... | collective-permute-start | bytes 319496 | tf_op jit(solution)/shard_map/ppermute | solution.py:29
  29.0 5.9 %collective-permute-start.7 = (f32[128,256]{1,0:T(8,128)S(1)}, f32[128,256]{1,0:T(8,128)S(1)}, u32[]{:S(2)}, u32[]{:S(2)}) collective-permute-start(f32[128,256]{1,0:T(8,128)S(1)} %add.35), channel_id=1, source_target_pairs={{0,2},{1,3},{2,0},{3,1},{4,6},{5,7},{6,4},{7,5},{8,10},{9,11},{10,... | collective-permute-start | bytes 393224 | tf_op jit(solution)/shard_map/ppermute | solution.py:29
  32.0 5.7 %collective-permute-start.9 = (f16[208,256]{1,0:T(8,128)(2,1)S(1)}, f16[208,256]{1,0:T(8,128)(2,1)S(1)}, u32[]{:S(2)}, u32[]{:S(2)}) collective-permute-start(f16[208,256]{1,0:T(8,128)(2,1)S(1)} %select_convert_fusion), channel_id=1, source_target_pairs={{0,16},{4,20},{8,24},{12,28},{16,0},{20,4},{24,8},{28,12},{1,17},{... | collective-permute-start | bytes 319496 | tf_op jit(solution)/shard_map/ppermute | solution.py:29

commit v2 on v1

--- a/solution.py
+++ b/solution.py
@@ -11,8 +11,10 @@
 BF16 = jnp.bfloat16
 F16 = jnp.float16
 VMEM_LIMIT = 32 * 1024 * 1024
+LOAD_LIMIT = 54 * 1024 * 1024 + 512 * 1024
 LANES = 128
-TAIL = 16
+CHUNKS = 8
+TAIL = 8
 TOP = 13.0
 WHOLE = pl.BlockSpec(memory_space=pltpu.VMEM)
 
@@ -76,6 +78,115 @@
     g_ref[...] = lax.dot_general(
         x.reshape(rows, x.shape[2]), kr, (((0,), (0,)), ((), ())), preferred_element_type=F32
     )
+
+
+def load(offsets, x_hbm, a_hbm, b_hbm, c_hbm, x_ref, a_ref, b_ref, cb_ref, ga_ref, g_ref, sems):
+    s_rows, rank = b_ref.shape
+    r_rows = a_ref.shape[0]
+    h_own = c_hbm.shape[0]
+    width = g_ref.shape[0] // len(offsets)
+    small = [
+        pltpu.make_async_copy(a_hbm, a_ref, sems.at[0]),
+        pltpu.make_async_copy(b_hbm, b_ref, sems.at[1]),
+        pltpu.make_async_copy(c_hbm, cb_ref.at[pl.ds(0, h_own)], sems.at[2]),
+        pltpu.make_async_copy(b_hbm, cb_ref.at[pl.ds(h_own, s_rows)], sems.at[3]),
+    ]
+    rows = r_rows // CHUNKS
+    chunks = [
+        pltpu.make_async_copy(x_hbm.at[pl.ds(i * rows, rows)], x_ref.at[pl.ds(i * rows, rows)], sems.at[4 + i])
+        for i in range(CHUNKS)
+    ]
+    for copy in small + chunks:
+        copy.start()
+    for copy in small:
+        copy.wait()
+    ga_ref[...] = gram(a_ref[...])
+    me = lax.axis_index("src")
+    at = [pl.ds(pl.multiple_of((me ^ o) * width, width), width) for o in offsets]
+    for i, copy in enumerate(chunks):
+        mine = pl.ds(i * rows, rows)
+        kr = (a_ref[mine][:, None, :] * b_ref[...][None]).reshape(rows * s_rows, rank)
+        copy.wait()
+        x = jnp.concatenate([x_ref[mine, :, a] for a in at], axis=2).reshape(rows * s_rows, 2 * width)
+        part = lax.dot_general(x, kr, (((0,), (0,)), ((), ())), preferred_element_type=F32)
+        g_ref[...] = part if i == 0 else g_ref[...] + part
+
+
+def meet(to_height, g_ref, in_ref, own_ref, mate_ref, cy_ref, ga_ref, keep_ref, away_ref, *top_refs):
+    h_own = cy_ref.shape[0]
+    s_rows = own_ref.shape[0] - h_own
+    sources = pl.ds(h_own, s_rows)
+    m = ga_ref[...] * (gram(own_ref[sources]) + gram(mate_ref[sources]))
+    g = g_ref[...] + in_ref[...]
+    keep_ref[...] = (times(own_ref[0:h_own], m) - g[0:h_own]) * to_height
+    away_ref[...] = (times(cy_ref[...], m) - g[h_own:]) * to_height
+    for top, part in zip(top_refs, (keep_ref, away_ref)):
+        top[...] = column_top(part[...])
+
+
+def project_four(scales, x_ref, a_ref, b_ref, ga_ref, own_ref, mate_ref, cy_ref, pa_ref, ps_ref, top_ref, heights):
+    s_rows, rank = b_ref.shape
+    r_rows = a_ref.shape[0]
+    h_own = cy_ref.shape[0]
+    me = lax.axis_index("src")
+    parts = (own_ref[0:h_own], mate_ref[0:h_own], cy_ref[...], mate_ref[h_own + s_rows :])
+    for o, part in enumerate(parts):
+        heights[pl.ds(pl.multiple_of((me ^ o) * h_own, h_own), h_own)] = part
+    x = x_ref[...].reshape(r_rows * s_rows, x_ref.shape[2])
+    proj = jnp.dot(x, heights[...], preferred_element_type=F32).reshape(r_rows, s_rows, rank)
+    pa = (proj * b_ref[...].astype(F32)[None]).sum(1)
+    ps = (proj * a_ref[...].astype(F32)[:, None, :]).sum(0)
+    gc = gram(heights[...])
+    to_radius, _, to_source = scales
+    pa_ref[...] = (times(a_ref[...], gram(b_ref[...]) * gc) - pa) * to_radius
+    ps_ref[...] = (times(b_ref[...], ga_ref[...] * gc) - ps) * to_source
+    top_ref[...] = column_top(ps_ref[...])
+
+
+def local_four(slab, radius_factor, height_factor, source_factor, scales):
+    r_rows, s_rows, width = slab.shape
+    h_own, rank = height_factor.shape
+    work = 2 * r_rows * s_rows * width * rank
+    cy = swap(height_factor, "src", 2)
+    x, a, b, cb, ga, g_away = pl.pallas_call(
+        functools.partial(load, (1, 3)),
+        in_specs=[pl.BlockSpec(memory_space=pl.ANY)] * 4,
+        out_specs=[WHOLE] * 6,
+        out_shape=[
+            pltpu.VMEM(slab.shape, BF16),
+            pltpu.VMEM(radius_factor.shape, BF16),
+            pltpu.VMEM(source_factor.shape, BF16),
+            pltpu.VMEM((h_own + s_rows, rank), BF16),
+            pltpu.VMEM((rank, rank), F32),
+            pltpu.VMEM((width // 2, rank), F32),
+        ],
+        scratch_shapes=[pltpu.SemaphoreType.DMA((4 + CHUNKS,))],
+        compiler_params=pltpu.CompilerParams(vmem_limit_bytes=LOAD_LIMIT),
+        cost_estimate=pl.CostEstimate(flops=2 * work, bytes_accessed=0, transcendentals=0),
+    )(slab, radius_factor, source_factor, height_factor)
+    g_in = swap(g_away, "src", 1)
+    cby = jnp.concatenate([cb, after(cy, g_away)], axis=0)
+    mate = swap(cby, "src", 1)
+    (g_keep,) = call(
+        functools.partial(height_terms, (0, 2)), [((width // 2, rank), F32)], (x, after(a, cby), b), work // 2
+    )
+    keep, away, keep_top, away_top = call(
+        functools.partial(meet, scales[1]),
+        [((h_own, rank), F32), ((h_own, rank), F32), ((1, rank), F32), ((1, rank), F32)],
+        (g_keep, g_in, cb, mate, cy, ga),
+        work // 8,
+    )
+    away = pack(padded(away), exponent(away_top))
+    share_in, e_in = unpack(swap(away, "src", 2))
+    share_in = share_in[:h_own]
+    pa, ps, ps_top = call(
+        functools.partial(project_four, scales),
+        [((r_rows, rank), F32), ((s_rows, rank), F32), ((1, rank), F32)],
+        (x, after(a, away), b, ga, cb, mate, cy),
+        work,
+        scratch=[pltpu.VMEM((width, rank), BF16)],
+    )
+    return pa, ps, keep + share_in, exponent(jnp.maximum(ps_top, keep_top + jnp.exp2(e_in)))
 
 
 def project(scales, n_src, x_ref, a_ref, b_ref, ga_ref, *refs):
@@ -102,36 +213,12 @@
     ph_ref[...] = times(blocks[0][0:h_own], ga * gb) * to_height
 
 
-def split(v_ref, h_ref, s_ref):
-    h_own = h_ref.shape[0]
-    h_ref[...] = v_ref[0:h_own]
-    s_ref[...] = v_ref[h_own : h_own + s_ref.shape[0]]
-
-
-def pack(v, e):
-    rows = lax.broadcasted_iota(jnp.int32, v.shape, 0)
-    return jnp.where(rows < v.shape[0] - TAIL, v * jnp.exp2(TOP - e), e).astype(F16)
-
-
-def unpack(m):
-    e = m[-1:].astype(F32)
-    return m.astype(F32) * jnp.exp2(e - TOP), e
-
-
-def per_device(slab, radius_factor, height_factor, source_factor):
-    n_rad, n_src = lax.axis_size("rad"), lax.axis_size("src")
+def local_any(slab, radius_factor, height_factor, source_factor, scales):
+    n_src = lax.axis_size("src")
     r_rows, s_rows, width = slab.shape
     h_own, rank = height_factor.shape
-    total_r, total_s = r_rows * n_rad, s_rows * n_src
-    scales = (
-        (total_s * width) ** -0.5,
-        (total_r * total_s) ** -0.5,
-        (total_r * width) ** -0.5,
-    )
     work = 2 * r_rows * s_rows * width * rank
     src_bits = [1 << i for i in range(n_src.bit_length() - 1)]
-    rad_bits = [1 << i for i in range(n_rad.bit_length() - 1)]
-
     a, b, cb, ga = call(
         prepare,
         [((r_rows, rank), BF16), ((s_rows, rank), BF16), ((h_own + s_rows, rank), BF16), ((rank, rank), F32)],
@@ -175,19 +262,66 @@
         scratch=[pltpu.VMEM((width, rank), BF16)],
     )
     ph = ph - (g[:h_own] + share_in) * scales[1]
-    v = jnp.concatenate([ph, ps, jnp.zeros((TAIL, rank), F32)], axis=0)
-    top = jnp.max(jnp.abs(v), axis=0, keepdims=True)
-    e = jnp.clip(jnp.ceil(jnp.log2(jnp.maximum(top, 1e-30))), -100.0, 100.0)
-    bits = list(src_bits)
-    for i, bit in enumerate(rad_bits):
+    return pa, ps, ph, exponent(jnp.maximum(column_top(ph), column_top(ps)))
+
+
+def split(v_ref, h_ref, s_ref):
+    h_own = h_ref.shape[0]
+    h_ref[...] = v_ref[0:h_own]
+    s_ref[...] = v_ref[h_own : h_own + s_ref.shape[0]]
+
+
+def exponent(top):
+    return jnp.clip(jnp.ceil(jnp.log2(jnp.maximum(top, 1e-30))), -100.0, 100.0)
+
+
+def pack(v, e):
+    rows = lax.broadcasted_iota(jnp.int32, v.shape, 0)
+    return jnp.where(rows < v.shape[0] - TAIL, v * jnp.exp2(TOP - e), e).astype(F16)
+
+
+def unpack(m):
+    e = m[-1:].astype(F32)
+    return m.astype(F32) * jnp.exp2(e - TOP), e
+
+
+def padded(*parts):
+    return jnp.concatenate([*parts, jnp.zeros((TAIL, parts[0].shape[1]), F32)], axis=0)
+
+
+def column_top(v):
+    return jnp.max(jnp.abs(v), axis=0, keepdims=True)
+
+
+def per_device(slab, radius_factor, height_factor, source_factor):
+    n_rad, n_src = lax.axis_size("rad"), lax.axis_size("src")
+    r_rows, s_rows, width = slab.shape
+    h_own, rank = height_factor.shape
+    total_r, total_s = r_rows * n_rad, s_rows * n_src
+    scales = (
+        (total_s * width) ** -0.5,
+        (total_r * total_s) ** -0.5,
+        (total_r * width) ** -0.5,
+    )
+    src_bits = [1 << i for i in range(n_src.bit_length() - 1)]
+    rad_bits = [1 << i for i in range(n_rad.bit_length() - 1)]
+
+    local = local_four if n_src == 4 and h_own % LANES == 0 else local_any
+    pa, ps, ph, e = local(slab, radius_factor, height_factor, source_factor, scales)
+    v = padded(ph, ps)
+    bits = src_bits[::-1]
+    for stage in [rad_bits[i : i + 2] for i in range(0, len(rad_bits), 2)]:
         m = pack(v, e)
+        others = [0, *stage] if len(stage) == 1 else [0, stage[0], stage[1], sum(stage)]
+        terms = [unpack(m)] + [unpack(swap(m, "rad", o)) for o in others[1:]]
         if bits:
-            pa, m = lax.optimization_barrier((pa, m))
+            pa = after(pa, m)
             pa = pa + swap(pa, "src", bits.pop(0))
-        other, e_other = unpack(swap(m, "rad", bit))
-        v, e = unpack(m)
-        v = v + other
-        e = jnp.maximum(e, e_other) + 1.0
+        values = [value for value, _ in terms]
+        while len(values) > 1:
+            values = [a + b for a, b in zip(values[0::2], values[1::2])]
+        (v,) = values
+        e = functools.reduce(jnp.maximum, [x for _, x in terms]) + len(stage)
     for bit in bits:
         pa = pa + swap(pa, "src", bit)
     grad_height, grad_source = pl.pallas_call(
@@ -195,7 +329,7 @@
         in_specs=[WHOLE],
         out_specs=[WHOLE] * 2,
         out_shape=[jax.ShapeDtypeStruct((h_own, rank), F32), jax.ShapeDtypeStruct((s_rows, rank), F32)],
-    )(inside(v))
+    )(inside(after(v, pa)))
     return pa, grad_height, grad_source
 
 

time: 38.7 us -> 32.4 us (0.84)
  local copies, waits for them, and re-layouts: 5.9 us -> 0.09 us
  Pallas kernels: 6.39 us -> 9.55 us
  starting transfers between devices: 13.1 us -> 10.6 us
  waiting for transfers between devices: 10.9 us -> 9.94 us
    unnamed x12 -> x1, local copies, waits for them, and re-layouts: 5.81 us -> 0.01 us
    pallas_call x0 -> x1, Pallas kernels: none -> 4.28 us  [local_four(): pl.pallas_call(functools.partial(load, (1, 3)), in_specs=[pl.BlockSpec(me...]
    ppermute x10, starting transfers between devices: 13.1 us -> 10.6 us  [swap(): lax.ppermute(x, axis, [(i, i ^ bit) for i in range(lax.axis_size(axis))])]
    pallas_call x4 -> x3, Pallas kernels: 5.71 us -> 4.59 us  [call(): pl.pallas_call(body, in_specs=[WHOLE] * len(args), out_specs=[WHOLE] * le...]
    ppermute x10, waiting for transfers between devices: 10.9 us -> 9.94 us  [swap(): lax.ppermute(x, axis, [(i, i ^ bit) for i in range(lax.axis_size(axis))])]
  transfers between devices with their start and end apart: 10 -> 10, of which waited for: 5 -> 5; matrix products, arithmetic and copies ran while one was open for 3% -> 1% of each run, Pallas kernels for 11% -> 26%
where the time goes in v2:
time: 32.4 us; the launch traced here: 32.2 us
  starting transfers between devices  10.6 us (33%)
  waiting for transfers between devices  9.94 us (31%)
  Pallas kernels  9.55 us (29%)
  other arithmetic  1.22 us (4%)
  between operations  0.79 us (2%)
    ppermute x10, starting transfers between devices, swap(): lax.ppermute(x, axis, [(i, i ^ bit) for i in range(lax.axis_size(axis))])  10.6 us
    ppermute x10, waiting for transfers between devices, swap(): lax.ppermute(x, axis, [(i, i ^ bit) for i in range(lax.axis_size(axis))])  9.94 us
    pallas_call x3, Pallas kernels, call(): pl.pallas_call(body, in_specs=[WHOLE] * len(args), out_specs=[WHOLE] * le...  4.59 us
    pallas_call x1, Pallas kernels, local_four(): pl.pallas_call(functools.partial(load, (1, 3)), in_specs=[pl.BlockSpec(me...  4.28 us
    add x2, other arithmetic, per_device(): pa = pa + swap(pa, 'src', bits.pop(0))  0.69 us
    pallas_call x1, Pallas kernels, per_device(): pl.pallas_call(split, in_specs=[WHOLE], out_specs=[WHOLE] * 2, out_shape=...  0.68 us
  transfers between devices with their start and end apart: 10, of which 5 were waited for; matrix products, arithmetic and copies ran while one was open for 1% of the time, Pallas kernels for 26%

profile of v2, /device:TPU:0, one launch (start us, length us, event | category | flops | bytes accessed | tf_op | source)
XLA Modules:
  0.0 32.2 jit_solution(13171479612419880491)
XLA Ops:
  0.6 3.0 %collective-permute-start = (bf16[128,256]{1,0:T(8,128)(2,1)}, bf16[128,256]{1,0:T(8,128)(2,1)S(1)}, u32[]{:S(2)}, u32[]{:S(2)}) collective-permute-start(bf16[128,256]{1,0:T(8,128)(2,1)} %c_hbm.1), channel_id=1, source_target_pairs={{0,2},{1,3},{2,0},{3,1},{4,6},{5,7},{6,4},{7,5},{8,10},{9,11},{10,... | collective-permute-start | bytes 196616 | tf_op jit(solution)/shard_map/ppermute | solution.py:31
  3.7 4.3 %shard_map.67 = (bf16[128,64,512]{2,1,0:T(8,128)(2,1)S(1)}, bf16[128,256]{1,0:T(8,128)(2,1)S(1)}, bf16[64,256]{1,0:T(8,128)(2,1)S(1)}, bf16[192,256]{1,0:T(8,128...) custom-call(bf16[128,64,512]{2,1,0:T(8,128)(2,1)} %x_hbm.1, bf16[128,256]{1,0:T(8,128)(2,1)} %a_hbm.1, ...), custom_call_target="tpu_custom_call" | custom-call | flops 4294967296 | tf_op jit(solution)/shard_map/pallas_call | solution.py:151
  8.0 0.1 collective-permute-start.1
  8.1 0.1 pad.3.clone
  8.1 0.0 collective-permute-done.cy_ref
  8.2 0.5 %collective-permute-start.2 = (bf16[320,256]{1,0:T(8,128)(2,1)S(1)}, bf16[320,256]{1,0:T(8,128)(2,1)S(1)}, u32[]{:S(2)}, u32[]{:S(2)}) collective-permute-start(bf16[320,256]{1,0:T(8,128)(2,1)S(1)} %constant_dynamic-update-slice_fusion), channel_id=1, source_target_pairs={{0,1},{1,0},{2,3},{3,2},{4,5},{5,4},{6,7},{7,6},{8,9},{9,8},{10,11... | collective-permute-start | bytes 491528 | tf_op jit(solution)/shard_map/ppermute | solution.py:31
  8.7 1.3 %shard_map.68.g_ref = f32[256,256]{1,0:T(8,128)S(1)} custom-call(bf16[128,64,512]{2,1,0:T(8,128)(2,1)S(1)} %get-tuple-element.24.x_ref, bf16[128,256]{1,0:T(8,128)(2,1)S(1)} %get-tuple-element.34.a_ref, bf16[64,256]{1,0:T(8,128)(2,1)S(1)} %get-tuple-element.30.b_ref), custom_call_target="tpu_custom_call" | custom-call | flops 1073741824 | tf_op jit(solution)/shard_map/pallas_call | solution.py:35
  10.0 0.0 collective-permute-done.2.mate_ref
  10.0 0.0 collective-permute-done.1.in_ref
  10.0 0.6 %shard_map.69 = (f32[128,256]{1,0:T(8,128)S(1)}, f32[128,256]{1,0:T(8,128)S(1)}, f32[1,256]{1,0:T(1,128)S(1)}, f32[1,256]{1,0:T(1,128)S(1)}) custom-call(f32[256,256]{1,0:T(8,128)S(1)} %shard_map.68.g_ref, f32[256,256]{1,0:T(8,128)S(1)} %collective-permute-done.1.in_ref, bf16[192,256]{1,0:T(8,128)(2,1)S(1)} %get-tuple-element.26.own_ref, ...), custom_call_target="tpu_custom_call" | custom-call | flops 268435456 | tf_op jit(solution)/shard_map/pallas_call | solution.py:35
  10.6 0.1 select_convert_fusion.1
  10.7 0.1 collective-permute-start.3
  10.8 2.7 %shard_map.70 = (f32[128,256]{1,0:T(8,128)S(1)}, f32[64,256]{1,0:T(8,128)S(1)}, f32[1,256]{1,0:T(1,128)S(1)}) custom-call(bf16[128,64,512]{2,1,0:T(8,128)(2,1)S(1)} %get-tuple-element.24.x_ref, bf16[128,256]{1,0:T(8,128)(2,1)S(1)} %get-tuple-element.34.a_ref, bf16[64,256]{1,0:T(8,128)(2,1)S(1)} %get-tuple-element.30.b_ref, ...), custom_call_target="tpu_custom_call" | custom-call | flops 2147483648 | tf_op jit(solution)/shard_map/pallas_call | solution.py:35
  13.5 1.6 %collective-permute-done.3 = f16[136,256]{1,0:T(8,128)(2,1)S(1)} collective-permute-done((f16[136,256]{1,0:T(8,128)(2,1)S(1)}, f16[136,256]{1,0:T(8,128)(2,1)S(1)}, u32[]{:S(2)}, u32[]{:S(2)}) %collective-permute-start.3) | collective-permute-done | bytes 69664 | tf_op jit(solution)/shard_map/ppermute | solution.py:31
  15.2 0.1 fusion.1
  15.3 1.6 %collective-permute-start.5 = (f16[200,256]{1,0:T(8,128)(2,1)S(1)}, f16[200,256]{1,0:T(8,128)(2,1)S(1)}, u32[]{:S(2)}, u32[]{:S(2)}) collective-permute-start(f16[200,256]{1,0:T(8,128)(2,1)S(1)} %fusion.1), channel_id=1, source_target_pairs={{0,4},{4,0},{8,12},{12,8},{16,20},{20,16},{24,28},{28,24},{1,5},{5... | collective-permute-start | bytes 307208 | tf_op jit(solution)/shard_map/ppermute | solution.py:31
  16.9 1.6 %collective-permute-start.6 = (f16[200,256]{1,0:T(8,128)(2,1)S(1)}, f16[200,256]{1,0:T(8,128)(2,1)S(1)}, u32[]{:S(2)}, u32[]{:S(2)}) collective-permute-start(f16[200,256]{1,0:T(8,128)(2,1)S(1)} %fusion.1), channel_id=1, source_target_pairs={{0,8},{4,12},{8,0},{12,4},{16,24},{20,28},{24,16},{28,20},{1,9},{5... | collective-permute-start | bytes 307208 | tf_op jit(solution)/shard_map/ppermute | solution.py:31
  18.4 0.4 %collective-permute-start.7 = (f16[200,256]{1,0:T(8,128)(2,1)S(1)}, f16[200,256]{1,0:T(8,128)(2,1)S(1)}, u32[]{:S(2)}, u32[]{:S(2)}) collective-permute-start(f16[200,256]{1,0:T(8,128)(2,1)S(1)} %fusion.1), channel_id=1, source_target_pairs={{0,12},{4,8},{8,4},{12,0},{16,28},{20,24},{24,20},{28,16},{1,13},{... | collective-permute-start | bytes 307208 | tf_op jit(solution)/shard_map/ppermute | solution.py:31
  18.9 0.5 %collective-permute-start.4 = (f32[128,256]{1,0:T(8,128)S(1)}, f32[128,256]{1,0:T(8,128)S(1)}, u32[]{:S(2)}, u32[]{:S(2)}) collective-permute-start(f32[128,256]{1,0:T(8,128)S(1)} %get-tuple-element.40), channel_id=1, source_target_pairs={{0,2},{1,3},{2,0},{3,1},{4,6},{5,7},{6,4},{7,5},{8,10},{9,11},{10,... | collective-permute-start | bytes 393224 | tf_op jit(solution)/shard_map/ppermute | solution.py:31
  19.3 0.9 %collective-permute-done.5 = f16[200,256]{1,0:T(8,128)(2,1)S(1)} collective-permute-done((f16[200,256]{1,0:T(8,128)(2,1)S(1)}, f16[200,256]{1,0:T(8,128)(2,1)S(1)}, u32[]{:S(2)}, u32[]{:S(2)}) %collective-permute-start.5) | collective-permute-done | bytes 102432 | tf_op jit(solution)/shard_map/ppermute | solution.py:31
  20.2 1.4 %collective-permute-done.6 = f16[200,256]{1,0:T(8,128)(2,1)S(1)} collective-permute-done((f16[200,256]{1,0:T(8,128)(2,1)S(1)}, f16[200,256]{1,0:T(8,128)(2,1)S(1)}, u32[]{:S(2)}, u32[]{:S(2)}) %collective-permute-start.6) | collective-permute-done | bytes 102432 | tf_op jit(solution)/shard_map/ppermute | solution.py:31
  21.6 2.4 %collective-permute-done.7 = f16[200,256]{1,0:T(8,128)(2,1)S(1)} collective-permute-done((f16[200,256]{1,0:T(8,128)(2,1)S(1)}, f16[200,256]{1,0:T(8,128)(2,1)S(1)}, u32[]{:S(2)}, u32[]{:S(2)}) %collective-permute-start.7) | collective-permute-done | bytes 102432 | tf_op jit(solution)/shard_map/ppermute | solution.py:31
  24.0 0.2 select_convert_fusion
  24.2 2.8 %collective-permute-start.9 = (f16[200,256]{1,0:T(8,128)(2,1)S(1)}, f16[200,256]{1,0:T(8,128)(2,1)S(1)}, u32[]{:S(2)}, u32[]{:S(2)}) collective-permute-start(f16[200,256]{1,0:T(8,128)(2,1)S(1)} %select_convert_fusion), channel_id=1, source_target_pairs={{0,16},{4,20},{8,24},{12,28},{16,0},{20,4},{24,8},{28,12},{1,17},{... | collective-permute-start | bytes 307208 | tf_op jit(solution)/shard_map/ppermute | solution.py:31
  27.0 0.0 collective-permute-done.4
  27.0 0.1 collective-permute-start.8
  27.1 3.7 %collective-permute-done.9 = f16[200,256]{1,0:T(8,128)(2,1)S(1)} collective-permute-done((f16[200,256]{1,0:T(8,128)(2,1)S(1)}, f16[200,256]{1,0:T(8,128)(2,1)S(1)}, u32[]{:S(2)}, u32[]{:S(2)}) %collective-permute-start.9) | collective-permute-done | bytes 102432 | tf_op jit(solution)/shard_map/ppermute | solution.py:31
  30.9 0.0 collective-permute-done.8
  30.9 0.7 %add.47 = f32[128,256]{1,0:T(8,128)} add(f32[128,256]{1,0:T(8,128)S(1)} %add.41, f32[128,256]{1,0:T(8,128)S(1)} %collective-permute-done.8) | non-fusion elementwise | flops 32768 | bytes 393216 | tf_op jit(solution)/shard_map/add | solution.py:319
  31.5 0.7 %shard_map.71 = (f32[128,256]{1,0:T(8,128)}, f32[64,256]{1,0:T(8,128)}) custom-call(f32[200,256]{1,0:T(8,128)S(1)} %multiply_add_fusion.v_ref), custom_call_target="tpu_custom_call" | custom-call | tf_op jit(solution)/shard_map/pallas_call | solution.py:327
  (13 shorter events, 0.2 us)
Async XLA Ops:
  0.6 7.5 %collective-permute-start = (bf16[128,256]{1,0:T(8,128)(2,1)}, bf16[128,256]{1,0:T(8,128)(2,1)S(1)}, u32[]{:S(2)}, u32[]{:S(2)}) collective-permute-start(bf16[128,256]{1,0:T(8,128)(2,1)} %c_hbm.1), channel_id=1, source_target_pairs={{0,2},{1,3},{2,0},{3,1},{4,6},{5,7},{6,4},{7,5},{8,10},{9,11},{10,... | collective-permute-start | bytes 196616 | tf_op jit(solution)/shard_map/ppermute | solution.py:31
  8.0 2.1 %collective-permute-start.1 = (f32[256,256]{1,0:T(8,128)S(1)}, f32[256,256]{1,0:T(8,128)S(1)}, u32[]{:S(2)}, u32[]{:S(2)}) collective-permute-start(f32[256,256]{1,0:T(8,128)S(1)} %get-tuple-element.27), channel_id=1, source_target_pairs={{0,1},{1,0},{2,3},{3,2},{4,5},{5,4},{6,7},{7,6},{8,9},{9,8},{10,11... | collective-permute-start | bytes 786440 | tf_op jit(solution)/shard_map/ppermute | solution.py:31
  8.2 1.9 %collective-permute-start.2 = (bf16[320,256]{1,0:T(8,128)(2,1)S(1)}, bf16[320,256]{1,0:T(8,128)(2,1)S(1)}, u32[]{:S(2)}, u32[]{:S(2)}) collective-permute-start(bf16[320,256]{1,0:T(8,128)(2,1)S(1)} %constant_dynamic-update-slice_fusion), channel_id=1, source_target_pairs={{0,1},{1,0},{2,3},{3,2},{4,5},{5,4},{6,7},{7,6},{8,9},{9,8},{10,11... | collective-permute-start | bytes 491528 | tf_op jit(solution)/shard_map/ppermute | solution.py:31
  10.7 4.4 %collective-permute-start.3 = (f16[136,256]{1,0:T(8,128)(2,1)S(1)}, f16[136,256]{1,0:T(8,128)(2,1)S(1)}, u32[]{:S(2)}, u32[]{:S(2)}) collective-permute-start(f16[136,256]{1,0:T(8,128)(2,1)S(1)} %select_convert_fusion.1), channel_id=1, source_target_pairs={{0,2},{1,3},{2,0},{3,1},{4,6},{5,7},{6,4},{7,5},{8,10},{9,11},{10,... | collective-permute-start | bytes 208904 | tf_op jit(solution)/shard_map/ppermute | solution.py:31
  15.3 4.9 %collective-permute-start.5 = (f16[200,256]{1,0:T(8,128)(2,1)S(1)}, f16[200,256]{1,0:T(8,128)(2,1)S(1)}, u32[]{:S(2)}, u32[]{:S(2)}) collective-permute-start(f16[200,256]{1,0:T(8,128)(2,1)S(1)} %fusion.1), channel_id=1, source_target_pairs={{0,4},{4,0},{8,12},{12,8},{16,20},{20,16},{24,28},{28,24},{1,5},{5... | collective-permute-start | bytes 307208 | tf_op jit(solution)/shard_map/ppermute | solution.py:31
  16.9 4.7 %collective-permute-start.6 = (f16[200,256]{1,0:T(8,128)(2,1)S(1)}, f16[200,256]{1,0:T(8,128)(2,1)S(1)}, u32[]{:S(2)}, u32[]{:S(2)}) collective-permute-start(f16[200,256]{1,0:T(8,128)(2,1)S(1)} %fusion.1), channel_id=1, source_target_pairs={{0,8},{4,12},{8,0},{12,4},{16,24},{20,28},{24,16},{28,20},{1,9},{5... | collective-permute-start | bytes 307208 | tf_op jit(solution)/shard_map/ppermute | solution.py:31
  18.4 5.6 %collective-permute-start.7 = (f16[200,256]{1,0:T(8,128)(2,1)S(1)}, f16[200,256]{1,0:T(8,128)(2,1)S(1)}, u32[]{:S(2)}, u32[]{:S(2)}) collective-permute-start(f16[200,256]{1,0:T(8,128)(2,1)S(1)} %fusion.1), channel_id=1, source_target_pairs={{0,12},{4,8},{8,4},{12,0},{16,28},{20,24},{24,20},{28,16},{1,13},{... | collective-permute-start | bytes 307208 | tf_op jit(solution)/shard_map/ppermute | solution.py:31
  18.9 8.2 %collective-permute-start.4 = (f32[128,256]{1,0:T(8,128)S(1)}, f32[128,256]{1,0:T(8,128)S(1)}, u32[]{:S(2)}, u32[]{:S(2)}) collective-permute-start(f32[128,256]{1,0:T(8,128)S(1)} %get-tuple-element.40), channel_id=1, source_target_pairs={{0,2},{1,3},{2,0},{3,1},{4,6},{5,7},{6,4},{7,5},{8,10},{9,11},{10,... | collective-permute-start | bytes 393224 | tf_op jit(solution)/shard_map/ppermute | solution.py:31
  24.2 6.6 %collective-permute-start.9 = (f16[200,256]{1,0:T(8,128)(2,1)S(1)}, f16[200,256]{1,0:T(8,128)(2,1)S(1)}, u32[]{:S(2)}, u32[]{:S(2)}) collective-permute-start(f16[200,256]{1,0:T(8,128)(2,1)S(1)} %select_convert_fusion), channel_id=1, source_target_pairs={{0,16},{4,20},{8,24},{12,28},{16,0},{20,4},{24,8},{28,12},{1,17},{... | collective-permute-start | bytes 307208 | tf_op jit(solution)/shard_map/ppermute | solution.py:31
  27.0 3.8 %collective-permute-start.8 = (f32[128,256]{1,0:T(8,128)S(1)}, f32[128,256]{1,0:T(8,128)S(1)}, u32[]{:S(2)}, u32[]{:S(2)}) collective-permute-start(f32[128,256]{1,0:T(8,128)S(1)} %add.41), channel_id=1, source_target_pairs={{0,1},{1,0},{2,3},{3,2},{4,5},{5,4},{6,7},{7,6},{8,9},{9,8},{10,11... | collective-permute-start | bytes 393224 | tf_op jit(solution)/shard_map/ppermute | solution.py:31

commit v3 on v2

--- a/solution.py
+++ b/solution.py
@@ -51,6 +51,14 @@
     hi = m.astype(BF16)
     lo = (m - hi.astype(F32)).astype(BF16)
     return jnp.dot(x, hi, preferred_element_type=F32) + jnp.dot(x, lo, preferred_element_type=F32)
+
+
+def exponent(top):
+    return jnp.clip(jnp.ceil(jnp.log2(jnp.maximum(top, 1e-30))), -100.0, 100.0)
+
+
+def column_top(v):
+    return jnp.max(jnp.abs(v), axis=0, keepdims=True)
 
 
 def prepare(a_ref, b_ref, c_ref, a_out, b_out, cb_out, ga_out):
@@ -112,19 +120,38 @@
         g_ref[...] = part if i == 0 else g_ref[...] + part
 
 
-def meet(to_height, g_ref, in_ref, own_ref, mate_ref, cy_ref, ga_ref, keep_ref, away_ref, *top_refs):
+def write_message(m_ref, *parts):
+    top = functools.reduce(jnp.maximum, [column_top(part) for part in parts])
+    e = exponent(top)
+    scale = jnp.exp2(TOP - e)
+    at = 0
+    for part in parts:
+        m_ref[at : at + part.shape[0]] = part * scale
+        at += part.shape[0]
+    m_ref[at:] = jnp.broadcast_to(e, (m_ref.shape[0] - at, e.shape[1]))
+
+
+def meet(to_height, g_ref, in_ref, own_ref, mate_ref, cy_ref, ga_ref, keep_ref, m_ref):
     h_own = cy_ref.shape[0]
     s_rows = own_ref.shape[0] - h_own
     sources = pl.ds(h_own, s_rows)
     m = ga_ref[...] * (gram(own_ref[sources]) + gram(mate_ref[sources]))
     g = g_ref[...] + in_ref[...]
     keep_ref[...] = (times(own_ref[0:h_own], m) - g[0:h_own]) * to_height
-    away_ref[...] = (times(cy_ref[...], m) - g[h_own:]) * to_height
-    for top, part in zip(top_refs, (keep_ref, away_ref)):
-        top[...] = column_top(part[...])
-
-
-def project_four(scales, x_ref, a_ref, b_ref, ga_ref, own_ref, mate_ref, cy_ref, pa_ref, ps_ref, top_ref, heights):
+    write_message(m_ref, (times(cy_ref[...], m) - g[h_own:]) * to_height)
+
+
+def combine(keep_ref, in_ref, ps_ref, m_ref):
+    h_own = keep_ref.shape[0]
+    share = keep_ref[...] + in_ref[0:h_own] * jnp.exp2(in_ref[h_own : h_own + 1] - TOP)
+    write_message(m_ref, share, ps_ref[...])
+
+
+def radius(to_radius, a_ref, b_ref, gc_ref, slab_ref, pa_ref):
+    pa_ref[...] = (times(a_ref[...], gram(b_ref[...]) * gc_ref[...]) - slab_ref[...]) * to_radius
+
+
+def project_four(to_source, x_ref, a_ref, b_ref, ga_ref, own_ref, mate_ref, cy_ref, pa_ref, ps_ref, gc_ref, heights):
     s_rows, rank = b_ref.shape
     r_rows = a_ref.shape[0]
     h_own = cy_ref.shape[0]
@@ -134,13 +161,11 @@
         heights[pl.ds(pl.multiple_of((me ^ o) * h_own, h_own), h_own)] = part
     x = x_ref[...].reshape(r_rows * s_rows, x_ref.shape[2])
     proj = jnp.dot(x, heights[...], preferred_element_type=F32).reshape(r_rows, s_rows, rank)
-    pa = (proj * b_ref[...].astype(F32)[None]).sum(1)
+    pa_ref[...] = (proj * b_ref[...].astype(F32)[None]).sum(1)
     ps = (proj * a_ref[...].astype(F32)[:, None, :]).sum(0)
     gc = gram(heights[...])
-    to_radius, _, to_source = scales
-    pa_ref[...] = (times(a_ref[...], gram(b_ref[...]) * gc) - pa) * to_radius
+    gc_ref[...] = gc
     ps_ref[...] = (times(b_ref[...], ga_ref[...] * gc) - ps) * to_source
-    top_ref[...] = column_top(ps_ref[...])
 
 
 def local_four(slab, radius_factor, height_factor, source_factor, scales):
@@ -170,23 +195,27 @@
     (g_keep,) = call(
         functools.partial(height_terms, (0, 2)), [((width // 2, rank), F32)], (x, after(a, cby), b), work // 2
     )
-    keep, away, keep_top, away_top = call(
+    keep, away = call(
         functools.partial(meet, scales[1]),
-        [((h_own, rank), F32), ((h_own, rank), F32), ((1, rank), F32), ((1, rank), F32)],
+        [((h_own, rank), F32), ((h_own + TAIL, rank), F32)],
         (g_keep, g_in, cb, mate, cy, ga),
         work // 8,
     )
-    away = pack(padded(away), exponent(away_top))
-    share_in, e_in = unpack(swap(away, "src", 2))
-    share_in = share_in[:h_own]
-    pa, ps, ps_top = call(
-        functools.partial(project_four, scales),
-        [((r_rows, rank), F32), ((s_rows, rank), F32), ((1, rank), F32)],
+    away = away.astype(F16)
+    share_in = swap(away, "src", 2)
+    pa, ps, gc = call(
+        functools.partial(project_four, scales[2]),
+        [((r_rows, rank), F32), ((s_rows, rank), F32), ((rank, rank), F32)],
         (x, after(a, away), b, ga, cb, mate, cy),
         work,
         scratch=[pltpu.VMEM((width, rank), BF16)],
     )
-    return pa, ps, keep + share_in, exponent(jnp.maximum(ps_top, keep_top + jnp.exp2(e_in)))
+    (m,) = call(combine, [((h_own + s_rows + TAIL, rank), F32)], (keep, share_in.astype(F32), ps), work // 32)
+    m = m.astype(F16)
+    (pa,) = call(
+        functools.partial(radius, scales[0]), [((r_rows, rank), F32)], (a, b, gc, after(pa, m)), work // 32
+    )
+    return pa, m
 
 
 def project(scales, n_src, x_ref, a_ref, b_ref, ga_ref, *refs):
@@ -262,17 +291,15 @@
         scratch=[pltpu.VMEM((width, rank), BF16)],
     )
     ph = ph - (g[:h_own] + share_in) * scales[1]
-    return pa, ps, ph, exponent(jnp.maximum(column_top(ph), column_top(ps)))
-
-
-def split(v_ref, h_ref, s_ref):
+    e = exponent(jnp.maximum(column_top(ph), column_top(ps)))
+    return pa, pack(jnp.concatenate([ph, ps, jnp.zeros((TAIL, rank), F32)], axis=0), e)
+
+
+def finish(v_ref, pa_ref, in_ref, r_ref, h_ref, s_ref):
     h_own = h_ref.shape[0]
+    r_ref[...] = pa_ref[...] + in_ref[...]
     h_ref[...] = v_ref[0:h_own]
     s_ref[...] = v_ref[h_own : h_own + s_ref.shape[0]]
-
-
-def exponent(top):
-    return jnp.clip(jnp.ceil(jnp.log2(jnp.maximum(top, 1e-30))), -100.0, 100.0)
 
 
 def pack(v, e):
@@ -283,14 +310,6 @@
 def unpack(m):
     e = m[-1:].astype(F32)
     return m.astype(F32) * jnp.exp2(e - TOP), e
-
-
-def padded(*parts):
-    return jnp.concatenate([*parts, jnp.zeros((TAIL, parts[0].shape[1]), F32)], axis=0)
-
-
-def column_top(v):
-    return jnp.max(jnp.abs(v), axis=0, keepdims=True)
 
 
 def per_device(slab, radius_factor, height_factor, source_factor):
@@ -307,30 +326,30 @@
     rad_bits = [1 << i for i in range(n_rad.bit_length() - 1)]
 
     local = local_four if n_src == 4 and h_own % LANES == 0 else local_any
-    pa, ps, ph, e = local(slab, radius_factor, height_factor, source_factor, scales)
-    v = padded(ph, ps)
+    pa, m = local(slab, radius_factor, height_factor, source_factor, scales)
     bits = src_bits[::-1]
-    for stage in [rad_bits[i : i + 2] for i in range(0, len(rad_bits), 2)]:
-        m = pack(v, e)
-        others = [0, *stage] if len(stage) == 1 else [0, stage[0], stage[1], sum(stage)]
-        terms = [unpack(m)] + [unpack(swap(m, "rad", o)) for o in others[1:]]
-        if bits:
+    stages = [rad_bits[i : i + 2] for i in range(0, len(rad_bits), 2)]
+    for i, stage in enumerate(stages):
+        others = stage if len(stage) == 1 else [*stage, sum(stage)]
+        terms = [unpack(m)] + [unpack(swap(m, "rad", o)) for o in others]
+        if len(bits) > 1:
             pa = after(pa, m)
             pa = pa + swap(pa, "src", bits.pop(0))
         values = [value for value, _ in terms]
         while len(values) > 1:
             values = [a + b for a, b in zip(values[0::2], values[1::2])]
         (v,) = values
-        e = functools.reduce(jnp.maximum, [x for _, x in terms]) + len(stage)
-    for bit in bits:
-        pa = pa + swap(pa, "src", bit)
-    grad_height, grad_source = pl.pallas_call(
-        split,
-        in_specs=[WHOLE],
-        out_specs=[WHOLE] * 2,
-        out_shape=[jax.ShapeDtypeStruct((h_own, rank), F32), jax.ShapeDtypeStruct((s_rows, rank), F32)],
-    )(inside(after(v, pa)))
-    return pa, grad_height, grad_source
+        if i + 1 < len(stages):
+            m = pack(v, functools.reduce(jnp.maximum, [x for _, x in terms]) + len(stage))
+    while len(bits) > 1:
+        pa = pa + swap(pa, "src", bits.pop(0))
+    pa_in = swap(after(pa, m), "src", bits[0])
+    return pl.pallas_call(
+        finish,
+        in_specs=[WHOLE] * 3,
+        out_specs=[WHOLE] * 3,
+        out_shape=[jax.ShapeDtypeStruct((rows, rank), F32) for rows in (r_rows, h_own, s_rows)],
+    )(inside(v), inside(pa), inside(pa_in))
 
 
 def solution(mesh):

time: 32.4 us -> 31.5 us (0.972)
  other arithmetic: 1.22 us -> 0.25 us
  Pallas kernels: 9.55 us -> 10 us
  waiting for transfers between devices: 9.94 us -> 9.6 us
    add x2 -> x1, other arithmetic: 0.69 us -> 0.02 us  [per_device(): pa = pa + swap(pa, 'src', bits.pop(0))]
    pallas_call x3 -> x5, Pallas kernels: 4.59 us -> 4.98 us  [call(): pl.pallas_call(body, in_specs=[WHOLE] * len(args), out_specs=[WHOLE] * le...]
    ppermute x10, waiting for transfers between devices: 9.94 us -> 9.6 us  [swap(): lax.ppermute(x, axis, [(i, i ^ bit) for i in range(lax.axis_size(axis))])]
  transfers between devices with their start and end apart: 10 -> 10, of which waited for: 5 -> 5; matrix products, arithmetic and copies ran while one was open for 1% -> 1% of each run, Pallas kernels for 26% -> 28%
where the time goes in v3:
time: 31.5 us; the launch traced here: 31.3 us
  starting transfers between devices  10.6 us (34%)
  Pallas kernels  10 us (32%)
  waiting for transfers between devices  9.6 us (30%)
  between operations  0.79 us (3%)
    ppermute x10, starting transfers between devices, swap(): lax.ppermute(x, axis, [(i, i ^ bit) for i in range(lax.axis_size(axis))])  10.6 us
    ppermute x10, waiting for transfers between devices, swap(): lax.ppermute(x, axis, [(i, i ^ bit) for i in range(lax.axis_size(axis))])  9.6 us
    pallas_call x5, Pallas kernels, call(): pl.pallas_call(body, in_specs=[WHOLE] * len(args), out_specs=[WHOLE] * le...  4.98 us
    pallas_call x1, Pallas kernels, local_four(): pl.pallas_call(functools.partial(load, (1, 3)), in_specs=[pl.BlockSpec(me...  4.28 us
    pallas_call x1, Pallas kernels, per_device(): pl.pallas_call(finish, in_specs=[WHOLE] * 3, out_specs=[WHOLE] * 3, out_s...  0.74 us
  transfers between devices with their start and end apart: 10, of which 5 were waited for; matrix products, arithmetic and copies ran while one was open for 1% of the time, Pallas kernels for 28%

profile of v3, /device:TPU:0, one launch (start us, length us, event | category | flops | bytes accessed | tf_op | source)
XLA Modules:
  0.0 31.3 jit_solution(4088619741805906994)
XLA Ops:
  0.6 3.0 %collective-permute-start = (bf16[128,256]{1,0:T(8,128)(2,1)}, bf16[128,256]{1,0:T(8,128)(2,1)S(1)}, u32[]{:S(2)}, u32[]{:S(2)}) collective-permute-start(bf16[128,256]{1,0:T(8,128)(2,1)} %c_hbm.1), channel_id=1, source_target_pairs={{0,2},{1,3},{2,0},{3,1},{4,6},{5,7},{6,4},{7,5},{8,10},{9,11},{10,... | collective-permute-start | bytes 196616 | tf_op jit(solution)/shard_map/ppermute | solution.py:31
  3.7 4.3 %shard_map.67 = (bf16[128,64,512]{2,1,0:T(8,128)(2,1)S(1)}, bf16[128,256]{1,0:T(8,128)(2,1)S(1)}, bf16[64,256]{1,0:T(8,128)(2,1)S(1)}, bf16[192,256]{1,0:T(8,128...) custom-call(bf16[128,64,512]{2,1,0:T(8,128)(2,1)} %x_hbm.1, bf16[128,256]{1,0:T(8,128)(2,1)} %a_hbm.1, ...), custom_call_target="tpu_custom_call" | custom-call | flops 4294967296 | tf_op jit(solution)/shard_map/pallas_call | solution.py:176
  8.0 0.1 collective-permute-start.1
  8.0 0.0 collective-permute-done.cy_ref
  8.1 0.5 %collective-permute-start.2 = (bf16[320,256]{1,0:T(8,128)(2,1)S(1)}, bf16[320,256]{1,0:T(8,128)(2,1)S(1)}, u32[]{:S(2)}, u32[]{:S(2)}) collective-permute-start(bf16[320,256]{1,0:T(8,128)(2,1)S(1)} %constant_dynamic-update-slice_fusion), channel_id=1, source_target_pairs={{0,1},{1,0},{2,3},{3,2},{4,5},{5,4},{6,7},{7,6},{8,9},{9,8},{10,11... | collective-permute-start | bytes 491528 | tf_op jit(solution)/shard_map/ppermute | solution.py:31
  8.6 1.3 %shard_map.68.g_ref = f32[256,256]{1,0:T(8,128)S(1)} custom-call(bf16[128,64,512]{2,1,0:T(8,128)(2,1)S(1)} %get-tuple-element.20.x_ref, bf16[128,256]{1,0:T(8,128)(2,1)S(1)} %get-tuple-element.30.a_ref, bf16[64,256]{1,0:T(8,128)(2,1)S(1)} %get-tuple-element.26.b_ref), custom_call_target="tpu_custom_call" | custom-call | flops 1073741824 | tf_op jit(solution)/shard_map/pallas_call | solution.py:35
  9.9 0.0 collective-permute-done.2.mate_ref
  9.9 0.0 collective-permute-done.1.in_ref
  10.0 0.6 %shard_map.69 = (f32[128,256]{1,0:T(8,128)S(1)}, f32[136,256]{1,0:T(8,128)S(1)}) custom-call(f32[256,256]{1,0:T(8,128)S(1)} %shard_map.68.g_ref, f32[256,256]{1,0:T(8,128)S(1)} %collective-permute-done.1.in_ref, bf16[192,256]{1,0:T(8,128)(2,1)S(1)} %get-tuple-element.22.own_ref, bf16[320,256]{1,0:T(8,128)(2,1)S(1)} %collective-permute-done.2.mate_ref, ...), custom_call_target="tpu_custom_call" | custom-call | flops 268435456 | tf_op jit(solution)/shard_map/pallas_call | solution.py:35
  10.6 0.1 collective-permute-start.3
  10.7 2.6 %shard_map.70 = (f32[128,256]{1,0:T(8,128)S(1)}, f32[64,256]{1,0:T(8,128)S(1)}, f32[256,256]{1,0:T(8,128)S(1)}) custom-call(bf16[128,64,512]{2,1,0:T(8,128)(2,1)S(1)} %get-tuple-element.20.x_ref, bf16[128,256]{1,0:T(8,128)(2,1)S(1)} %get-tuple-element.30.a_ref, bf16[64,256]{1,0:T(8,128)(2,1)S(1)} %get-tuple-element.26.b_ref, ...), custom_call_target="tpu_custom_call" | custom-call | flops 2147483648 | tf_op jit(solution)/shard_map/pallas_call | solution.py:35
  13.3 1.7 %collective-permute-done.3 = f16[136,256]{1,0:T(8,128)(2,1)S(1)} collective-permute-done((f16[136,256]{1,0:T(8,128)(2,1)S(1)}, f16[136,256]{1,0:T(8,128)(2,1)S(1)}, u32[]{:S(2)}, u32[]{:S(2)}) %collective-permute-start.3) | collective-permute-done | bytes 69664 | tf_op jit(solution)/shard_map/ppermute | solution.py:31
  15.0 0.1 shard_map.71
  15.1 1.6 %collective-permute-start.4 = (f16[200,256]{1,0:T(8,128)(2,1)S(1)}, f16[200,256]{1,0:T(8,128)(2,1)S(1)}, u32[]{:S(2)}, u32[]{:S(2)}) collective-permute-start(f16[200,256]{1,0:T(8,128)(2,1)S(1)} %convert_element_type.50), channel_id=1, source_target_pairs={{0,4},{4,0},{8,12},{12,8},{16,20},{20,16},{24,28},{28,24},{1,5},{5... | collective-permute-start | bytes 307208 | tf_op jit(solution)/shard_map/ppermute | solution.py:31
  16.6 1.6 %collective-permute-start.5 = (f16[200,256]{1,0:T(8,128)(2,1)S(1)}, f16[200,256]{1,0:T(8,128)(2,1)S(1)}, u32[]{:S(2)}, u32[]{:S(2)}) collective-permute-start(f16[200,256]{1,0:T(8,128)(2,1)S(1)} %convert_element_type.50), channel_id=1, source_target_pairs={{0,8},{4,12},{8,0},{12,4},{16,24},{20,28},{24,16},{28,20},{1,9},{5... | collective-permute-start | bytes 307208 | tf_op jit(solution)/shard_map/ppermute | solution.py:31
  18.2 0.4 %collective-permute-start.6 = (f16[200,256]{1,0:T(8,128)(2,1)S(1)}, f16[200,256]{1,0:T(8,128)(2,1)S(1)}, u32[]{:S(2)}, u32[]{:S(2)}) collective-permute-start(f16[200,256]{1,0:T(8,128)(2,1)S(1)} %convert_element_type.50), channel_id=1, source_target_pairs={{0,12},{4,8},{8,4},{12,0},{16,28},{20,24},{24,20},{28,16},{1,13},{... | collective-permute-start | bytes 307208 | tf_op jit(solution)/shard_map/ppermute | solution.py:31
  18.6 0.4 %shard_map.72 = f32[128,256]{1,0:T(8,128)S(1)} custom-call(bf16[128,256]{1,0:T(8,128)(2,1)S(1)} %get-tuple-element.30.a_ref, bf16[64,256]{1,0:T(8,128)(2,1)S(1)} %get-tuple-element.26.b_ref, f32[256,256]{1,0:T(8,128)S(1)} %get-tuple-element.32.gc_ref, f32[128,256]{1,0:T(8,128)S(1)} %get-tuple-element.34.slab_ref), custom_call_target="tpu_custom_call" | custom-call | flops 67108864 | tf_op jit(solution)/shard_map/pallas_call | solution.py:35
  19.0 0.4 %collective-permute-start.8 = (f32[128,256]{1,0:T(8,128)S(1)}, f32[128,256]{1,0:T(8,128)S(1)}, u32[]{:S(2)}, u32[]{:S(2)}) collective-permute-start(f32[128,256]{1,0:T(8,128)S(1)} %shard_map.72), channel_id=1, source_target_pairs={{0,2},{1,3},{2,0},{3,1},{4,6},{5,7},{6,4},{7,5},{8,10},{9,11},{10,... | collective-permute-start | bytes 393224 | tf_op jit(solution)/shard_map/ppermute | solution.py:31
  19.5 0.5 %collective-permute-done.4 = f16[200,256]{1,0:T(8,128)(2,1)S(1)} collective-permute-done((f16[200,256]{1,0:T(8,128)(2,1)S(1)}, f16[200,256]{1,0:T(8,128)(2,1)S(1)}, u32[]{:S(2)}, u32[]{:S(2)}) %collective-permute-start.4) | collective-permute-done | bytes 102432 | tf_op jit(solution)/shard_map/ppermute | solution.py:31
  19.9 1.4 %collective-permute-done.5 = f16[200,256]{1,0:T(8,128)(2,1)S(1)} collective-permute-done((f16[200,256]{1,0:T(8,128)(2,1)S(1)}, f16[200,256]{1,0:T(8,128)(2,1)S(1)}, u32[]{:S(2)}, u32[]{:S(2)}) %collective-permute-start.5) | collective-permute-done | bytes 102432 | tf_op jit(solution)/shard_map/ppermute | solution.py:31
  21.3 2.4 %collective-permute-done.6 = f16[200,256]{1,0:T(8,128)(2,1)S(1)} collective-permute-done((f16[200,256]{1,0:T(8,128)(2,1)S(1)}, f16[200,256]{1,0:T(8,128)(2,1)S(1)}, u32[]{:S(2)}, u32[]{:S(2)}) %collective-permute-start.6) | collective-permute-done | bytes 102432 | tf_op jit(solution)/shard_map/ppermute | solution.py:31
  23.8 0.1 select_convert_fusion
  23.9 2.9 %collective-permute-start.7 = (f16[200,256]{1,0:T(8,128)(2,1)S(1)}, f16[200,256]{1,0:T(8,128)(2,1)S(1)}, u32[]{:S(2)}, u32[]{:S(2)}) collective-permute-start(f16[200,256]{1,0:T(8,128)(2,1)S(1)} %select_convert_fusion), channel_id=1, source_target_pairs={{0,16},{4,20},{8,24},{12,28},{16,0},{20,4},{24,8},{28,12},{1,17},{... | collective-permute-start | bytes 307208 | tf_op jit(solution)/shard_map/ppermute | solution.py:31
  26.8 0.0 collective-permute-done.8
  26.8 0.1 collective-permute-start.9
  26.9 3.6 %collective-permute-done.7 = f16[200,256]{1,0:T(8,128)(2,1)S(1)} collective-permute-done((f16[200,256]{1,0:T(8,128)(2,1)S(1)}, f16[200,256]{1,0:T(8,128)(2,1)S(1)}, u32[]{:S(2)}, u32[]{:S(2)}) %collective-permute-start.7) | collective-permute-done | bytes 102432 | tf_op jit(solution)/shard_map/ppermute | solution.py:31
  30.6 0.0 collective-permute-done.9.in_ref
  30.6 0.7 %shard_map.73 = (f32[128,256]{1,0:T(8,128)}, f32[128,256]{1,0:T(8,128)}, f32[64,256]{1,0:T(8,128)}) custom-call(f32[200,256]{1,0:T(8,128)S(1)} %multiply_add_fusion.v_ref, f32[128,256]{1,0:T(8,128)S(1)} %add.33.pa_ref, f32[128,256]{1,0:T(8,128)S(1)} %collective-permute-done.9.in_ref), custom_call_target="tpu_custom_call" | custom-call | tf_op jit(solution)/shard_map/pallas_call | solution.py:347
  (11 shorter events, 0.2 us)
Async XLA Ops:
  0.6 7.4 %collective-permute-start = (bf16[128,256]{1,0:T(8,128)(2,1)}, bf16[128,256]{1,0:T(8,128)(2,1)S(1)}, u32[]{:S(2)}, u32[]{:S(2)}) collective-permute-start(bf16[128,256]{1,0:T(8,128)(2,1)} %c_hbm.1), channel_id=1, source_target_pairs={{0,2},{1,3},{2,0},{3,1},{4,6},{5,7},{6,4},{7,5},{8,10},{9,11},{10,... | collective-permute-start | bytes 196616 | tf_op jit(solution)/shard_map/ppermute | solution.py:31
  8.0 2.0 %collective-permute-start.1 = (f32[256,256]{1,0:T(8,128)S(1)}, f32[256,256]{1,0:T(8,128)S(1)}, u32[]{:S(2)}, u32[]{:S(2)}) collective-permute-start(f32[256,256]{1,0:T(8,128)S(1)} %get-tuple-element.23), channel_id=1, source_target_pairs={{0,1},{1,0},{2,3},{3,2},{4,5},{5,4},{6,7},{7,6},{8,9},{9,8},{10,11... | collective-permute-start | bytes 786440 | tf_op jit(solution)/shard_map/ppermute | solution.py:31
  8.1 1.9 %collective-permute-start.2 = (bf16[320,256]{1,0:T(8,128)(2,1)S(1)}, bf16[320,256]{1,0:T(8,128)(2,1)S(1)}, u32[]{:S(2)}, u32[]{:S(2)}) collective-permute-start(bf16[320,256]{1,0:T(8,128)(2,1)S(1)} %constant_dynamic-update-slice_fusion), channel_id=1, source_target_pairs={{0,1},{1,0},{2,3},{3,2},{4,5},{5,4},{6,7},{7,6},{8,9},{9,8},{10,11... | collective-permute-start | bytes 491528 | tf_op jit(solution)/shard_map/ppermute | solution.py:31
  10.6 4.4 %collective-permute-start.3 = (f16[136,256]{1,0:T(8,128)(2,1)S(1)}, f16[136,256]{1,0:T(8,128)(2,1)S(1)}, u32[]{:S(2)}, u32[]{:S(2)}) collective-permute-start(f16[136,256]{1,0:T(8,128)(2,1)S(1)} %convert_element_type.48), channel_id=1, source_target_pairs={{0,2},{1,3},{2,0},{3,1},{4,6},{5,7},{6,4},{7,5},{8,10},{9,11},{10,... | collective-permute-start | bytes 208904 | tf_op jit(solution)/shard_map/ppermute | solution.py:31
  15.1 4.9 %collective-permute-start.4 = (f16[200,256]{1,0:T(8,128)(2,1)S(1)}, f16[200,256]{1,0:T(8,128)(2,1)S(1)}, u32[]{:S(2)}, u32[]{:S(2)}) collective-permute-start(f16[200,256]{1,0:T(8,128)(2,1)S(1)} %convert_element_type.50), channel_id=1, source_target_pairs={{0,4},{4,0},{8,12},{12,8},{16,20},{20,16},{24,28},{28,24},{1,5},{5... | collective-permute-start | bytes 307208 | tf_op jit(solution)/shard_map/ppermute | solution.py:31
  16.6 4.7 %collective-permute-start.5 = (f16[200,256]{1,0:T(8,128)(2,1)S(1)}, f16[200,256]{1,0:T(8,128)(2,1)S(1)}, u32[]{:S(2)}, u32[]{:S(2)}) collective-permute-start(f16[200,256]{1,0:T(8,128)(2,1)S(1)} %convert_element_type.50), channel_id=1, source_target_pairs={{0,8},{4,12},{8,0},{12,4},{16,24},{20,28},{24,16},{28,20},{1,9},{5... | collective-permute-start | bytes 307208 | tf_op jit(solution)/shard_map/ppermute | solution.py:31
  18.2 5.6 %collective-permute-start.6 = (f16[200,256]{1,0:T(8,128)(2,1)S(1)}, f16[200,256]{1,0:T(8,128)(2,1)S(1)}, u32[]{:S(2)}, u32[]{:S(2)}) collective-permute-start(f16[200,256]{1,0:T(8,128)(2,1)S(1)} %convert_element_type.50), channel_id=1, source_target_pairs={{0,12},{4,8},{8,4},{12,0},{16,28},{20,24},{24,20},{28,16},{1,13},{... | collective-permute-start | bytes 307208 | tf_op jit(solution)/shard_map/ppermute | solution.py:31
  19.0 7.7 %collective-permute-start.8 = (f32[128,256]{1,0:T(8,128)S(1)}, f32[128,256]{1,0:T(8,128)S(1)}, u32[]{:S(2)}, u32[]{:S(2)}) collective-permute-start(f32[128,256]{1,0:T(8,128)S(1)} %shard_map.72), channel_id=1, source_target_pairs={{0,2},{1,3},{2,0},{3,1},{4,6},{5,7},{6,4},{7,5},{8,10},{9,11},{10,... | collective-permute-start | bytes 393224 | tf_op jit(solution)/shard_map/ppermute | solution.py:31
  23.9 6.6 %collective-permute-start.7 = (f16[200,256]{1,0:T(8,128)(2,1)S(1)}, f16[200,256]{1,0:T(8,128)(2,1)S(1)}, u32[]{:S(2)}, u32[]{:S(2)}) collective-permute-start(f16[200,256]{1,0:T(8,128)(2,1)S(1)} %select_convert_fusion), channel_id=1, source_target_pairs={{0,16},{4,20},{8,24},{12,28},{16,0},{20,4},{24,8},{28,12},{1,17},{... | collective-permute-start | bytes 307208 | tf_op jit(solution)/shard_map/ppermute | solution.py:31
  26.8 3.8 %collective-permute-start.9 = (f32[128,256]{1,0:T(8,128)S(1)}, f32[128,256]{1,0:T(8,128)S(1)}, u32[]{:S(2)}, u32[]{:S(2)}) collective-permute-start(f32[128,256]{1,0:T(8,128)S(1)} %add.33.pa_ref), channel_id=1, source_target_pairs={{0,1},{1,0},{2,3},{3,2},{4,5},{5,4},{6,7},{7,6},{8,9},{9,8},{10,11... | collective-permute-start | bytes 393224 | tf_op jit(solution)/shard_map/ppermute | solution.py:31

commit v4 on v3

--- a/solution.py
+++ b/solution.py
@@ -47,9 +47,13 @@
     return lax.dot_general(x, x, (((0,), (0,)), ((), ())), preferred_element_type=F32)
 
 
+def halves(m):
+    hi = m.astype(BF16)
+    return hi, (m - hi.astype(F32)).astype(BF16)
+
+
 def times(x, m):
-    hi = m.astype(BF16)
-    lo = (m - hi.astype(F32)).astype(BF16)
+    hi, lo = halves(m)
     return jnp.dot(x, hi, preferred_element_type=F32) + jnp.dot(x, lo, preferred_element_type=F32)
 
 
@@ -120,6 +124,22 @@
         g_ref[...] = part if i == 0 else g_ref[...] + part
 
 
+def begin(o_ref):
+    o_ref[...] = jnp.zeros_like(o_ref)
+
+
+def products(a_in, b_in, t_ref, a_ref, b_ref, ga_ref):
+    a_ref[...] = a_in[...]
+    b_ref[...] = b_in[...]
+    ga_ref[...] = gram(a_in[...])
+
+
+def terms(b_ref, b1_ref, ga_ref, own_ref, c2_ref, keep_ref, away_ref):
+    parts = halves(ga_ref[...] * (gram(b_ref[...]) + gram(b1_ref[...])))
+    for rows, out in ((own_ref, keep_ref), (c2_ref, away_ref)):
+        out[...] = sum(jnp.dot(rows[...], part, preferred_element_type=F32) for part in parts)
+
+
 def write_message(m_ref, *parts):
     top = functools.reduce(jnp.maximum, [column_top(part) for part in parts])
     e = exponent(top)
@@ -131,14 +151,11 @@
     m_ref[at:] = jnp.broadcast_to(e, (m_ref.shape[0] - at, e.shape[1]))
 
 
-def meet(to_height, g_ref, in_ref, own_ref, mate_ref, cy_ref, ga_ref, keep_ref, m_ref):
-    h_own = cy_ref.shape[0]
-    s_rows = own_ref.shape[0] - h_own
-    sources = pl.ds(h_own, s_rows)
-    m = ga_ref[...] * (gram(own_ref[sources]) + gram(mate_ref[sources]))
+def meet(to_height, g_ref, in_ref, keep_in, away_in, keep_ref, m_ref):
+    h_own = keep_in.shape[0]
     g = g_ref[...] + in_ref[...]
-    keep_ref[...] = (times(own_ref[0:h_own], m) - g[0:h_own]) * to_height
-    write_message(m_ref, (times(cy_ref[...], m) - g[h_own:]) * to_height)
+    keep_ref[...] = (keep_in[...] - g[0:h_own]) * to_height
+    write_message(m_ref, (away_in[...] - g[h_own:]) * to_height)
 
 
 def combine(keep_ref, in_ref, ps_ref, m_ref):
@@ -151,14 +168,13 @@
     pa_ref[...] = (times(a_ref[...], gram(b_ref[...]) * gc_ref[...]) - slab_ref[...]) * to_radius
 
 
-def project_four(to_source, x_ref, a_ref, b_ref, ga_ref, own_ref, mate_ref, cy_ref, pa_ref, ps_ref, gc_ref, heights):
+def project_four(to_source, x_ref, a_ref, b_ref, ga_ref, c0, c1, c2, c3, pa_ref, ps_ref, gc_ref, heights):
     s_rows, rank = b_ref.shape
     r_rows = a_ref.shape[0]
-    h_own = cy_ref.shape[0]
+    h_own = c0.shape[0]
     me = lax.axis_index("src")
-    parts = (own_ref[0:h_own], mate_ref[0:h_own], cy_ref[...], mate_ref[h_own + s_rows :])
-    for o, part in enumerate(parts):
-        heights[pl.ds(pl.multiple_of((me ^ o) * h_own, h_own), h_own)] = part
+    for o, part in enumerate((c0, c1, c2, c3)):
+        heights[pl.ds(pl.multiple_of((me ^ o) * h_own, h_own), h_own)] = part[...]
     x = x_ref[...].reshape(r_rows * s_rows, x_ref.shape[2])
     proj = jnp.dot(x, heights[...], preferred_element_type=F32).reshape(r_rows, s_rows, rank)
     pa_ref[...] = (proj * b_ref[...].astype(F32)[None]).sum(1)
@@ -172,41 +188,37 @@
     r_rows, s_rows, width = slab.shape
     h_own, rank = height_factor.shape
     work = 2 * r_rows * s_rows * width * rank
-    cy = swap(height_factor, "src", 2)
-    x, a, b, cb, ga, g_away = pl.pallas_call(
-        functools.partial(load, (1, 3)),
-        in_specs=[pl.BlockSpec(memory_space=pl.ANY)] * 4,
-        out_specs=[WHOLE] * 6,
-        out_shape=[
-            pltpu.VMEM(slab.shape, BF16),
-            pltpu.VMEM(radius_factor.shape, BF16),
-            pltpu.VMEM(source_factor.shape, BF16),
-            pltpu.VMEM((h_own + s_rows, rank), BF16),
-            pltpu.VMEM((rank, rank), F32),
-            pltpu.VMEM((width // 2, rank), F32),
-        ],
-        scratch_shapes=[pltpu.SemaphoreType.DMA((4 + CHUNKS,))],
-        compiler_params=pltpu.CompilerParams(vmem_limit_bytes=LOAD_LIMIT),
-        cost_estimate=pl.CostEstimate(flops=2 * work, bytes_accessed=0, transcendentals=0),
-    )(slab, radius_factor, source_factor, height_factor)
+    c2 = swap(height_factor, "src", 2)
+    c3 = swap(height_factor, "src", 3)
+    c1 = swap(height_factor, "src", 1)
+    b1 = swap(source_factor, "src", 1)
+    (tick,) = call(begin, [((8, LANES), F32)], (), 2 * work)
+    a, b, ga = call(
+        products,
+        [((r_rows, rank), BF16), ((s_rows, rank), BF16), ((rank, rank), F32)],
+        (radius_factor, source_factor, tick),
+        work // 8,
+        resident=False,
+    )
+    half, block = [((width // 2, rank), F32)], [((h_own, rank), F32)]
+    (g_away,) = call(functools.partial(height_terms, (1, 3)), half, (slab, a, b), 2 * work, resident=False)
     g_in = swap(g_away, "src", 1)
-    cby = jnp.concatenate([cb, after(cy, g_away)], axis=0)
-    mate = swap(cby, "src", 1)
     (g_keep,) = call(
-        functools.partial(height_terms, (0, 2)), [((width // 2, rank), F32)], (x, after(a, cby), b), work // 2
-    )
+        functools.partial(height_terms, (0, 2)), half, (slab, after(a, g_away, b1), b), 4 * work
+    )
+    keep, away = call(terms, block * 2, (after(b, g_keep), b1, ga, height_factor, c2), work // 8)
     keep, away = call(
         functools.partial(meet, scales[1]),
-        [((h_own, rank), F32), ((h_own + TAIL, rank), F32)],
-        (g_keep, g_in, cb, mate, cy, ga),
-        work // 8,
+        block + [((h_own + TAIL, rank), F32)],
+        (g_keep, g_in, keep, away),
+        work // 32,
     )
     away = away.astype(F16)
     share_in = swap(away, "src", 2)
     pa, ps, gc = call(
         functools.partial(project_four, scales[2]),
         [((r_rows, rank), F32), ((s_rows, rank), F32), ((rank, rank), F32)],
-        (x, after(a, away), b, ga, cb, mate, cy),
+        (slab, after(a, away), b, ga, height_factor, c1, c2, c3),
         work,
         scratch=[pltpu.VMEM((width, rank), BF16)],
     )

time: 31.5 us -> 30.2 us (0.959)
  starting transfers between devices: 10.6 us -> 14.4 us
  Pallas kernels: 10 us -> 7.28 us
  waiting for transfers between devices: 9.6 us -> 7.3 us
    pallas_call x1 -> x0, Pallas kernels: 4.28 us -> none  [local_four(): pl.pallas_call(functools.partial(load, (1, 3)), in_specs=[pl.BlockSpec(me...]
    ppermute x10 -> x12, starting transfers between devices: 10.6 us -> 14.4 us  [swap(): lax.ppermute(x, axis, [(i, i ^ bit) for i in range(lax.axis_size(axis))])]
    ppermute x10 -> x12, waiting for transfers between devices: 9.6 us -> 7.3 us  [swap(): lax.ppermute(x, axis, [(i, i ^ bit) for i in range(lax.axis_size(axis))])]
    pallas_call x5 -> x9, Pallas kernels: 4.98 us -> 6.54 us  [call(): pl.pallas_call(body, in_specs=[WHOLE] * len(args), out_specs=[WHOLE] * le...]
  transfers between devices with their start and end apart: 10 -> 12, of which waited for: 5 -> 4; matrix products, arithmetic and copies ran while one was open for 1% -> 1% of each run, Pallas kernels for 28% -> 22%
where the time goes in v4:
time: 30.2 us; the launch traced here: 30.1 us
  starting transfers between devices  14.4 us (48%)
  waiting for transfers between devices  7.3 us (24%)
  Pallas kernels  7.28 us (24%)
  between operations  0.82 us (3%)
    ppermute x12, starting transfers between devices, swap(): lax.ppermute(x, axis, [(i, i ^ bit) for i in range(lax.axis_size(axis))])  14.4 us
    ppermute x12, waiting for transfers between devices, swap(): lax.ppermute(x, axis, [(i, i ^ bit) for i in range(lax.axis_size(axis))])  7.3 us
    pallas_call x9, Pallas kernels, call(): pl.pallas_call(body, in_specs=[WHOLE] * len(args), out_specs=[WHOLE] * le...  6.54 us
    pallas_call x1, Pallas kernels, per_device(): pl.pallas_call(finish, in_specs=[WHOLE] * 3, out_specs=[WHOLE] * 3, out_s...  0.74 us
  transfers between devices with their start and end apart: 12, of which 4 were waited for; matrix products, arithmetic and copies ran while one was open for 1% of the time, Pallas kernels for 22%

profile of v4, /device:TPU:0, one launch (start us, length us, event | category | flops | bytes accessed | tf_op | source)
XLA Modules:
  0.0 30.1 jit_solution(14567402960945795000)
XLA Ops:
  0.7 3.0 %collective-permute-start.2 = (bf16[128,256]{1,0:T(8,128)(2,1)}, bf16[128,256]{1,0:T(8,128)(2,1)S(1)}, u32[]{:S(2)}, u32[]{:S(2)}) collective-permute-start(bf16[128,256]{1,0:T(8,128)(2,1)} %c0.1), channel_id=1, source_target_pairs={{0,2},{1,3},{2,0},{3,1},{4,6},{5,7},{6,4},{7,5},{8,10},{9,11},{10,... | collective-permute-start | bytes 196616 | tf_op jit(solution)/shard_map/ppermute | solution.py:31
  3.7 0.2 collective-permute-start.5
  3.9 0.3 %collective-permute-start = (bf16[64,256]{1,0:T(8,128)(2,1)}, bf16[64,256]{1,0:T(8,128)(2,1)S(1)}, u32[]{:S(2)}, u32[]{:S(2)}) collective-permute-start(bf16[64,256]{1,0:T(8,128)(2,1)} %b_in.1), channel_id=1, source_target_pairs={{0,1},{1,0},{2,3},{3,2},{4,5},{5,4},{6,7},{7,6},{8,9},{9,8},{10,11... | collective-permute-start | bytes 98312 | tf_op jit(solution)/shard_map/ppermute | solution.py:31
  4.2 0.2 shard_map.68
  4.4 1.3 %shard_map.69 = f32[256,256]{1,0:T(8,128)S(1)} custom-call(bf16[128,64,512]{2,1,0:T(8,128)(2,1)S(1)} %copy-done, bf16[128,256]{1,0:T(8,128)(2,1)S(1)} %get-tuple-element.28.a_ref, bf16[64,256]{1,0:T(8,128)(2,1)S(1)} %get-tuple-element.22.b_ref), custom_call_target="tpu_custom_call" | custom-call | flops 4294967296 | tf_op jit(solution)/shard_map/pallas_call | solution.py:35
  5.8 0.0 copy-start.1
  5.8 0.3 collective-permute-start.1
  6.0 0.0 collective-permute-done.b1_ref
  6.0 1.3 %shard_map.70.g_ref = f32[256,256]{1,0:T(8,128)S(1)} custom-call(bf16[128,64,512]{2,1,0:T(8,128)(2,1)S(1)} %copy-done, bf16[128,256]{1,0:T(8,128)(2,1)S(1)} %get-tuple-element.28.a_ref, bf16[64,256]{1,0:T(8,128)(2,1)S(1)} %get-tuple-element.22.b_ref), custom_call_target="tpu_custom_call" | custom-call | flops 8589934592 | tf_op jit(solution)/shard_map/pallas_call | solution.py:35
  7.3 0.0 collective-permute-done.2.c2_ref.c2
  7.4 0.6 %shard_map.71 = (f32[128,256]{1,0:T(8,128)S(1)}, f32[128,256]{1,0:T(8,128)S(1)}) custom-call(bf16[64,256]{1,0:T(8,128)(2,1)S(1)} %get-tuple-element.22.b_ref, bf16[64,256]{1,0:T(8,128)(2,1)S(1)} %collective-permute-done.b1_ref, f32[256,256]{1,0:T(8,128)S(1)} %get-tuple-element.23.ga_ref, bf16[128,256]{1,0:T(8,128)(2,1)S(1)} %copy-done.1, ...), custom_call_target="tpu_custom_call" | custom-call | flops 268435456 | tf_op jit(solution)/shard_map/pallas_call | solution.py:35
  7.9 0.0 collective-permute-done.1.in_ref
  7.9 0.1 shard_map.72
  8.0 2.5 %collective-permute-start.3 = (f16[136,256]{1,0:T(8,128)(2,1)S(1)}, f16[136,256]{1,0:T(8,128)(2,1)S(1)}, u32[]{:S(2)}, u32[]{:S(2)}) collective-permute-start(f16[136,256]{1,0:T(8,128)(2,1)S(1)} %convert_element_type.48), channel_id=1, source_target_pairs={{0,2},{1,3},{2,0},{3,1},{4,6},{5,7},{6,4},{7,5},{8,10},{9,11},{10,... | collective-permute-start | bytes 208904 | tf_op jit(solution)/shard_map/ppermute | solution.py:31
  10.5 0.0 collective-permute-done.4.c1
  10.5 0.0 collective-permute-done.5.c3
  10.5 2.6 %shard_map.73 = (f32[128,256]{1,0:T(8,128)S(1)}, f32[64,256]{1,0:T(8,128)S(1)}, f32[256,256]{1,0:T(8,128)S(1)}) custom-call(bf16[128,64,512]{2,1,0:T(8,128)(2,1)S(1)} %copy-done, bf16[128,256]{1,0:T(8,128)(2,1)S(1)} %get-tuple-element.28.a_ref, bf16[64,256]{1,0:T(8,128)(2,1)S(1)} %get-tuple-element.22.b_ref, f32[256,256]{1,0:T(8,128)S(1)} %get-tuple-element.23.ga_ref, ...), custom_call_target="tpu_custom_call" | custom-call | flops 2147483648 | tf_op jit(solution)/shard_map/pallas_call | solution.py:35
  13.2 0.2 collective-permute-done.3
  13.4 0.1 shard_map.74
  13.5 1.8 %collective-permute-start.6 = (f16[200,256]{1,0:T(8,128)(2,1)S(1)}, f16[200,256]{1,0:T(8,128)(2,1)S(1)}, u32[]{:S(2)}, u32[]{:S(2)}) collective-permute-start(f16[200,256]{1,0:T(8,128)(2,1)S(1)} %convert_element_type.50), channel_id=1, source_target_pairs={{0,4},{4,0},{8,12},{12,8},{16,20},{20,16},{24,28},{28,24},{1,5},{5... | collective-permute-start | bytes 307208 | tf_op jit(solution)/shard_map/ppermute | solution.py:31
  15.2 1.6 %collective-permute-start.7 = (f16[200,256]{1,0:T(8,128)(2,1)S(1)}, f16[200,256]{1,0:T(8,128)(2,1)S(1)}, u32[]{:S(2)}, u32[]{:S(2)}) collective-permute-start(f16[200,256]{1,0:T(8,128)(2,1)S(1)} %convert_element_type.50), channel_id=1, source_target_pairs={{0,8},{4,12},{8,0},{12,4},{16,24},{20,28},{24,16},{28,20},{1,9},{5... | collective-permute-start | bytes 307208 | tf_op jit(solution)/shard_map/ppermute | solution.py:31
  16.8 0.2 collective-permute-start.8
  17.0 0.4 %shard_map.75 = f32[128,256]{1,0:T(8,128)S(1)} custom-call(bf16[128,256]{1,0:T(8,128)(2,1)S(1)} %get-tuple-element.28.a_ref, bf16[64,256]{1,0:T(8,128)(2,1)S(1)} %get-tuple-element.22.b_ref, f32[256,256]{1,0:T(8,128)S(1)} %get-tuple-element.30.gc_ref, f32[128,256]{1,0:T(8,128)S(1)} %get-tuple-element.32.slab_ref), custom_call_target="tpu_custom_call" | custom-call | flops 67108864 | tf_op jit(solution)/shard_map/pallas_call | solution.py:35
  17.5 1.8 %collective-permute-start.10 = (f32[128,256]{1,0:T(8,128)S(1)}, f32[128,256]{1,0:T(8,128)S(1)}, u32[]{:S(2)}, u32[]{:S(2)}) collective-permute-start(f32[128,256]{1,0:T(8,128)S(1)} %shard_map.75), channel_id=1, source_target_pairs={{0,2},{1,3},{2,0},{3,1},{4,6},{5,7},{6,4},{7,5},{8,10},{9,11},{10,... | collective-permute-start | bytes 393224 | tf_op jit(solution)/shard_map/ppermute | solution.py:31
  19.3 0.0 collective-permute-done.6
  19.3 1.6 %collective-permute-done.7 = f16[200,256]{1,0:T(8,128)(2,1)S(1)} collective-permute-done((f16[200,256]{1,0:T(8,128)(2,1)S(1)}, f16[200,256]{1,0:T(8,128)(2,1)S(1)}, u32[]{:S(2)}, u32[]{:S(2)}) %collective-permute-start.7) | collective-permute-done | bytes 102432 | tf_op jit(solution)/shard_map/ppermute | solution.py:31
  20.8 1.6 %collective-permute-done.8 = f16[200,256]{1,0:T(8,128)(2,1)S(1)} collective-permute-done((f16[200,256]{1,0:T(8,128)(2,1)S(1)}, f16[200,256]{1,0:T(8,128)(2,1)S(1)}, u32[]{:S(2)}, u32[]{:S(2)}) %collective-permute-start.8) | collective-permute-done | bytes 102432 | tf_op jit(solution)/shard_map/ppermute | solution.py:31
  22.4 0.1 select_convert_fusion
  22.5 2.7 %collective-permute-start.9 = (f16[200,256]{1,0:T(8,128)(2,1)S(1)}, f16[200,256]{1,0:T(8,128)(2,1)S(1)}, u32[]{:S(2)}, u32[]{:S(2)}) collective-permute-start(f16[200,256]{1,0:T(8,128)(2,1)S(1)} %select_convert_fusion), channel_id=1, source_target_pairs={{0,16},{4,20},{8,24},{12,28},{16,0},{20,4},{24,8},{28,12},{1,17},{... | collective-permute-start | bytes 307208 | tf_op jit(solution)/shard_map/ppermute | solution.py:31
  25.2 0.1 collective-permute-start.11
  25.3 3.9 %collective-permute-done.9 = f16[200,256]{1,0:T(8,128)(2,1)S(1)} collective-permute-done((f16[200,256]{1,0:T(8,128)(2,1)S(1)}, f16[200,256]{1,0:T(8,128)(2,1)S(1)}, u32[]{:S(2)}, u32[]{:S(2)}) %collective-permute-start.9) | collective-permute-done | bytes 102432 | tf_op jit(solution)/shard_map/ppermute | solution.py:31
  29.3 0.7 %shard_map.76 = (f32[128,256]{1,0:T(8,128)}, f32[128,256]{1,0:T(8,128)}, f32[64,256]{1,0:T(8,128)}) custom-call(f32[200,256]{1,0:T(8,128)S(1)} %multiply_add_fusion.v_ref, f32[128,256]{1,0:T(8,128)S(1)} %add.33.pa_ref, f32[128,256]{1,0:T(8,128)S(1)} %collective-permute-done.11.in_ref), custom_call_target="tpu_custom_call" | custom-call | tf_op jit(solution)/shard_map/pallas_call | solution.py:359
  (20 shorter events, 0.2 us)
Async XLA Ops:
  0.6 3.6 %copy-start.3 = (bf16[64,256]{1,0:T(8,128)(2,1)S(1)}, bf16[64,256]{1,0:T(8,128)(2,1)}, u32[]{:S(2)}) copy-start(bf16[64,256]{1,0:T(8,128)(2,1)} %b_in.1) | copy-start | bytes 98308
  0.6 3.6 %copy-start.2 = (bf16[128,256]{1,0:T(8,128)(2,1)S(1)}, bf16[128,256]{1,0:T(8,128)(2,1)}, u32[]{:S(2)}) copy-start(bf16[128,256]{1,0:T(8,128)(2,1)} %a_in.1) | copy-start | bytes 196612
  0.7 3.8 %copy-start = (bf16[128,64,512]{2,1,0:T(8,128)(2,1)S(1)}, bf16[128,64,512]{2,1,0:T(8,128)(2,1)}, u32[]{:S(2)}) copy-start(bf16[128,64,512]{2,1,0:T(8,128)(2,1)} %x_ref.5) | copy-start | bytes 25165828
  0.7 6.7 %collective-permute-start.2 = (bf16[128,256]{1,0:T(8,128)(2,1)}, bf16[128,256]{1,0:T(8,128)(2,1)S(1)}, u32[]{:S(2)}, u32[]{:S(2)}) collective-permute-start(bf16[128,256]{1,0:T(8,128)(2,1)} %c0.1), channel_id=1, source_target_pairs={{0,2},{1,3},{2,0},{3,1},{4,6},{5,7},{6,4},{7,5},{8,10},{9,11},{10,... | collective-permute-start | bytes 196616 | tf_op jit(solution)/shard_map/ppermute | solution.py:31
  3.7 6.8 %collective-permute-start.4 = (bf16[128,256]{1,0:T(8,128)(2,1)}, bf16[128,256]{1,0:T(8,128)(2,1)S(1)}, u32[]{:S(2)}, u32[]{:S(2)}) collective-permute-start(bf16[128,256]{1,0:T(8,128)(2,1)} %c0.1), channel_id=1, source_target_pairs={{0,1},{1,0},{2,3},{3,2},{4,5},{5,4},{6,7},{7,6},{8,9},{9,8},{10,11... | collective-permute-start | bytes 196616 | tf_op jit(solution)/shard_map/ppermute | solution.py:31
  3.7 6.8 %collective-permute-start.5 = (bf16[128,256]{1,0:T(8,128)(2,1)}, bf16[128,256]{1,0:T(8,128)(2,1)S(1)}, u32[]{:S(2)}, u32[]{:S(2)}) collective-permute-start(bf16[128,256]{1,0:T(8,128)(2,1)} %c0.1), channel_id=1, source_target_pairs={{0,3},{1,2},{2,1},{3,0},{4,7},{5,6},{6,5},{7,4},{8,11},{9,10},{10,... | collective-permute-start | bytes 196616 | tf_op jit(solution)/shard_map/ppermute | solution.py:31
  3.9 2.1 %collective-permute-start = (bf16[64,256]{1,0:T(8,128)(2,1)}, bf16[64,256]{1,0:T(8,128)(2,1)S(1)}, u32[]{:S(2)}, u32[]{:S(2)}) collective-permute-start(bf16[64,256]{1,0:T(8,128)(2,1)} %b_in.1), channel_id=1, source_target_pairs={{0,1},{1,0},{2,3},{3,2},{4,5},{5,4},{6,7},{7,6},{8,9},{9,8},{10,11... | collective-permute-start | bytes 98312 | tf_op jit(solution)/shard_map/ppermute | solution.py:31
  5.8 1.6 %copy-start.1 = (bf16[128,256]{1,0:T(8,128)(2,1)S(1)}, bf16[128,256]{1,0:T(8,128)(2,1)}, u32[]{:S(2)}) copy-start(bf16[128,256]{1,0:T(8,128)(2,1)} %c0.1) | copy-start | bytes 196612
  5.8 2.2 %collective-permute-start.1 = (f32[256,256]{1,0:T(8,128)S(1)}, f32[256,256]{1,0:T(8,128)S(1)}, u32[]{:S(2)}, u32[]{:S(2)}) collective-permute-start(f32[256,256]{1,0:T(8,128)S(1)} %shard_map.69), channel_id=1, source_target_pairs={{0,1},{1,0},{2,3},{3,2},{4,5},{5,4},{6,7},{7,6},{8,9},{9,8},{10,11... | collective-permute-start | bytes 786440 | tf_op jit(solution)/shard_map/ppermute | solution.py:31
  8.0 5.3 %collective-permute-start.3 = (f16[136,256]{1,0:T(8,128)(2,1)S(1)}, f16[136,256]{1,0:T(8,128)(2,1)S(1)}, u32[]{:S(2)}, u32[]{:S(2)}) collective-permute-start(f16[136,256]{1,0:T(8,128)(2,1)S(1)} %convert_element_type.48), channel_id=1, source_target_pairs={{0,2},{1,3},{2,0},{3,1},{4,6},{5,7},{6,4},{7,5},{8,10},{9,11},{10,... | collective-permute-start | bytes 208904 | tf_op jit(solution)/shard_map/ppermute | solution.py:31
  13.5 5.8 %collective-permute-start.6 = (f16[200,256]{1,0:T(8,128)(2,1)S(1)}, f16[200,256]{1,0:T(8,128)(2,1)S(1)}, u32[]{:S(2)}, u32[]{:S(2)}) collective-permute-start(f16[200,256]{1,0:T(8,128)(2,1)S(1)} %convert_element_type.50), channel_id=1, source_target_pairs={{0,4},{4,0},{8,12},{12,8},{16,20},{20,16},{24,28},{28,24},{1,5},{5... | collective-permute-start | bytes 307208 | tf_op jit(solution)/shard_map/ppermute | solution.py:31
  15.2 5.6 %collective-permute-start.7 = (f16[200,256]{1,0:T(8,128)(2,1)S(1)}, f16[200,256]{1,0:T(8,128)(2,1)S(1)}, u32[]{:S(2)}, u32[]{:S(2)}) collective-permute-start(f16[200,256]{1,0:T(8,128)(2,1)S(1)} %convert_element_type.50), channel_id=1, source_target_pairs={{0,8},{4,12},{8,0},{12,4},{16,24},{20,28},{24,16},{28,20},{1,9},{5... | collective-permute-start | bytes 307208 | tf_op jit(solution)/shard_map/ppermute | solution.py:31
  16.8 5.6 %collective-permute-start.8 = (f16[200,256]{1,0:T(8,128)(2,1)S(1)}, f16[200,256]{1,0:T(8,128)(2,1)S(1)}, u32[]{:S(2)}, u32[]{:S(2)}) collective-permute-start(f16[200,256]{1,0:T(8,128)(2,1)S(1)} %convert_element_type.50), channel_id=1, source_target_pairs={{0,12},{4,8},{8,4},{12,0},{16,28},{20,24},{24,20},{28,16},{1,13},{... | collective-permute-start | bytes 307208 | tf_op jit(solution)/shard_map/ppermute | solution.py:31
  17.5 7.7 %collective-permute-start.10 = (f32[128,256]{1,0:T(8,128)S(1)}, f32[128,256]{1,0:T(8,128)S(1)}, u32[]{:S(2)}, u32[]{:S(2)}) collective-permute-start(f32[128,256]{1,0:T(8,128)S(1)} %shard_map.75), channel_id=1, source_target_pairs={{0,2},{1,3},{2,0},{3,1},{4,6},{5,7},{6,4},{7,5},{8,10},{9,11},{10,... | collective-permute-start | bytes 393224 | tf_op jit(solution)/shard_map/ppermute | solution.py:31
  22.5 6.7 %collective-permute-start.9 = (f16[200,256]{1,0:T(8,128)(2,1)S(1)}, f16[200,256]{1,0:T(8,128)(2,1)S(1)}, u32[]{:S(2)}, u32[]{:S(2)}) collective-permute-start(f16[200,256]{1,0:T(8,128)(2,1)S(1)} %select_convert_fusion), channel_id=1, source_target_pairs={{0,16},{4,20},{8,24},{12,28},{16,0},{20,4},{24,8},{28,12},{1,17},{... | collective-permute-start | bytes 307208 | tf_op jit(solution)/shard_map/ppermute | solution.py:31
  25.2 4.1 %collective-permute-start.11 = (f32[128,256]{1,0:T(8,128)S(1)}, f32[128,256]{1,0:T(8,128)S(1)}, u32[]{:S(2)}, u32[]{:S(2)}) collective-permute-start(f32[128,256]{1,0:T(8,128)S(1)} %add.33.pa_ref), channel_id=1, source_target_pairs={{0,1},{1,0},{2,3},{3,2},{4,5},{5,4},{6,7},{7,6},{8,9},{9,8},{10,11... | collective-permute-start | bytes 393224 | tf_op jit(solution)/shard_map/ppermute | solution.py:31

commit v5 on v4

--- a/solution.py
+++ b/solution.py
@@ -342,7 +342,7 @@
     bits = src_bits[::-1]
     stages = [rad_bits[i : i + 2] for i in range(0, len(rad_bits), 2)]
     for i, stage in enumerate(stages):
-        others = stage if len(stage) == 1 else [*stage, sum(stage)]
+        others = stage if len(stage) == 1 else [sum(stage), stage[1], stage[0]]
         terms = [unpack(m)] + [unpack(swap(m, "rad", o)) for o in others]
         if len(bits) > 1:
             pa = after(pa, m)

time: 30.2 us -> 29.8 us (0.987)
  waiting for transfers between devices: 7.3 us -> 6.85 us
    ppermute x12, waiting for transfers between devices: 7.3 us -> 6.85 us  [swap(): lax.ppermute(x, axis, [(i, i ^ bit) for i in range(lax.axis_size(axis))])]
where the time goes in v5:
time: 29.8 us; the launch traced here: 29.7 us
  starting transfers between devices  14.4 us (48%)
  Pallas kernels  7.28 us (24%)
  waiting for transfers between devices  6.85 us (23%)
  between operations  0.82 us (3%)
    ppermute x12, starting transfers between devices, swap(): lax.ppermute(x, axis, [(i, i ^ bit) for i in range(lax.axis_size(axis))])  14.4 us
    ppermute x12, waiting for transfers between devices, swap(): lax.ppermute(x, axis, [(i, i ^ bit) for i in range(lax.axis_size(axis))])  6.85 us
    pallas_call x9, Pallas kernels, call(): pl.pallas_call(body, in_specs=[WHOLE] * len(args), out_specs=[WHOLE] * le...  6.54 us
    pallas_call x1, Pallas kernels, per_device(): pl.pallas_call(finish, in_specs=[WHOLE] * 3, out_specs=[WHOLE] * 3, out_s...  0.74 us
  transfers between devices with their start and end apart: 12, of which 4 were waited for; matrix products, arithmetic and copies ran while one was open for 1% of the time, Pallas kernels for 22%

profile of v5, /device:TPU:0, one launch (start us, length us, event | category | flops | bytes accessed | tf_op | source)
XLA Modules:
  0.0 29.7 jit_solution(14122387933167428181)
XLA Ops:
  0.7 3.0 %collective-permute-start.2 = (bf16[128,256]{1,0:T(8,128)(2,1)}, bf16[128,256]{1,0:T(8,128)(2,1)S(1)}, u32[]{:S(2)}, u32[]{:S(2)}) collective-permute-start(bf16[128,256]{1,0:T(8,128)(2,1)} %c0.1), channel_id=1, source_target_pairs={{0,2},{1,3},{2,0},{3,1},{4,6},{5,7},{6,4},{7,5},{8,10},{9,11},{10,... | collective-permute-start | bytes 196616 | tf_op jit(solution)/shard_map/ppermute | solution.py:31
  3.7 0.0 collective-permute-start.4
  3.7 0.2 collective-permute-start.5
  3.9 0.3 %collective-permute-start = (bf16[64,256]{1,0:T(8,128)(2,1)}, bf16[64,256]{1,0:T(8,128)(2,1)S(1)}, u32[]{:S(2)}, u32[]{:S(2)}) collective-permute-start(bf16[64,256]{1,0:T(8,128)(2,1)} %b_in.1), channel_id=1, source_target_pairs={{0,1},{1,0},{2,3},{3,2},{4,5},{5,4},{6,7},{7,6},{8,9},{9,8},{10,11... | collective-permute-start | bytes 98312 | tf_op jit(solution)/shard_map/ppermute | solution.py:31
  4.2 0.2 shard_map.68
  4.4 1.3 %shard_map.69 = f32[256,256]{1,0:T(8,128)S(1)} custom-call(bf16[128,64,512]{2,1,0:T(8,128)(2,1)S(1)} %copy-done, bf16[128,256]{1,0:T(8,128)(2,1)S(1)} %get-tuple-element.28.a_ref, bf16[64,256]{1,0:T(8,128)(2,1)S(1)} %get-tuple-element.22.b_ref), custom_call_target="tpu_custom_call" | custom-call | flops 4294967296 | tf_op jit(solution)/shard_map/pallas_call | solution.py:35
  5.8 0.0 copy-start.1
  5.8 0.3 collective-permute-start.1
  6.0 0.0 collective-permute-done.b1_ref
  6.0 1.3 %shard_map.70.g_ref = f32[256,256]{1,0:T(8,128)S(1)} custom-call(bf16[128,64,512]{2,1,0:T(8,128)(2,1)S(1)} %copy-done, bf16[128,256]{1,0:T(8,128)(2,1)S(1)} %get-tuple-element.28.a_ref, bf16[64,256]{1,0:T(8,128)(2,1)S(1)} %get-tuple-element.22.b_ref), custom_call_target="tpu_custom_call" | custom-call | flops 8589934592 | tf_op jit(solution)/shard_map/pallas_call | solution.py:35
  7.4 0.6 %shard_map.71 = (f32[128,256]{1,0:T(8,128)S(1)}, f32[128,256]{1,0:T(8,128)S(1)}) custom-call(bf16[64,256]{1,0:T(8,128)(2,1)S(1)} %get-tuple-element.22.b_ref, bf16[64,256]{1,0:T(8,128)(2,1)S(1)} %collective-permute-done.b1_ref, f32[256,256]{1,0:T(8,128)S(1)} %get-tuple-element.23.ga_ref, bf16[128,256]{1,0:T(8,128)(2,1)S(1)} %copy-done.1, ...), custom_call_target="tpu_custom_call" | custom-call | flops 268435456 | tf_op jit(solution)/shard_map/pallas_call | solution.py:35
  7.9 0.1 shard_map.72
  8.0 2.5 %collective-permute-start.3 = (f16[136,256]{1,0:T(8,128)(2,1)S(1)}, f16[136,256]{1,0:T(8,128)(2,1)S(1)}, u32[]{:S(2)}, u32[]{:S(2)}) collective-permute-start(f16[136,256]{1,0:T(8,128)(2,1)S(1)} %convert_element_type.48), channel_id=1, source_target_pairs={{0,2},{1,3},{2,0},{3,1},{4,6},{5,7},{6,4},{7,5},{8,10},{9,11},{10,... | collective-permute-start | bytes 208904 | tf_op jit(solution)/shard_map/ppermute | solution.py:31
  10.5 0.0 collective-permute-done.5.c3
  10.5 2.6 %shard_map.73 = (f32[128,256]{1,0:T(8,128)S(1)}, f32[64,256]{1,0:T(8,128)S(1)}, f32[256,256]{1,0:T(8,128)S(1)}) custom-call(bf16[128,64,512]{2,1,0:T(8,128)(2,1)S(1)} %copy-done, bf16[128,256]{1,0:T(8,128)(2,1)S(1)} %get-tuple-element.28.a_ref, bf16[64,256]{1,0:T(8,128)(2,1)S(1)} %get-tuple-element.22.b_ref, f32[256,256]{1,0:T(8,128)S(1)} %get-tuple-element.23.ga_ref, ...), custom_call_target="tpu_custom_call" | custom-call | flops 2147483648 | tf_op jit(solution)/shard_map/pallas_call | solution.py:35
  13.2 0.2 collective-permute-done.3
  13.4 0.1 shard_map.74
  13.5 2.8 %collective-permute-start.6 = (f16[200,256]{1,0:T(8,128)(2,1)S(1)}, f16[200,256]{1,0:T(8,128)(2,1)S(1)}, u32[]{:S(2)}, u32[]{:S(2)}) collective-permute-start(f16[200,256]{1,0:T(8,128)(2,1)S(1)} %convert_element_type.50), channel_id=1, source_target_pairs={{0,12},{4,8},{8,4},{12,0},{16,28},{20,24},{24,20},{28,16},{1,13},{... | collective-permute-start | bytes 307208 | tf_op jit(solution)/shard_map/ppermute | solution.py:31
  16.3 0.4 %collective-permute-start.7 = (f16[200,256]{1,0:T(8,128)(2,1)S(1)}, f16[200,256]{1,0:T(8,128)(2,1)S(1)}, u32[]{:S(2)}, u32[]{:S(2)}) collective-permute-start(f16[200,256]{1,0:T(8,128)(2,1)S(1)} %convert_element_type.50), channel_id=1, source_target_pairs={{0,8},{4,12},{8,0},{12,4},{16,24},{20,28},{24,16},{28,20},{1,9},{5... | collective-permute-start | bytes 307208 | tf_op jit(solution)/shard_map/ppermute | solution.py:31
  16.7 0.3 %collective-permute-start.8 = (f16[200,256]{1,0:T(8,128)(2,1)S(1)}, f16[200,256]{1,0:T(8,128)(2,1)S(1)}, u32[]{:S(2)}, u32[]{:S(2)}) collective-permute-start(f16[200,256]{1,0:T(8,128)(2,1)S(1)} %convert_element_type.50), channel_id=1, source_target_pairs={{0,4},{4,0},{8,12},{12,8},{16,20},{20,16},{24,28},{28,24},{1,5},{5... | collective-permute-start | bytes 307208 | tf_op jit(solution)/shard_map/ppermute | solution.py:31
  17.0 0.4 %shard_map.75 = f32[128,256]{1,0:T(8,128)S(1)} custom-call(bf16[128,256]{1,0:T(8,128)(2,1)S(1)} %get-tuple-element.28.a_ref, bf16[64,256]{1,0:T(8,128)(2,1)S(1)} %get-tuple-element.22.b_ref, f32[256,256]{1,0:T(8,128)S(1)} %get-tuple-element.30.gc_ref, f32[128,256]{1,0:T(8,128)S(1)} %get-tuple-element.32.slab_ref), custom_call_target="tpu_custom_call" | custom-call | flops 67108864 | tf_op jit(solution)/shard_map/pallas_call | solution.py:35
  17.5 1.8 %collective-permute-start.10 = (f32[128,256]{1,0:T(8,128)S(1)}, f32[128,256]{1,0:T(8,128)S(1)}, u32[]{:S(2)}, u32[]{:S(2)}) collective-permute-start(f32[128,256]{1,0:T(8,128)S(1)} %shard_map.75), channel_id=1, source_target_pairs={{0,2},{1,3},{2,0},{3,1},{4,6},{5,7},{6,4},{7,5},{8,10},{9,11},{10,... | collective-permute-start | bytes 393224 | tf_op jit(solution)/shard_map/ppermute | solution.py:31
  19.3 0.9 %collective-permute-done.6 = f16[200,256]{1,0:T(8,128)(2,1)S(1)} collective-permute-done((f16[200,256]{1,0:T(8,128)(2,1)S(1)}, f16[200,256]{1,0:T(8,128)(2,1)S(1)}, u32[]{:S(2)}, u32[]{:S(2)}) %collective-permute-start.6) | collective-permute-done | bytes 102432 | tf_op jit(solution)/shard_map/ppermute | solution.py:31
  20.1 1.4 %collective-permute-done.7 = f16[200,256]{1,0:T(8,128)(2,1)S(1)} collective-permute-done((f16[200,256]{1,0:T(8,128)(2,1)S(1)}, f16[200,256]{1,0:T(8,128)(2,1)S(1)}, u32[]{:S(2)}, u32[]{:S(2)}) %collective-permute-start.7) | collective-permute-done | bytes 102432 | tf_op jit(solution)/shard_map/ppermute | solution.py:31
  21.5 0.0 collective-permute-done.8
  21.6 0.1 select_convert_fusion
  21.7 2.7 %collective-permute-start.9 = (f16[200,256]{1,0:T(8,128)(2,1)S(1)}, f16[200,256]{1,0:T(8,128)(2,1)S(1)}, u32[]{:S(2)}, u32[]{:S(2)}) collective-permute-start(f16[200,256]{1,0:T(8,128)(2,1)S(1)} %select_convert_fusion), channel_id=1, source_target_pairs={{0,16},{4,20},{8,24},{12,28},{16,0},{20,4},{24,8},{28,12},{1,17},{... | collective-permute-start | bytes 307208 | tf_op jit(solution)/shard_map/ppermute | solution.py:31
  24.4 0.0 collective-permute-done.10
  24.4 0.1 collective-permute-start.11
  24.5 4.3 %collective-permute-done.9 = f16[200,256]{1,0:T(8,128)(2,1)S(1)} collective-permute-done((f16[200,256]{1,0:T(8,128)(2,1)S(1)}, f16[200,256]{1,0:T(8,128)(2,1)S(1)}, u32[]{:S(2)}, u32[]{:S(2)}) %collective-permute-start.9) | collective-permute-done | bytes 102432 | tf_op jit(solution)/shard_map/ppermute | solution.py:31
  28.9 0.0 collective-permute-done.11.in_ref
  28.9 0.7 %shard_map.76 = (f32[128,256]{1,0:T(8,128)}, f32[128,256]{1,0:T(8,128)}, f32[64,256]{1,0:T(8,128)}) custom-call(f32[200,256]{1,0:T(8,128)S(1)} %multiply_add_fusion.v_ref, f32[128,256]{1,0:T(8,128)S(1)} %add.33.pa_ref, f32[128,256]{1,0:T(8,128)S(1)} %collective-permute-done.11.in_ref), custom_call_target="tpu_custom_call" | custom-call | tf_op jit(solution)/shard_map/pallas_call | solution.py:359
  (20 shorter events, 0.2 us)
Async XLA Ops:
  0.6 3.6 %copy-start.3 = (bf16[64,256]{1,0:T(8,128)(2,1)S(1)}, bf16[64,256]{1,0:T(8,128)(2,1)}, u32[]{:S(2)}) copy-start(bf16[64,256]{1,0:T(8,128)(2,1)} %b_in.1) | copy-start | bytes 98308
  0.6 3.6 %copy-start.2 = (bf16[128,256]{1,0:T(8,128)(2,1)S(1)}, bf16[128,256]{1,0:T(8,128)(2,1)}, u32[]{:S(2)}) copy-start(bf16[128,256]{1,0:T(8,128)(2,1)} %a_in.1) | copy-start | bytes 196612
  0.7 3.8 %copy-start = (bf16[128,64,512]{2,1,0:T(8,128)(2,1)S(1)}, bf16[128,64,512]{2,1,0:T(8,128)(2,1)}, u32[]{:S(2)}) copy-start(bf16[128,64,512]{2,1,0:T(8,128)(2,1)} %x_ref.5) | copy-start | bytes 25165828
  0.7 6.7 %collective-permute-start.2 = (bf16[128,256]{1,0:T(8,128)(2,1)}, bf16[128,256]{1,0:T(8,128)(2,1)S(1)}, u32[]{:S(2)}, u32[]{:S(2)}) collective-permute-start(bf16[128,256]{1,0:T(8,128)(2,1)} %c0.1), channel_id=1, source_target_pairs={{0,2},{1,3},{2,0},{3,1},{4,6},{5,7},{6,4},{7,5},{8,10},{9,11},{10,... | collective-permute-start | bytes 196616 | tf_op jit(solution)/shard_map/ppermute | solution.py:31
  3.7 6.8 %collective-permute-start.4 = (bf16[128,256]{1,0:T(8,128)(2,1)}, bf16[128,256]{1,0:T(8,128)(2,1)S(1)}, u32[]{:S(2)}, u32[]{:S(2)}) collective-permute-start(bf16[128,256]{1,0:T(8,128)(2,1)} %c0.1), channel_id=1, source_target_pairs={{0,1},{1,0},{2,3},{3,2},{4,5},{5,4},{6,7},{7,6},{8,9},{9,8},{10,11... | collective-permute-start | bytes 196616 | tf_op jit(solution)/shard_map/ppermute | solution.py:31
  3.7 6.8 %collective-permute-start.5 = (bf16[128,256]{1,0:T(8,128)(2,1)}, bf16[128,256]{1,0:T(8,128)(2,1)S(1)}, u32[]{:S(2)}, u32[]{:S(2)}) collective-permute-start(bf16[128,256]{1,0:T(8,128)(2,1)} %c0.1), channel_id=1, source_target_pairs={{0,3},{1,2},{2,1},{3,0},{4,7},{5,6},{6,5},{7,4},{8,11},{9,10},{10,... | collective-permute-start | bytes 196616 | tf_op jit(solution)/shard_map/ppermute | solution.py:31
  3.9 2.1 %collective-permute-start = (bf16[64,256]{1,0:T(8,128)(2,1)}, bf16[64,256]{1,0:T(8,128)(2,1)S(1)}, u32[]{:S(2)}, u32[]{:S(2)}) collective-permute-start(bf16[64,256]{1,0:T(8,128)(2,1)} %b_in.1), channel_id=1, source_target_pairs={{0,1},{1,0},{2,3},{3,2},{4,5},{5,4},{6,7},{7,6},{8,9},{9,8},{10,11... | collective-permute-start | bytes 98312 | tf_op jit(solution)/shard_map/ppermute | solution.py:31
  5.8 1.6 %copy-start.1 = (bf16[128,256]{1,0:T(8,128)(2,1)S(1)}, bf16[128,256]{1,0:T(8,128)(2,1)}, u32[]{:S(2)}) copy-start(bf16[128,256]{1,0:T(8,128)(2,1)} %c0.1) | copy-start | bytes 196612
  5.8 2.2 %collective-permute-start.1 = (f32[256,256]{1,0:T(8,128)S(1)}, f32[256,256]{1,0:T(8,128)S(1)}, u32[]{:S(2)}, u32[]{:S(2)}) collective-permute-start(f32[256,256]{1,0:T(8,128)S(1)} %shard_map.69), channel_id=1, source_target_pairs={{0,1},{1,0},{2,3},{3,2},{4,5},{5,4},{6,7},{7,6},{8,9},{9,8},{10,11... | collective-permute-start | bytes 786440 | tf_op jit(solution)/shard_map/ppermute | solution.py:31
  8.0 5.3 %collective-permute-start.3 = (f16[136,256]{1,0:T(8,128)(2,1)S(1)}, f16[136,256]{1,0:T(8,128)(2,1)S(1)}, u32[]{:S(2)}, u32[]{:S(2)}) collective-permute-start(f16[136,256]{1,0:T(8,128)(2,1)S(1)} %convert_element_type.48), channel_id=1, source_target_pairs={{0,2},{1,3},{2,0},{3,1},{4,6},{5,7},{6,4},{7,5},{8,10},{9,11},{10,... | collective-permute-start | bytes 208904 | tf_op jit(solution)/shard_map/ppermute | solution.py:31
  13.5 6.7 %collective-permute-start.6 = (f16[200,256]{1,0:T(8,128)(2,1)S(1)}, f16[200,256]{1,0:T(8,128)(2,1)S(1)}, u32[]{:S(2)}, u32[]{:S(2)}) collective-permute-start(f16[200,256]{1,0:T(8,128)(2,1)S(1)} %convert_element_type.50), channel_id=1, source_target_pairs={{0,12},{4,8},{8,4},{12,0},{16,28},{20,24},{24,20},{28,16},{1,13},{... | collective-permute-start | bytes 307208 | tf_op jit(solution)/shard_map/ppermute | solution.py:31
  16.3 5.3 %collective-permute-start.7 = (f16[200,256]{1,0:T(8,128)(2,1)S(1)}, f16[200,256]{1,0:T(8,128)(2,1)S(1)}, u32[]{:S(2)}, u32[]{:S(2)}) collective-permute-start(f16[200,256]{1,0:T(8,128)(2,1)S(1)} %convert_element_type.50), channel_id=1, source_target_pairs={{0,8},{4,12},{8,0},{12,4},{16,24},{20,28},{24,16},{28,20},{1,9},{5... | collective-permute-start | bytes 307208 | tf_op jit(solution)/shard_map/ppermute | solution.py:31
  16.7 4.8 %collective-permute-start.8 = (f16[200,256]{1,0:T(8,128)(2,1)S(1)}, f16[200,256]{1,0:T(8,128)(2,1)S(1)}, u32[]{:S(2)}, u32[]{:S(2)}) collective-permute-start(f16[200,256]{1,0:T(8,128)(2,1)S(1)} %convert_element_type.50), channel_id=1, source_target_pairs={{0,4},{4,0},{8,12},{12,8},{16,20},{20,16},{24,28},{28,24},{1,5},{5... | collective-permute-start | bytes 307208 | tf_op jit(solution)/shard_map/ppermute | solution.py:31
  17.5 7.0 %collective-permute-start.10 = (f32[128,256]{1,0:T(8,128)S(1)}, f32[128,256]{1,0:T(8,128)S(1)}, u32[]{:S(2)}, u32[]{:S(2)}) collective-permute-start(f32[128,256]{1,0:T(8,128)S(1)} %shard_map.75), channel_id=1, source_target_pairs={{0,2},{1,3},{2,0},{3,1},{4,6},{5,7},{6,4},{7,5},{8,10},{9,11},{10,... | collective-permute-start | bytes 393224 | tf_op jit(solution)/shard_map/ppermute | solution.py:31
  21.7 7.2 %collective-permute-start.9 = (f16[200,256]{1,0:T(8,128)(2,1)S(1)}, f16[200,256]{1,0:T(8,128)(2,1)S(1)}, u32[]{:S(2)}, u32[]{:S(2)}) collective-permute-start(f16[200,256]{1,0:T(8,128)(2,1)S(1)} %select_convert_fusion), channel_id=1, source_target_pairs={{0,16},{4,20},{8,24},{12,28},{16,0},{20,4},{24,8},{28,12},{1,17},{... | collective-permute-start | bytes 307208 | tf_op jit(solution)/shard_map/ppermute | solution.py:31
  24.4 4.5 %collective-permute-start.11 = (f32[128,256]{1,0:T(8,128)S(1)}, f32[128,256]{1,0:T(8,128)S(1)}, u32[]{:S(2)}, u32[]{:S(2)}) collective-permute-start(f32[128,256]{1,0:T(8,128)S(1)} %add.33.pa_ref), channel_id=1, source_target_pairs={{0,1},{1,0},{2,3},{3,2},{4,5},{5,4},{6,7},{7,6},{8,9},{9,8},{10,11... | collective-permute-start | bytes 393224 | tf_op jit(solution)/shard_map/ppermute | solution.py:31

commit v6 on v5

--- a/solution.py
+++ b/solution.py
@@ -342,7 +342,10 @@
     bits = src_bits[::-1]
     stages = [rad_bits[i : i + 2] for i in range(0, len(rad_bits), 2)]
     for i, stage in enumerate(stages):
-        others = stage if len(stage) == 1 else [sum(stage), stage[1], stage[0]]
+        if len(stage) == 2:
+            others = [sum(stage), stage[1], stage[0]]
+        else:
+            others = [stage[0] + (stage[0] // 2 if i else 0)]
         terms = [unpack(m)] + [unpack(swap(m, "rad", o)) for o in others]
         if len(bits) > 1:
             pa = after(pa, m)

time: 29.8 us -> 29.2 us (0.980)
  waiting for transfers between devices: 6.85 us -> 5.16 us
  starting transfers between devices: 14.4 us -> 15.5 us
    ppermute x12, waiting for transfers between devices: 6.85 us -> 5.16 us  [swap(): lax.ppermute(x, axis, [(i, i ^ bit) for i in range(lax.axis_size(axis))])]
    ppermute x12, starting transfers between devices: 14.4 us -> 15.5 us  [swap(): lax.ppermute(x, axis, [(i, i ^ bit) for i in range(lax.axis_size(axis))])]
where the time goes in v6:
time: 29.2 us; the launch traced here: 29.1 us
  starting transfers between devices  15.5 us (53%)
  Pallas kernels  7.28 us (25%)
  waiting for transfers between devices  5.16 us (18%)
  between operations  0.82 us (3%)
    ppermute x12, starting transfers between devices, swap(): lax.ppermute(x, axis, [(i, i ^ bit) for i in range(lax.axis_size(axis))])  15.5 us
    pallas_call x9, Pallas kernels, call(): pl.pallas_call(body, in_specs=[WHOLE] * len(args), out_specs=[WHOLE] * le...  6.54 us
    ppermute x12, waiting for transfers between devices, swap(): lax.ppermute(x, axis, [(i, i ^ bit) for i in range(lax.axis_size(axis))])  5.16 us
    pallas_call x1, Pallas kernels, per_device(): pl.pallas_call(finish, in_specs=[WHOLE] * 3, out_specs=[WHOLE] * 3, out_s...  0.74 us
  transfers between devices with their start and end apart: 12, of which 4 were waited for; matrix products, arithmetic and copies ran while one was open for 1% of the time, Pallas kernels for 22%

profile of v6, /device:TPU:0, one launch (start us, length us, event | category | flops | bytes accessed | tf_op | source)
XLA Modules:
  0.0 29.1 jit_solution(14055845563490357141)
XLA Ops:
  0.7 3.0 %collective-permute-start.2 = (bf16[128,256]{1,0:T(8,128)(2,1)}, bf16[128,256]{1,0:T(8,128)(2,1)S(1)}, u32[]{:S(2)}, u32[]{:S(2)}) collective-permute-start(bf16[128,256]{1,0:T(8,128)(2,1)} %c0.1), channel_id=1, source_target_pairs={{0,2},{1,3},{2,0},{3,1},{4,6},{5,7},{6,4},{7,5},{8,10},{9,11},{10,... | collective-permute-start | bytes 196616 | tf_op jit(solution)/shard_map/ppermute | solution.py:31
  3.7 0.0 collective-permute-start.4
  3.7 0.2 collective-permute-start.5
  3.9 0.3 %collective-permute-start = (bf16[64,256]{1,0:T(8,128)(2,1)}, bf16[64,256]{1,0:T(8,128)(2,1)S(1)}, u32[]{:S(2)}, u32[]{:S(2)}) collective-permute-start(bf16[64,256]{1,0:T(8,128)(2,1)} %b_in.1), channel_id=1, source_target_pairs={{0,1},{1,0},{2,3},{3,2},{4,5},{5,4},{6,7},{7,6},{8,9},{9,8},{10,11... | collective-permute-start | bytes 98312 | tf_op jit(solution)/shard_map/ppermute | solution.py:31
  4.2 0.2 shard_map.68
  4.4 1.3 %shard_map.69 = f32[256,256]{1,0:T(8,128)S(1)} custom-call(bf16[128,64,512]{2,1,0:T(8,128)(2,1)S(1)} %copy-done, bf16[128,256]{1,0:T(8,128)(2,1)S(1)} %get-tuple-element.28.a_ref, bf16[64,256]{1,0:T(8,128)(2,1)S(1)} %get-tuple-element.22.b_ref), custom_call_target="tpu_custom_call" | custom-call | flops 4294967296 | tf_op jit(solution)/shard_map/pallas_call | solution.py:35
  5.8 0.0 copy-start.1
  5.8 0.3 collective-permute-start.1
  6.0 1.3 %shard_map.70.g_ref = f32[256,256]{1,0:T(8,128)S(1)} custom-call(bf16[128,64,512]{2,1,0:T(8,128)(2,1)S(1)} %copy-done, bf16[128,256]{1,0:T(8,128)(2,1)S(1)} %get-tuple-element.28.a_ref, bf16[64,256]{1,0:T(8,128)(2,1)S(1)} %get-tuple-element.22.b_ref), custom_call_target="tpu_custom_call" | custom-call | flops 8589934592 | tf_op jit(solution)/shard_map/pallas_call | solution.py:35
  7.3 0.0 collective-permute-done.2.c2_ref.c2
  7.4 0.6 %shard_map.71 = (f32[128,256]{1,0:T(8,128)S(1)}, f32[128,256]{1,0:T(8,128)S(1)}) custom-call(bf16[64,256]{1,0:T(8,128)(2,1)S(1)} %get-tuple-element.22.b_ref, bf16[64,256]{1,0:T(8,128)(2,1)S(1)} %collective-permute-done.b1_ref, f32[256,256]{1,0:T(8,128)S(1)} %get-tuple-element.23.ga_ref, bf16[128,256]{1,0:T(8,128)(2,1)S(1)} %copy-done.1, ...), custom_call_target="tpu_custom_call" | custom-call | flops 268435456 | tf_op jit(solution)/shard_map/pallas_call | solution.py:35
  7.9 0.0 collective-permute-done.1.in_ref
  7.9 0.1 shard_map.72
  8.0 2.5 %collective-permute-start.3 = (f16[136,256]{1,0:T(8,128)(2,1)S(1)}, f16[136,256]{1,0:T(8,128)(2,1)S(1)}, u32[]{:S(2)}, u32[]{:S(2)}) collective-permute-start(f16[136,256]{1,0:T(8,128)(2,1)S(1)} %convert_element_type.48), channel_id=1, source_target_pairs={{0,2},{1,3},{2,0},{3,1},{4,6},{5,7},{6,4},{7,5},{8,10},{9,11},{10,... | collective-permute-start | bytes 208904 | tf_op jit(solution)/shard_map/ppermute | solution.py:31
  10.5 0.0 collective-permute-done.4.c1
  10.5 0.0 collective-permute-done.5.c3
  10.5 2.6 %shard_map.73 = (f32[128,256]{1,0:T(8,128)S(1)}, f32[64,256]{1,0:T(8,128)S(1)}, f32[256,256]{1,0:T(8,128)S(1)}) custom-call(bf16[128,64,512]{2,1,0:T(8,128)(2,1)S(1)} %copy-done, bf16[128,256]{1,0:T(8,128)(2,1)S(1)} %get-tuple-element.28.a_ref, bf16[64,256]{1,0:T(8,128)(2,1)S(1)} %get-tuple-element.22.b_ref, f32[256,256]{1,0:T(8,128)S(1)} %get-tuple-element.23.ga_ref, ...), custom_call_target="tpu_custom_call" | custom-call | flops 2147483648 | tf_op jit(solution)/shard_map/pallas_call | solution.py:35
  13.2 0.2 collective-permute-done.3
  13.4 0.1 shard_map.74
  13.5 2.8 %collective-permute-start.6 = (f16[200,256]{1,0:T(8,128)(2,1)S(1)}, f16[200,256]{1,0:T(8,128)(2,1)S(1)}, u32[]{:S(2)}, u32[]{:S(2)}) collective-permute-start(f16[200,256]{1,0:T(8,128)(2,1)S(1)} %convert_element_type.50), channel_id=1, source_target_pairs={{0,12},{4,8},{8,4},{12,0},{16,28},{20,24},{24,20},{28,16},{1,13},{... | collective-permute-start | bytes 307208 | tf_op jit(solution)/shard_map/ppermute | solution.py:31
  16.3 0.4 %collective-permute-start.7 = (f16[200,256]{1,0:T(8,128)(2,1)S(1)}, f16[200,256]{1,0:T(8,128)(2,1)S(1)}, u32[]{:S(2)}, u32[]{:S(2)}) collective-permute-start(f16[200,256]{1,0:T(8,128)(2,1)S(1)} %convert_element_type.50), channel_id=1, source_target_pairs={{0,8},{4,12},{8,0},{12,4},{16,24},{20,28},{24,16},{28,20},{1,9},{5... | collective-permute-start | bytes 307208 | tf_op jit(solution)/shard_map/ppermute | solution.py:31
  16.7 0.3 %collective-permute-start.8 = (f16[200,256]{1,0:T(8,128)(2,1)S(1)}, f16[200,256]{1,0:T(8,128)(2,1)S(1)}, u32[]{:S(2)}, u32[]{:S(2)}) collective-permute-start(f16[200,256]{1,0:T(8,128)(2,1)S(1)} %convert_element_type.50), channel_id=1, source_target_pairs={{0,4},{4,0},{8,12},{12,8},{16,20},{20,16},{24,28},{28,24},{1,5},{5... | collective-permute-start | bytes 307208 | tf_op jit(solution)/shard_map/ppermute | solution.py:31
  17.0 0.4 %shard_map.75 = f32[128,256]{1,0:T(8,128)S(1)} custom-call(bf16[128,256]{1,0:T(8,128)(2,1)S(1)} %get-tuple-element.28.a_ref, bf16[64,256]{1,0:T(8,128)(2,1)S(1)} %get-tuple-element.22.b_ref, f32[256,256]{1,0:T(8,128)S(1)} %get-tuple-element.30.gc_ref, f32[128,256]{1,0:T(8,128)S(1)} %get-tuple-element.32.slab_ref), custom_call_target="tpu_custom_call" | custom-call | flops 67108864 | tf_op jit(solution)/shard_map/pallas_call | solution.py:35
  17.5 1.8 %collective-permute-start.10 = (f32[128,256]{1,0:T(8,128)S(1)}, f32[128,256]{1,0:T(8,128)S(1)}, u32[]{:S(2)}, u32[]{:S(2)}) collective-permute-start(f32[128,256]{1,0:T(8,128)S(1)} %shard_map.75), channel_id=1, source_target_pairs={{0,2},{1,3},{2,0},{3,1},{4,6},{5,7},{6,4},{7,5},{8,10},{9,11},{10,... | collective-permute-start | bytes 393224 | tf_op jit(solution)/shard_map/ppermute | solution.py:31
  19.3 0.9 %collective-permute-done.6 = f16[200,256]{1,0:T(8,128)(2,1)S(1)} collective-permute-done((f16[200,256]{1,0:T(8,128)(2,1)S(1)}, f16[200,256]{1,0:T(8,128)(2,1)S(1)}, u32[]{:S(2)}, u32[]{:S(2)}) %collective-permute-start.6) | collective-permute-done | bytes 102432 | tf_op jit(solution)/shard_map/ppermute | solution.py:31
  20.1 1.4 %collective-permute-done.7 = f16[200,256]{1,0:T(8,128)(2,1)S(1)} collective-permute-done((f16[200,256]{1,0:T(8,128)(2,1)S(1)}, f16[200,256]{1,0:T(8,128)(2,1)S(1)}, u32[]{:S(2)}, u32[]{:S(2)}) %collective-permute-start.7) | collective-permute-done | bytes 102432 | tf_op jit(solution)/shard_map/ppermute | solution.py:31
  21.5 0.0 collective-permute-done.8
  21.6 0.1 select_convert_fusion
  21.7 3.8 %collective-permute-start.9 = (f16[200,256]{1,0:T(8,128)(2,1)S(1)}, f16[200,256]{1,0:T(8,128)(2,1)S(1)}, u32[]{:S(2)}, u32[]{:S(2)}) collective-permute-start(f16[200,256]{1,0:T(8,128)(2,1)S(1)} %select_convert_fusion), channel_id=1, source_target_pairs={{0,24},{4,28},{8,16},{12,20},{16,8},{20,12},{24,0},{28,4},{1,25},{... | collective-permute-start | bytes 307208 | tf_op jit(solution)/shard_map/ppermute | solution.py:31
  25.5 0.1 collective-permute-start.11
  25.6 2.7 %collective-permute-done.9 = f16[200,256]{1,0:T(8,128)(2,1)S(1)} collective-permute-done((f16[200,256]{1,0:T(8,128)(2,1)S(1)}, f16[200,256]{1,0:T(8,128)(2,1)S(1)}, u32[]{:S(2)}, u32[]{:S(2)}) %collective-permute-start.9) | collective-permute-done | bytes 102432 | tf_op jit(solution)/shard_map/ppermute | solution.py:31
  28.3 0.7 %shard_map.76 = (f32[128,256]{1,0:T(8,128)}, f32[128,256]{1,0:T(8,128)}, f32[64,256]{1,0:T(8,128)}) custom-call(f32[200,256]{1,0:T(8,128)S(1)} %multiply_add_fusion.v_ref, f32[128,256]{1,0:T(8,128)S(1)} %add.33.pa_ref, f32[128,256]{1,0:T(8,128)S(1)} %collective-permute-done.11.in_ref), custom_call_target="tpu_custom_call" | custom-call | tf_op jit(solution)/shard_map/pallas_call | solution.py:362
  (20 shorter events, 0.2 us)
Async XLA Ops:
  0.6 3.6 %copy-start.3 = (bf16[64,256]{1,0:T(8,128)(2,1)S(1)}, bf16[64,256]{1,0:T(8,128)(2,1)}, u32[]{:S(2)}) copy-start(bf16[64,256]{1,0:T(8,128)(2,1)} %b_in.1) | copy-start | bytes 98308
  0.6 3.6 %copy-start.2 = (bf16[128,256]{1,0:T(8,128)(2,1)S(1)}, bf16[128,256]{1,0:T(8,128)(2,1)}, u32[]{:S(2)}) copy-start(bf16[128,256]{1,0:T(8,128)(2,1)} %a_in.1) | copy-start | bytes 196612
  0.7 3.8 %copy-start = (bf16[128,64,512]{2,1,0:T(8,128)(2,1)S(1)}, bf16[128,64,512]{2,1,0:T(8,128)(2,1)}, u32[]{:S(2)}) copy-start(bf16[128,64,512]{2,1,0:T(8,128)(2,1)} %x_ref.5) | copy-start | bytes 25165828
  0.7 6.7 %collective-permute-start.2 = (bf16[128,256]{1,0:T(8,128)(2,1)}, bf16[128,256]{1,0:T(8,128)(2,1)S(1)}, u32[]{:S(2)}, u32[]{:S(2)}) collective-permute-start(bf16[128,256]{1,0:T(8,128)(2,1)} %c0.1), channel_id=1, source_target_pairs={{0,2},{1,3},{2,0},{3,1},{4,6},{5,7},{6,4},{7,5},{8,10},{9,11},{10,... | collective-permute-start | bytes 196616 | tf_op jit(solution)/shard_map/ppermute | solution.py:31
  3.7 6.8 %collective-permute-start.4 = (bf16[128,256]{1,0:T(8,128)(2,1)}, bf16[128,256]{1,0:T(8,128)(2,1)S(1)}, u32[]{:S(2)}, u32[]{:S(2)}) collective-permute-start(bf16[128,256]{1,0:T(8,128)(2,1)} %c0.1), channel_id=1, source_target_pairs={{0,1},{1,0},{2,3},{3,2},{4,5},{5,4},{6,7},{7,6},{8,9},{9,8},{10,11... | collective-permute-start | bytes 196616 | tf_op jit(solution)/shard_map/ppermute | solution.py:31
  3.7 6.8 %collective-permute-start.5 = (bf16[128,256]{1,0:T(8,128)(2,1)}, bf16[128,256]{1,0:T(8,128)(2,1)S(1)}, u32[]{:S(2)}, u32[]{:S(2)}) collective-permute-start(bf16[128,256]{1,0:T(8,128)(2,1)} %c0.1), channel_id=1, source_target_pairs={{0,3},{1,2},{2,1},{3,0},{4,7},{5,6},{6,5},{7,4},{8,11},{9,10},{10,... | collective-permute-start | bytes 196616 | tf_op jit(solution)/shard_map/ppermute | solution.py:31
  3.9 2.1 %collective-permute-start = (bf16[64,256]{1,0:T(8,128)(2,1)}, bf16[64,256]{1,0:T(8,128)(2,1)S(1)}, u32[]{:S(2)}, u32[]{:S(2)}) collective-permute-start(bf16[64,256]{1,0:T(8,128)(2,1)} %b_in.1), channel_id=1, source_target_pairs={{0,1},{1,0},{2,3},{3,2},{4,5},{5,4},{6,7},{7,6},{8,9},{9,8},{10,11... | collective-permute-start | bytes 98312 | tf_op jit(solution)/shard_map/ppermute | solution.py:31
  5.8 1.6 %copy-start.1 = (bf16[128,256]{1,0:T(8,128)(2,1)S(1)}, bf16[128,256]{1,0:T(8,128)(2,1)}, u32[]{:S(2)}) copy-start(bf16[128,256]{1,0:T(8,128)(2,1)} %c0.1) | copy-start | bytes 196612
  5.8 2.2 %collective-permute-start.1 = (f32[256,256]{1,0:T(8,128)S(1)}, f32[256,256]{1,0:T(8,128)S(1)}, u32[]{:S(2)}, u32[]{:S(2)}) collective-permute-start(f32[256,256]{1,0:T(8,128)S(1)} %shard_map.69), channel_id=1, source_target_pairs={{0,1},{1,0},{2,3},{3,2},{4,5},{5,4},{6,7},{7,6},{8,9},{9,8},{10,11... | collective-permute-start | bytes 786440 | tf_op jit(solution)/shard_map/ppermute | solution.py:31
  8.0 5.3 %collective-permute-start.3 = (f16[136,256]{1,0:T(8,128)(2,1)S(1)}, f16[136,256]{1,0:T(8,128)(2,1)S(1)}, u32[]{:S(2)}, u32[]{:S(2)}) collective-permute-start(f16[136,256]{1,0:T(8,128)(2,1)S(1)} %convert_element_type.48), channel_id=1, source_target_pairs={{0,2},{1,3},{2,0},{3,1},{4,6},{5,7},{6,4},{7,5},{8,10},{9,11},{10,... | collective-permute-start | bytes 208904 | tf_op jit(solution)/shard_map/ppermute | solution.py:31
  13.5 6.7 %collective-permute-start.6 = (f16[200,256]{1,0:T(8,128)(2,1)S(1)}, f16[200,256]{1,0:T(8,128)(2,1)S(1)}, u32[]{:S(2)}, u32[]{:S(2)}) collective-permute-start(f16[200,256]{1,0:T(8,128)(2,1)S(1)} %convert_element_type.50), channel_id=1, source_target_pairs={{0,12},{4,8},{8,4},{12,0},{16,28},{20,24},{24,20},{28,16},{1,13},{... | collective-permute-start | bytes 307208 | tf_op jit(solution)/shard_map/ppermute | solution.py:31
  16.3 5.3 %collective-permute-start.7 = (f16[200,256]{1,0:T(8,128)(2,1)S(1)}, f16[200,256]{1,0:T(8,128)(2,1)S(1)}, u32[]{:S(2)}, u32[]{:S(2)}) collective-permute-start(f16[200,256]{1,0:T(8,128)(2,1)S(1)} %convert_element_type.50), channel_id=1, source_target_pairs={{0,8},{4,12},{8,0},{12,4},{16,24},{20,28},{24,16},{28,20},{1,9},{5... | collective-permute-start | bytes 307208 | tf_op jit(solution)/shard_map/ppermute | solution.py:31
  16.7 4.8 %collective-permute-start.8 = (f16[200,256]{1,0:T(8,128)(2,1)S(1)}, f16[200,256]{1,0:T(8,128)(2,1)S(1)}, u32[]{:S(2)}, u32[]{:S(2)}) collective-permute-start(f16[200,256]{1,0:T(8,128)(2,1)S(1)} %convert_element_type.50), channel_id=1, source_target_pairs={{0,4},{4,0},{8,12},{12,8},{16,20},{20,16},{24,28},{28,24},{1,5},{5... | collective-permute-start | bytes 307208 | tf_op jit(solution)/shard_map/ppermute | solution.py:31
  17.5 8.0 %collective-permute-start.10 = (f32[128,256]{1,0:T(8,128)S(1)}, f32[128,256]{1,0:T(8,128)S(1)}, u32[]{:S(2)}, u32[]{:S(2)}) collective-permute-start(f32[128,256]{1,0:T(8,128)S(1)} %shard_map.75), channel_id=1, source_target_pairs={{0,2},{1,3},{2,0},{3,1},{4,6},{5,7},{6,4},{7,5},{8,10},{9,11},{10,... | collective-permute-start | bytes 393224 | tf_op jit(solution)/shard_map/ppermute | solution.py:31
  21.7 6.6 %collective-permute-start.9 = (f16[200,256]{1,0:T(8,128)(2,1)S(1)}, f16[200,256]{1,0:T(8,128)(2,1)S(1)}, u32[]{:S(2)}, u32[]{:S(2)}) collective-permute-start(f16[200,256]{1,0:T(8,128)(2,1)S(1)} %select_convert_fusion), channel_id=1, source_target_pairs={{0,24},{4,28},{8,16},{12,20},{16,8},{20,12},{24,0},{28,4},{1,25},{... | collective-permute-start | bytes 307208 | tf_op jit(solution)/shard_map/ppermute | solution.py:31
  25.5 2.8 %collective-permute-start.11 = (f32[128,256]{1,0:T(8,128)S(1)}, f32[128,256]{1,0:T(8,128)S(1)}, u32[]{:S(2)}, u32[]{:S(2)}) collective-permute-start(f32[128,256]{1,0:T(8,128)S(1)} %add.33.pa_ref), channel_id=1, source_target_pairs={{0,1},{1,0},{2,3},{3,2},{4,5},{5,4},{6,7},{7,6},{8,9},{9,8},{10,11... | collective-permute-start | bytes 393224 | tf_op jit(solution)/shard_map/ppermute | solution.py:31

commit v7 on v6

--- a/solution.py
+++ b/solution.py
@@ -134,10 +134,13 @@
     ga_ref[...] = gram(a_in[...])
 
 
-def terms(b_ref, b1_ref, ga_ref, own_ref, c2_ref, keep_ref, away_ref):
-    parts = halves(ga_ref[...] * (gram(b_ref[...]) + gram(b1_ref[...])))
-    for rows, out in ((own_ref, keep_ref), (c2_ref, away_ref)):
-        out[...] = sum(jnp.dot(rows[...], part, preferred_element_type=F32) for part in parts)
+def height_and_gram(offsets, x_ref, a_ref, b_ref, b1_ref, ga_ref, g_ref, hi_ref, lo_ref):
+    hi_ref[...], lo_ref[...] = halves(ga_ref[...] * (gram(b_ref[...]) + gram(b1_ref[...])))
+    height_terms(offsets, x_ref, a_ref, b_ref, g_ref)
+
+
+def through(rows_ref, hi_ref, lo_ref):
+    return sum(jnp.dot(rows_ref[...], part[...], preferred_element_type=F32) for part in (hi_ref, lo_ref))
 
 
 def write_message(m_ref, *parts):
@@ -151,11 +154,10 @@
     m_ref[at:] = jnp.broadcast_to(e, (m_ref.shape[0] - at, e.shape[1]))
 
 
-def meet(to_height, g_ref, in_ref, keep_in, away_in, keep_ref, m_ref):
-    h_own = keep_in.shape[0]
-    g = g_ref[...] + in_ref[...]
-    keep_ref[...] = (keep_in[...] - g[0:h_own]) * to_height
-    write_message(m_ref, (away_in[...] - g[h_own:]) * to_height)
+def meet(to_height, g_ref, in_ref, c2_ref, hi_ref, lo_ref, keep_ref, m_ref):
+    h_own = keep_ref.shape[0]
+    write_message(m_ref, (through(c2_ref, hi_ref, lo_ref) - (g_ref[h_own:] + in_ref[h_own:])) * to_height)
+    keep_ref[...] = g_ref[0:h_own] + in_ref[0:h_own]
 
 
 def combine(keep_ref, in_ref, ps_ref, m_ref):
@@ -168,7 +170,10 @@
     pa_ref[...] = (times(a_ref[...], gram(b_ref[...]) * gc_ref[...]) - slab_ref[...]) * to_radius
 
 
-def project_four(to_source, x_ref, a_ref, b_ref, ga_ref, c0, c1, c2, c3, pa_ref, ps_ref, gc_ref, heights):
+def project_four(
+    to_height, to_source, x_ref, a_ref, b_ref, ga_ref, slab_ref, hi_ref, lo_ref, c0, c1, c2, c3,
+    pa_ref, ps_ref, gc_ref, keep_ref, heights,
+):
     s_rows, rank = b_ref.shape
     r_rows = a_ref.shape[0]
     h_own = c0.shape[0]
@@ -179,6 +184,7 @@
     proj = jnp.dot(x, heights[...], preferred_element_type=F32).reshape(r_rows, s_rows, rank)
     pa_ref[...] = (proj * b_ref[...].astype(F32)[None]).sum(1)
     ps = (proj * a_ref[...].astype(F32)[:, None, :]).sum(0)
+    keep_ref[...] = (through(c0, hi_ref, lo_ref) - slab_ref[...]) * to_height
     gc = gram(heights[...])
     gc_ref[...] = gc
     ps_ref[...] = (times(b_ref[...], ga_ref[...] * gc) - ps) * to_source
@@ -203,22 +209,24 @@
     half, block = [((width // 2, rank), F32)], [((h_own, rank), F32)]
     (g_away,) = call(functools.partial(height_terms, (1, 3)), half, (slab, a, b), 2 * work, resident=False)
     g_in = swap(g_away, "src", 1)
-    (g_keep,) = call(
-        functools.partial(height_terms, (0, 2)), half, (slab, after(a, g_away, b1), b), 4 * work
-    )
-    keep, away = call(terms, block * 2, (after(b, g_keep), b1, ga, height_factor, c2), work // 8)
-    keep, away = call(
+    g_keep, hi, lo = call(
+        functools.partial(height_and_gram, (0, 2)),
+        half + [((rank, rank), BF16)] * 2,
+        (slab, after(a, g_away), b, b1, ga),
+        4 * work,
+    )
+    slab_part, away = call(
         functools.partial(meet, scales[1]),
         block + [((h_own + TAIL, rank), F32)],
-        (g_keep, g_in, keep, away),
+        (g_keep, g_in, c2, hi, lo),
         work // 32,
     )
     away = away.astype(F16)
     share_in = swap(away, "src", 2)
-    pa, ps, gc = call(
-        functools.partial(project_four, scales[2]),
-        [((r_rows, rank), F32), ((s_rows, rank), F32), ((rank, rank), F32)],
-        (slab, after(a, away), b, ga, height_factor, c1, c2, c3),
+    pa, ps, gc, keep = call(
+        functools.partial(project_four, scales[1], scales[2]),
+        [((r_rows, rank), F32), ((s_rows, rank), F32), ((rank, rank), F32)] + block,
+        (slab, after(a, away), b, ga, slab_part, hi, lo, height_factor, c1, c2, c3),
         work,
         scratch=[pltpu.VMEM((width, rank), BF16)],
     )

time: 29.2 us -> 28.9 us (0.990)
  Pallas kernels: 7.28 us -> 6.97 us
    pallas_call x9 -> x8, Pallas kernels: 6.54 us -> 6.23 us  [call(): pl.pallas_call(body, in_specs=[WHOLE] * len(args), out_specs=[WHOLE] * le...]
  transfers between devices with their start and end apart: 12 -> 12, of which waited for: 4 -> 3; matrix products, arithmetic and copies ran while one was open for 1% -> 1% of each run, Pallas kernels for 22% -> 22%
where the time goes in v7:
time: 28.9 us; the launch traced here: 28.7 us
  starting transfers between devices  15.7 us (54%)
  Pallas kernels  6.97 us (24%)
  waiting for transfers between devices  5.03 us (17%)
  between operations  0.8 us (3%)
    ppermute x12, starting transfers between devices, swap(): lax.ppermute(x, axis, [(i, i ^ bit) for i in range(lax.axis_size(axis))])  15.7 us
    pallas_call x8, Pallas kernels, call(): pl.pallas_call(body, in_specs=[WHOLE] * len(args), out_specs=[WHOLE] * le...  6.23 us
    ppermute x12, waiting for transfers between devices, swap(): lax.ppermute(x, axis, [(i, i ^ bit) for i in range(lax.axis_size(axis))])  5.03 us
    pallas_call x1, Pallas kernels, per_device(): pl.pallas_call(finish, in_specs=[WHOLE] * 3, out_specs=[WHOLE] * 3, out_s...  0.74 us
  transfers between devices with their start and end apart: 12, of which 3 were waited for; matrix products, arithmetic and copies ran while one was open for 1% of the time, Pallas kernels for 22%

profile of v7, /device:TPU:0, one launch (start us, length us, event | category | flops | bytes accessed | tf_op | source)
XLA Modules:
  0.0 28.7 jit_solution(5706817407438196312)
XLA Ops:
  0.7 3.0 %collective-permute-start.2 = (bf16[128,256]{1,0:T(8,128)(2,1)}, bf16[128,256]{1,0:T(8,128)(2,1)S(1)}, u32[]{:S(2)}, u32[]{:S(2)}) collective-permute-start(bf16[128,256]{1,0:T(8,128)(2,1)} %c0.1), channel_id=1, source_target_pairs={{0,2},{1,3},{2,0},{3,1},{4,6},{5,7},{6,4},{7,5},{8,10},{9,11},{10,... | collective-permute-start | bytes 196616 | tf_op jit(solution)/shard_map/ppermute | solution.py:31
  3.7 0.0 collective-permute-start.3
  3.7 0.2 collective-permute-start.4
  3.9 0.3 %collective-permute-start = (bf16[64,256]{1,0:T(8,128)(2,1)}, bf16[64,256]{1,0:T(8,128)(2,1)S(1)}, u32[]{:S(2)}, u32[]{:S(2)}) collective-permute-start(bf16[64,256]{1,0:T(8,128)(2,1)} %b_in.1), channel_id=1, source_target_pairs={{0,1},{1,0},{2,3},{3,2},{4,5},{5,4},{6,7},{7,6},{8,9},{9,8},{10,11... | collective-permute-start | bytes 98312 | tf_op jit(solution)/shard_map/ppermute | solution.py:31
  4.2 0.2 shard_map.68
  4.4 1.3 %shard_map.69 = f32[256,256]{1,0:T(8,128)S(1)} custom-call(bf16[128,64,512]{2,1,0:T(8,128)(2,1)S(1)} %copy-done, bf16[128,256]{1,0:T(8,128)(2,1)S(1)} %get-tuple-element.28.a_ref, bf16[64,256]{1,0:T(8,128)(2,1)S(1)} %get-tuple-element.21.b_ref), custom_call_target="tpu_custom_call" | custom-call | flops 4294967296 | tf_op jit(solution)/shard_map/pallas_call | solution.py:35
  5.8 0.3 collective-permute-start.1
  6.0 0.0 collective-permute-done.b1_ref
  6.0 1.4 %shard_map.70 = (f32[256,256]{1,0:T(8,128)S(1)}, bf16[256,256]{1,0:T(8,128)(2,1)S(1)}, bf16[256,256]{1,0:T(8,128)(2,1)S(1)}) custom-call(bf16[128,64,512]{2,1,0:T(8,128)(2,1)S(1)} %copy-done, bf16[128,256]{1,0:T(8,128)(2,1)S(1)} %get-tuple-element.28.a_ref, bf16[64,256]{1,0:T(8,128)(2,1)S(1)} %get-tuple-element.21.b_ref, ...), custom_call_target="tpu_custom_call" | custom-call | flops 8589934592 | tf_op jit(solution)/shard_map/pallas_call | solution.py:35
  7.4 0.0 collective-permute-done.2.c2_ref.c2
  7.4 0.0 collective-permute-done.1.in_ref
  7.4 0.2 shard_map.71
  7.7 2.6 %collective-permute-start.5 = (f16[136,256]{1,0:T(8,128)(2,1)S(1)}, f16[136,256]{1,0:T(8,128)(2,1)S(1)}, u32[]{:S(2)}, u32[]{:S(2)}) collective-permute-start(f16[136,256]{1,0:T(8,128)(2,1)S(1)} %convert_element_type.48), channel_id=1, source_target_pairs={{0,2},{1,3},{2,0},{3,1},{4,6},{5,7},{6,4},{7,5},{8,10},{9,11},{10,... | collective-permute-start | bytes 208904 | tf_op jit(solution)/shard_map/ppermute | solution.py:31
  10.3 0.0 collective-permute-done.3.c1
  10.3 0.0 collective-permute-done.4.c3
  10.3 2.7 %shard_map.72 = (f32[128,256]{1,0:T(8,128)S(1)}, f32[64,256]{1,0:T(8,128)S(1)}, f32[256,256]{1,0:T(8,128)S(1)}, f32[128,256]{1,0:T(8,128)S(1)}) custom-call(bf16[128,64,512]{2,1,0:T(8,128)(2,1)S(1)} %copy-done, bf16[128,256]{1,0:T(8,128)(2,1)S(1)} %get-tuple-element.28.a_ref, bf16[64,256]{1,0:T(8,128)(2,1)S(1)} %get-tuple-element.21.b_ref, ...), custom_call_target="tpu_custom_call" | custom-call | flops 2147483648 | tf_op jit(solution)/shard_map/pallas_call | solution.py:35
  13.0 0.0 collective-permute-done.5
  13.0 0.1 shard_map.73
  13.1 2.8 %collective-permute-start.6 = (f16[200,256]{1,0:T(8,128)(2,1)S(1)}, f16[200,256]{1,0:T(8,128)(2,1)S(1)}, u32[]{:S(2)}, u32[]{:S(2)}) collective-permute-start(f16[200,256]{1,0:T(8,128)(2,1)S(1)} %convert_element_type.50), channel_id=1, source_target_pairs={{0,12},{4,8},{8,4},{12,0},{16,28},{20,24},{24,20},{28,16},{1,13},{... | collective-permute-start | bytes 307208 | tf_op jit(solution)/shard_map/ppermute | solution.py:31
  15.9 0.4 %collective-permute-start.7 = (f16[200,256]{1,0:T(8,128)(2,1)S(1)}, f16[200,256]{1,0:T(8,128)(2,1)S(1)}, u32[]{:S(2)}, u32[]{:S(2)}) collective-permute-start(f16[200,256]{1,0:T(8,128)(2,1)S(1)} %convert_element_type.50), channel_id=1, source_target_pairs={{0,8},{4,12},{8,0},{12,4},{16,24},{20,28},{24,16},{28,20},{1,9},{5... | collective-permute-start | bytes 307208 | tf_op jit(solution)/shard_map/ppermute | solution.py:31
  16.3 0.3 %collective-permute-start.8 = (f16[200,256]{1,0:T(8,128)(2,1)S(1)}, f16[200,256]{1,0:T(8,128)(2,1)S(1)}, u32[]{:S(2)}, u32[]{:S(2)}) collective-permute-start(f16[200,256]{1,0:T(8,128)(2,1)S(1)} %convert_element_type.50), channel_id=1, source_target_pairs={{0,4},{4,0},{8,12},{12,8},{16,20},{20,16},{24,28},{28,24},{1,5},{5... | collective-permute-start | bytes 307208 | tf_op jit(solution)/shard_map/ppermute | solution.py:31
  16.7 0.4 %shard_map.74 = f32[128,256]{1,0:T(8,128)S(1)} custom-call(bf16[128,256]{1,0:T(8,128)(2,1)S(1)} %get-tuple-element.28.a_ref, bf16[64,256]{1,0:T(8,128)(2,1)S(1)} %get-tuple-element.21.b_ref, f32[256,256]{1,0:T(8,128)S(1)} %get-tuple-element.32.gc_ref, f32[128,256]{1,0:T(8,128)S(1)} %get-tuple-element.34.slab_ref), custom_call_target="tpu_custom_call" | custom-call | flops 67108864 | tf_op jit(solution)/shard_map/pallas_call | solution.py:35
  17.1 1.8 %collective-permute-start.10 = (f32[128,256]{1,0:T(8,128)S(1)}, f32[128,256]{1,0:T(8,128)S(1)}, u32[]{:S(2)}, u32[]{:S(2)}) collective-permute-start(f32[128,256]{1,0:T(8,128)S(1)} %shard_map.74), channel_id=1, source_target_pairs={{0,2},{1,3},{2,0},{3,1},{4,6},{5,7},{6,4},{7,5},{8,10},{9,11},{10,... | collective-permute-start | bytes 393224 | tf_op jit(solution)/shard_map/ppermute | solution.py:31
  18.9 0.9 %collective-permute-done.6 = f16[200,256]{1,0:T(8,128)(2,1)S(1)} collective-permute-done((f16[200,256]{1,0:T(8,128)(2,1)S(1)}, f16[200,256]{1,0:T(8,128)(2,1)S(1)}, u32[]{:S(2)}, u32[]{:S(2)}) %collective-permute-start.6) | collective-permute-done | bytes 102432 | tf_op jit(solution)/shard_map/ppermute | solution.py:31
  19.8 1.4 %collective-permute-done.7 = f16[200,256]{1,0:T(8,128)(2,1)S(1)} collective-permute-done((f16[200,256]{1,0:T(8,128)(2,1)S(1)}, f16[200,256]{1,0:T(8,128)(2,1)S(1)}, u32[]{:S(2)}, u32[]{:S(2)}) %collective-permute-start.7) | collective-permute-done | bytes 102432 | tf_op jit(solution)/shard_map/ppermute | solution.py:31
  21.2 0.0 collective-permute-done.8
  21.2 0.1 select_convert_fusion
  21.3 3.8 %collective-permute-start.9 = (f16[200,256]{1,0:T(8,128)(2,1)S(1)}, f16[200,256]{1,0:T(8,128)(2,1)S(1)}, u32[]{:S(2)}, u32[]{:S(2)}) collective-permute-start(f16[200,256]{1,0:T(8,128)(2,1)S(1)} %select_convert_fusion), channel_id=1, source_target_pairs={{0,24},{4,28},{8,16},{12,20},{16,8},{20,12},{24,0},{28,4},{1,25},{... | collective-permute-start | bytes 307208 | tf_op jit(solution)/shard_map/ppermute | solution.py:31
  25.1 0.0 collective-permute-done.10
  25.2 0.1 collective-permute-start.11
  25.3 2.7 %collective-permute-done.9 = f16[200,256]{1,0:T(8,128)(2,1)S(1)} collective-permute-done((f16[200,256]{1,0:T(8,128)(2,1)S(1)}, f16[200,256]{1,0:T(8,128)(2,1)S(1)}, u32[]{:S(2)}, u32[]{:S(2)}) %collective-permute-start.9) | collective-permute-done | bytes 102432 | tf_op jit(solution)/shard_map/ppermute | solution.py:31
  28.0 0.7 %shard_map.75 = (f32[128,256]{1,0:T(8,128)}, f32[128,256]{1,0:T(8,128)}, f32[64,256]{1,0:T(8,128)}) custom-call(f32[200,256]{1,0:T(8,128)S(1)} %multiply_add_fusion.v_ref, f32[128,256]{1,0:T(8,128)S(1)} %add.33.pa_ref, f32[128,256]{1,0:T(8,128)S(1)} %collective-permute-done.11.in_ref), custom_call_target="tpu_custom_call" | custom-call | tf_op jit(solution)/shard_map/pallas_call | solution.py:370
  (19 shorter events, 0.2 us)
Async XLA Ops:
  0.6 3.6 %copy-start.3 = (bf16[64,256]{1,0:T(8,128)(2,1)S(1)}, bf16[64,256]{1,0:T(8,128)(2,1)}, u32[]{:S(2)}) copy-start(bf16[64,256]{1,0:T(8,128)(2,1)} %b_in.1) | copy-start | bytes 98308
  0.6 3.6 %copy-start.2 = (bf16[128,256]{1,0:T(8,128)(2,1)S(1)}, bf16[128,256]{1,0:T(8,128)(2,1)}, u32[]{:S(2)}) copy-start(bf16[128,256]{1,0:T(8,128)(2,1)} %a_in.1) | copy-start | bytes 196612
  0.7 3.8 %copy-start = (bf16[128,64,512]{2,1,0:T(8,128)(2,1)S(1)}, bf16[128,64,512]{2,1,0:T(8,128)(2,1)}, u32[]{:S(2)}) copy-start(bf16[128,64,512]{2,1,0:T(8,128)(2,1)} %x_ref.5) | copy-start | bytes 25165828
  0.7 6.7 %collective-permute-start.2 = (bf16[128,256]{1,0:T(8,128)(2,1)}, bf16[128,256]{1,0:T(8,128)(2,1)S(1)}, u32[]{:S(2)}, u32[]{:S(2)}) collective-permute-start(bf16[128,256]{1,0:T(8,128)(2,1)} %c0.1), channel_id=1, source_target_pairs={{0,2},{1,3},{2,0},{3,1},{4,6},{5,7},{6,4},{7,5},{8,10},{9,11},{10,... | collective-permute-start | bytes 196616 | tf_op jit(solution)/shard_map/ppermute | solution.py:31
  3.7 6.6 %collective-permute-start.3 = (bf16[128,256]{1,0:T(8,128)(2,1)}, bf16[128,256]{1,0:T(8,128)(2,1)S(1)}, u32[]{:S(2)}, u32[]{:S(2)}) collective-permute-start(bf16[128,256]{1,0:T(8,128)(2,1)} %c0.1), channel_id=1, source_target_pairs={{0,1},{1,0},{2,3},{3,2},{4,5},{5,4},{6,7},{7,6},{8,9},{9,8},{10,11... | collective-permute-start | bytes 196616 | tf_op jit(solution)/shard_map/ppermute | solution.py:31
  3.7 6.6 %collective-permute-start.4 = (bf16[128,256]{1,0:T(8,128)(2,1)}, bf16[128,256]{1,0:T(8,128)(2,1)S(1)}, u32[]{:S(2)}, u32[]{:S(2)}) collective-permute-start(bf16[128,256]{1,0:T(8,128)(2,1)} %c0.1), channel_id=1, source_target_pairs={{0,3},{1,2},{2,1},{3,0},{4,7},{5,6},{6,5},{7,4},{8,11},{9,10},{10,... | collective-permute-start | bytes 196616 | tf_op jit(solution)/shard_map/ppermute | solution.py:31
  3.9 2.1 %collective-permute-start = (bf16[64,256]{1,0:T(8,128)(2,1)}, bf16[64,256]{1,0:T(8,128)(2,1)S(1)}, u32[]{:S(2)}, u32[]{:S(2)}) collective-permute-start(bf16[64,256]{1,0:T(8,128)(2,1)} %b_in.1), channel_id=1, source_target_pairs={{0,1},{1,0},{2,3},{3,2},{4,5},{5,4},{6,7},{7,6},{8,9},{9,8},{10,11... | collective-permute-start | bytes 98312 | tf_op jit(solution)/shard_map/ppermute | solution.py:31
  5.8 1.6 %collective-permute-start.1 = (f32[256,256]{1,0:T(8,128)S(1)}, f32[256,256]{1,0:T(8,128)S(1)}, u32[]{:S(2)}, u32[]{:S(2)}) collective-permute-start(f32[256,256]{1,0:T(8,128)S(1)} %shard_map.69), channel_id=1, source_target_pairs={{0,1},{1,0},{2,3},{3,2},{4,5},{5,4},{6,7},{7,6},{8,9},{9,8},{10,11... | collective-permute-start | bytes 786440 | tf_op jit(solution)/shard_map/ppermute | solution.py:31
  6.0 4.3 %copy-start.1 = (bf16[128,256]{1,0:T(8,128)(2,1)S(1)}, bf16[128,256]{1,0:T(8,128)(2,1)}, u32[]{:S(2)}) copy-start(bf16[128,256]{1,0:T(8,128)(2,1)} %c0.1) | copy-start | bytes 196612
  7.7 5.3 %collective-permute-start.5 = (f16[136,256]{1,0:T(8,128)(2,1)S(1)}, f16[136,256]{1,0:T(8,128)(2,1)S(1)}, u32[]{:S(2)}, u32[]{:S(2)}) collective-permute-start(f16[136,256]{1,0:T(8,128)(2,1)S(1)} %convert_element_type.48), channel_id=1, source_target_pairs={{0,2},{1,3},{2,0},{3,1},{4,6},{5,7},{6,4},{7,5},{8,10},{9,11},{10,... | collective-permute-start | bytes 208904 | tf_op jit(solution)/shard_map/ppermute | solution.py:31
  13.1 6.7 %collective-permute-start.6 = (f16[200,256]{1,0:T(8,128)(2,1)S(1)}, f16[200,256]{1,0:T(8,128)(2,1)S(1)}, u32[]{:S(2)}, u32[]{:S(2)}) collective-permute-start(f16[200,256]{1,0:T(8,128)(2,1)S(1)} %convert_element_type.50), channel_id=1, source_target_pairs={{0,12},{4,8},{8,4},{12,0},{16,28},{20,24},{24,20},{28,16},{1,13},{... | collective-permute-start | bytes 307208 | tf_op jit(solution)/shard_map/ppermute | solution.py:31
  15.9 5.3 %collective-permute-start.7 = (f16[200,256]{1,0:T(8,128)(2,1)S(1)}, f16[200,256]{1,0:T(8,128)(2,1)S(1)}, u32[]{:S(2)}, u32[]{:S(2)}) collective-permute-start(f16[200,256]{1,0:T(8,128)(2,1)S(1)} %convert_element_type.50), channel_id=1, source_target_pairs={{0,8},{4,12},{8,0},{12,4},{16,24},{20,28},{24,16},{28,20},{1,9},{5... | collective-permute-start | bytes 307208 | tf_op jit(solution)/shard_map/ppermute | solution.py:31
  16.3 4.9 %collective-permute-start.8 = (f16[200,256]{1,0:T(8,128)(2,1)S(1)}, f16[200,256]{1,0:T(8,128)(2,1)S(1)}, u32[]{:S(2)}, u32[]{:S(2)}) collective-permute-start(f16[200,256]{1,0:T(8,128)(2,1)S(1)} %convert_element_type.50), channel_id=1, source_target_pairs={{0,4},{4,0},{8,12},{12,8},{16,20},{20,16},{24,28},{28,24},{1,5},{5... | collective-permute-start | bytes 307208 | tf_op jit(solution)/shard_map/ppermute | solution.py:31
  17.1 8.1 %collective-permute-start.10 = (f32[128,256]{1,0:T(8,128)S(1)}, f32[128,256]{1,0:T(8,128)S(1)}, u32[]{:S(2)}, u32[]{:S(2)}) collective-permute-start(f32[128,256]{1,0:T(8,128)S(1)} %shard_map.74), channel_id=1, source_target_pairs={{0,2},{1,3},{2,0},{3,1},{4,6},{5,7},{6,4},{7,5},{8,10},{9,11},{10,... | collective-permute-start | bytes 393224 | tf_op jit(solution)/shard_map/ppermute | solution.py:31
  21.3 6.6 %collective-permute-start.9 = (f16[200,256]{1,0:T(8,128)(2,1)S(1)}, f16[200,256]{1,0:T(8,128)(2,1)S(1)}, u32[]{:S(2)}, u32[]{:S(2)}) collective-permute-start(f16[200,256]{1,0:T(8,128)(2,1)S(1)} %select_convert_fusion), channel_id=1, source_target_pairs={{0,24},{4,28},{8,16},{12,20},{16,8},{20,12},{24,0},{28,4},{1,25},{... | collective-permute-start | bytes 307208 | tf_op jit(solution)/shard_map/ppermute | solution.py:31
  25.2 2.8 %collective-permute-start.11 = (f32[128,256]{1,0:T(8,128)S(1)}, f32[128,256]{1,0:T(8,128)S(1)}, u32[]{:S(2)}, u32[]{:S(2)}) collective-permute-start(f32[128,256]{1,0:T(8,128)S(1)} %add.33.pa_ref), channel_id=1, source_target_pairs={{0,1},{1,0},{2,3},{3,2},{4,5},{5,4},{6,7},{7,6},{8,9},{9,8},{10,11... | collective-permute-start | bytes 393224 | tf_op jit(solution)/shard_map/ppermute | solution.py:31

commit v8 on v7

--- a/solution.py
+++ b/solution.py
@@ -348,12 +348,12 @@
     local = local_four if n_src == 4 and h_own % LANES == 0 else local_any
     pa, m = local(slab, radius_factor, height_factor, source_factor, scales)
     bits = src_bits[::-1]
-    stages = [rad_bits[i : i + 2] for i in range(0, len(rad_bits), 2)]
+    stages = [rad_bits[i : i + 2] for i in range(0, len(rad_bits), 2)][::-1]
     for i, stage in enumerate(stages):
         if len(stage) == 2:
             others = [sum(stage), stage[1], stage[0]]
         else:
-            others = [stage[0] + (stage[0] // 2 if i else 0)]
+            others = [stage[0] + stage[0] // 2]
         terms = [unpack(m)] + [unpack(swap(m, "rad", o)) for o in others]
         if len(bits) > 1:
             pa = after(pa, m)

time: 28.9 us -> 28.8 us (level)
  transfers between devices with their start and end apart: 12 -> 12, of which waited for: 3 -> 4; matrix products, arithmetic and copies ran while one was open for 1% -> 1% of each run, Pallas kernels for 22% -> 22%
where the time goes in v8:
time: 28.8 us; the launch traced here: 28.7 us
  starting transfers between devices  15.5 us (54%)
  Pallas kernels  6.97 us (24%)
  waiting for transfers between devices  5.02 us (17%)
  between operations  0.8 us (3%)
  other arithmetic  0.32 us (1%)
    ppermute x12, starting transfers between devices, swap(): lax.ppermute(x, axis, [(i, i ^ bit) for i in range(lax.axis_size(axis))])  15.5 us
    pallas_call x8, Pallas kernels, call(): pl.pallas_call(body, in_specs=[WHOLE] * len(args), out_specs=[WHOLE] * le...  6.23 us
    ppermute x12, waiting for transfers between devices, swap(): lax.ppermute(x, axis, [(i, i ^ bit) for i in range(lax.axis_size(axis))])  5.02 us
    pallas_call x1, Pallas kernels, per_device(): pl.pallas_call(finish, in_specs=[WHOLE] * 3, out_specs=[WHOLE] * 3, out_s...  0.74 us
  transfers between devices with their start and end apart: 12, of which 4 were waited for; matrix products, arithmetic and copies ran while one was open for 1% of the time, Pallas kernels for 22%

profile of v8, /device:TPU:0, one launch (start us, length us, event | category | flops | bytes accessed | tf_op | source)
XLA Modules:
  0.0 28.7 jit_solution(17391776462366924252)
XLA Ops:
  0.7 3.0 %collective-permute-start.2 = (bf16[128,256]{1,0:T(8,128)(2,1)}, bf16[128,256]{1,0:T(8,128)(2,1)S(1)}, u32[]{:S(2)}, u32[]{:S(2)}) collective-permute-start(bf16[128,256]{1,0:T(8,128)(2,1)} %c0.1), channel_id=1, source_target_pairs={{0,2},{1,3},{2,0},{3,1},{4,6},{5,7},{6,4},{7,5},{8,10},{9,11},{10,... | collective-permute-start | bytes 196616 | tf_op jit(solution)/shard_map/ppermute | solution.py:31
  3.7 0.0 collective-permute-start.3
  3.7 0.2 collective-permute-start.4
  3.9 0.3 %collective-permute-start = (bf16[64,256]{1,0:T(8,128)(2,1)}, bf16[64,256]{1,0:T(8,128)(2,1)S(1)}, u32[]{:S(2)}, u32[]{:S(2)}) collective-permute-start(bf16[64,256]{1,0:T(8,128)(2,1)} %b_in.1), channel_id=1, source_target_pairs={{0,1},{1,0},{2,3},{3,2},{4,5},{5,4},{6,7},{7,6},{8,9},{9,8},{10,11... | collective-permute-start | bytes 98312 | tf_op jit(solution)/shard_map/ppermute | solution.py:31
  4.2 0.2 shard_map.68
  4.4 1.3 %shard_map.69 = f32[256,256]{1,0:T(8,128)S(1)} custom-call(bf16[128,64,512]{2,1,0:T(8,128)(2,1)S(1)} %copy-done, bf16[128,256]{1,0:T(8,128)(2,1)S(1)} %get-tuple-element.28.a_ref, bf16[64,256]{1,0:T(8,128)(2,1)S(1)} %get-tuple-element.21.b_ref), custom_call_target="tpu_custom_call" | custom-call | flops 4294967296 | tf_op jit(solution)/shard_map/pallas_call | solution.py:35
  5.8 0.3 collective-permute-start.1
  6.0 0.0 collective-permute-done.b1_ref
  6.0 1.4 %shard_map.70 = (f32[256,256]{1,0:T(8,128)S(1)}, bf16[256,256]{1,0:T(8,128)(2,1)S(1)}, bf16[256,256]{1,0:T(8,128)(2,1)S(1)}) custom-call(bf16[128,64,512]{2,1,0:T(8,128)(2,1)S(1)} %copy-done, bf16[128,256]{1,0:T(8,128)(2,1)S(1)} %get-tuple-element.28.a_ref, bf16[64,256]{1,0:T(8,128)(2,1)S(1)} %get-tuple-element.21.b_ref, ...), custom_call_target="tpu_custom_call" | custom-call | flops 8589934592 | tf_op jit(solution)/shard_map/pallas_call | solution.py:35
  7.4 0.0 collective-permute-done.1.in_ref
  7.4 0.2 shard_map.71
  7.7 2.6 %collective-permute-start.5 = (f16[136,256]{1,0:T(8,128)(2,1)S(1)}, f16[136,256]{1,0:T(8,128)(2,1)S(1)}, u32[]{:S(2)}, u32[]{:S(2)}) collective-permute-start(f16[136,256]{1,0:T(8,128)(2,1)S(1)} %convert_element_type.48), channel_id=1, source_target_pairs={{0,2},{1,3},{2,0},{3,1},{4,6},{5,7},{6,4},{7,5},{8,10},{9,11},{10,... | collective-permute-start | bytes 208904 | tf_op jit(solution)/shard_map/ppermute | solution.py:31
  10.3 0.0 collective-permute-done.3.c1
  10.3 0.0 collective-permute-done.4.c3
  10.3 2.7 %shard_map.72 = (f32[128,256]{1,0:T(8,128)S(1)}, f32[64,256]{1,0:T(8,128)S(1)}, f32[256,256]{1,0:T(8,128)S(1)}, f32[128,256]{1,0:T(8,128)S(1)}) custom-call(bf16[128,64,512]{2,1,0:T(8,128)(2,1)S(1)} %copy-done, bf16[128,256]{1,0:T(8,128)(2,1)S(1)} %get-tuple-element.28.a_ref, bf16[64,256]{1,0:T(8,128)(2,1)S(1)} %get-tuple-element.21.b_ref, ...), custom_call_target="tpu_custom_call" | custom-call | flops 2147483648 | tf_op jit(solution)/shard_map/pallas_call | solution.py:35
  13.0 0.0 collective-permute-done.5
  13.0 0.1 shard_map.73
  13.1 3.9 %collective-permute-start.6 = (f16[200,256]{1,0:T(8,128)(2,1)S(1)}, f16[200,256]{1,0:T(8,128)(2,1)S(1)}, u32[]{:S(2)}, u32[]{:S(2)}) collective-permute-start(f16[200,256]{1,0:T(8,128)(2,1)S(1)} %convert_element_type.50), channel_id=1, source_target_pairs={{0,24},{4,28},{8,16},{12,20},{16,8},{20,12},{24,0},{28,4},{1,25},{... | collective-permute-start | bytes 307208 | tf_op jit(solution)/shard_map/ppermute | solution.py:31
  17.0 0.4 %shard_map.74 = f32[128,256]{1,0:T(8,128)S(1)} custom-call(bf16[128,256]{1,0:T(8,128)(2,1)S(1)} %get-tuple-element.28.a_ref, bf16[64,256]{1,0:T(8,128)(2,1)S(1)} %get-tuple-element.21.b_ref, f32[256,256]{1,0:T(8,128)S(1)} %get-tuple-element.32.gc_ref, f32[128,256]{1,0:T(8,128)S(1)} %get-tuple-element.34.slab_ref), custom_call_target="tpu_custom_call" | custom-call | flops 67108864 | tf_op jit(solution)/shard_map/pallas_call | solution.py:35
  17.4 1.6 %collective-permute-start.10 = (f32[128,256]{1,0:T(8,128)S(1)}, f32[128,256]{1,0:T(8,128)S(1)}, u32[]{:S(2)}, u32[]{:S(2)}) collective-permute-start(f32[128,256]{1,0:T(8,128)S(1)} %shard_map.74), channel_id=1, source_target_pairs={{0,2},{1,3},{2,0},{3,1},{4,6},{5,7},{6,4},{7,5},{8,10},{9,11},{10,... | collective-permute-start | bytes 393224 | tf_op jit(solution)/shard_map/ppermute | solution.py:31
  19.0 1.0 %collective-permute-done.6 = f16[200,256]{1,0:T(8,128)(2,1)S(1)} collective-permute-done((f16[200,256]{1,0:T(8,128)(2,1)S(1)}, f16[200,256]{1,0:T(8,128)(2,1)S(1)}, u32[]{:S(2)}, u32[]{:S(2)}) %collective-permute-start.6) | collective-permute-done | bytes 102432 | tf_op jit(solution)/shard_map/ppermute | solution.py:31
  20.0 0.1 select_convert_fusion
  20.1 2.8 %collective-permute-start.7 = (f16[200,256]{1,0:T(8,128)(2,1)S(1)}, f16[200,256]{1,0:T(8,128)(2,1)S(1)}, u32[]{:S(2)}, u32[]{:S(2)}) collective-permute-start(f16[200,256]{1,0:T(8,128)(2,1)S(1)} %select_convert_fusion), channel_id=1, source_target_pairs={{0,12},{4,8},{8,4},{12,0},{16,28},{20,24},{24,20},{28,16},{1,13},{... | collective-permute-start | bytes 307208 | tf_op jit(solution)/shard_map/ppermute | solution.py:31
  22.9 0.2 collective-permute-start.8
  23.1 0.5 %collective-permute-start.9 = (f16[200,256]{1,0:T(8,128)(2,1)S(1)}, f16[200,256]{1,0:T(8,128)(2,1)S(1)}, u32[]{:S(2)}, u32[]{:S(2)}) collective-permute-start(f16[200,256]{1,0:T(8,128)(2,1)S(1)} %select_convert_fusion), channel_id=1, source_target_pairs={{0,4},{4,0},{8,12},{12,8},{16,20},{20,16},{24,28},{28,24},{1,5},{5... | collective-permute-start | bytes 307208 | tf_op jit(solution)/shard_map/ppermute | solution.py:31
  23.7 0.0 collective-permute-done.10
  23.7 0.1 collective-permute-start.11
  23.8 2.8 %collective-permute-done.7 = f16[200,256]{1,0:T(8,128)(2,1)S(1)} collective-permute-done((f16[200,256]{1,0:T(8,128)(2,1)S(1)}, f16[200,256]{1,0:T(8,128)(2,1)S(1)}, u32[]{:S(2)}, u32[]{:S(2)}) %collective-permute-start.7) | collective-permute-done | bytes 102432 | tf_op jit(solution)/shard_map/ppermute | solution.py:31
  26.6 1.1 %collective-permute-done.8 = f16[200,256]{1,0:T(8,128)(2,1)S(1)} collective-permute-done((f16[200,256]{1,0:T(8,128)(2,1)S(1)}, f16[200,256]{1,0:T(8,128)(2,1)S(1)}, u32[]{:S(2)}, u32[]{:S(2)}) %collective-permute-start.8) | collective-permute-done | bytes 102432 | tf_op jit(solution)/shard_map/ppermute | solution.py:31
  27.7 0.1 collective-permute-done.9
  27.8 0.1 add_add_fusion.v_ref
  27.9 0.7 %shard_map.75 = (f32[128,256]{1,0:T(8,128)}, f32[128,256]{1,0:T(8,128)}, f32[64,256]{1,0:T(8,128)}) custom-call(f32[200,256]{1,0:T(8,128)S(1)} %add_add_fusion.v_ref, f32[128,256]{1,0:T(8,128)S(1)} %add.33.pa_ref, f32[128,256]{1,0:T(8,128)S(1)} %collective-permute-done.11.in_ref), custom_call_target="tpu_custom_call" | custom-call | tf_op jit(solution)/shard_map/pallas_call | solution.py:370
  (21 shorter events, 0.1 us)
Async XLA Ops:
  0.6 3.6 %copy-start.3 = (bf16[64,256]{1,0:T(8,128)(2,1)S(1)}, bf16[64,256]{1,0:T(8,128)(2,1)}, u32[]{:S(2)}) copy-start(bf16[64,256]{1,0:T(8,128)(2,1)} %b_in.1) | copy-start | bytes 98308
  0.6 3.6 %copy-start.2 = (bf16[128,256]{1,0:T(8,128)(2,1)S(1)}, bf16[128,256]{1,0:T(8,128)(2,1)}, u32[]{:S(2)}) copy-start(bf16[128,256]{1,0:T(8,128)(2,1)} %a_in.1) | copy-start | bytes 196612
  0.7 3.8 %copy-start = (bf16[128,64,512]{2,1,0:T(8,128)(2,1)S(1)}, bf16[128,64,512]{2,1,0:T(8,128)(2,1)}, u32[]{:S(2)}) copy-start(bf16[128,64,512]{2,1,0:T(8,128)(2,1)} %x_ref.5) | copy-start | bytes 25165828
  0.7 6.7 %collective-permute-start.2 = (bf16[128,256]{1,0:T(8,128)(2,1)}, bf16[128,256]{1,0:T(8,128)(2,1)S(1)}, u32[]{:S(2)}, u32[]{:S(2)}) collective-permute-start(bf16[128,256]{1,0:T(8,128)(2,1)} %c0.1), channel_id=1, source_target_pairs={{0,2},{1,3},{2,0},{3,1},{4,6},{5,7},{6,4},{7,5},{8,10},{9,11},{10,... | collective-permute-start | bytes 196616 | tf_op jit(solution)/shard_map/ppermute | solution.py:31
  3.7 6.6 %collective-permute-start.3 = (bf16[128,256]{1,0:T(8,128)(2,1)}, bf16[128,256]{1,0:T(8,128)(2,1)S(1)}, u32[]{:S(2)}, u32[]{:S(2)}) collective-permute-start(bf16[128,256]{1,0:T(8,128)(2,1)} %c0.1), channel_id=1, source_target_pairs={{0,1},{1,0},{2,3},{3,2},{4,5},{5,4},{6,7},{7,6},{8,9},{9,8},{10,11... | collective-permute-start | bytes 196616 | tf_op jit(solution)/shard_map/ppermute | solution.py:31
  3.7 6.6 %collective-permute-start.4 = (bf16[128,256]{1,0:T(8,128)(2,1)}, bf16[128,256]{1,0:T(8,128)(2,1)S(1)}, u32[]{:S(2)}, u32[]{:S(2)}) collective-permute-start(bf16[128,256]{1,0:T(8,128)(2,1)} %c0.1), channel_id=1, source_target_pairs={{0,3},{1,2},{2,1},{3,0},{4,7},{5,6},{6,5},{7,4},{8,11},{9,10},{10,... | collective-permute-start | bytes 196616 | tf_op jit(solution)/shard_map/ppermute | solution.py:31
  3.9 2.1 %collective-permute-start = (bf16[64,256]{1,0:T(8,128)(2,1)}, bf16[64,256]{1,0:T(8,128)(2,1)S(1)}, u32[]{:S(2)}, u32[]{:S(2)}) collective-permute-start(bf16[64,256]{1,0:T(8,128)(2,1)} %b_in.1), channel_id=1, source_target_pairs={{0,1},{1,0},{2,3},{3,2},{4,5},{5,4},{6,7},{7,6},{8,9},{9,8},{10,11... | collective-permute-start | bytes 98312 | tf_op jit(solution)/shard_map/ppermute | solution.py:31
  5.8 1.6 %collective-permute-start.1 = (f32[256,256]{1,0:T(8,128)S(1)}, f32[256,256]{1,0:T(8,128)S(1)}, u32[]{:S(2)}, u32[]{:S(2)}) collective-permute-start(f32[256,256]{1,0:T(8,128)S(1)} %shard_map.69), channel_id=1, source_target_pairs={{0,1},{1,0},{2,3},{3,2},{4,5},{5,4},{6,7},{7,6},{8,9},{9,8},{10,11... | collective-permute-start | bytes 786440 | tf_op jit(solution)/shard_map/ppermute | solution.py:31
  6.0 4.3 %copy-start.1 = (bf16[128,256]{1,0:T(8,128)(2,1)S(1)}, bf16[128,256]{1,0:T(8,128)(2,1)}, u32[]{:S(2)}) copy-start(bf16[128,256]{1,0:T(8,128)(2,1)} %c0.1) | copy-start | bytes 196612
  7.7 5.3 %collective-permute-start.5 = (f16[136,256]{1,0:T(8,128)(2,1)S(1)}, f16[136,256]{1,0:T(8,128)(2,1)S(1)}, u32[]{:S(2)}, u32[]{:S(2)}) collective-permute-start(f16[136,256]{1,0:T(8,128)(2,1)S(1)} %convert_element_type.48), channel_id=1, source_target_pairs={{0,2},{1,3},{2,0},{3,1},{4,6},{5,7},{6,4},{7,5},{8,10},{9,11},{10,... | collective-permute-start | bytes 208904 | tf_op jit(solution)/shard_map/ppermute | solution.py:31
  13.1 6.9 %collective-permute-start.6 = (f16[200,256]{1,0:T(8,128)(2,1)S(1)}, f16[200,256]{1,0:T(8,128)(2,1)S(1)}, u32[]{:S(2)}, u32[]{:S(2)}) collective-permute-start(f16[200,256]{1,0:T(8,128)(2,1)S(1)} %convert_element_type.50), channel_id=1, source_target_pairs={{0,24},{4,28},{8,16},{12,20},{16,8},{20,12},{24,0},{28,4},{1,25},{... | collective-permute-start | bytes 307208 | tf_op jit(solution)/shard_map/ppermute | solution.py:31
  17.4 6.3 %collective-permute-start.10 = (f32[128,256]{1,0:T(8,128)S(1)}, f32[128,256]{1,0:T(8,128)S(1)}, u32[]{:S(2)}, u32[]{:S(2)}) collective-permute-start(f32[128,256]{1,0:T(8,128)S(1)} %shard_map.74), channel_id=1, source_target_pairs={{0,2},{1,3},{2,0},{3,1},{4,6},{5,7},{6,4},{7,5},{8,10},{9,11},{10,... | collective-permute-start | bytes 393224 | tf_op jit(solution)/shard_map/ppermute | solution.py:31
  20.1 6.5 %collective-permute-start.7 = (f16[200,256]{1,0:T(8,128)(2,1)S(1)}, f16[200,256]{1,0:T(8,128)(2,1)S(1)}, u32[]{:S(2)}, u32[]{:S(2)}) collective-permute-start(f16[200,256]{1,0:T(8,128)(2,1)S(1)} %select_convert_fusion), channel_id=1, source_target_pairs={{0,12},{4,8},{8,4},{12,0},{16,28},{20,24},{24,20},{28,16},{1,13},{... | collective-permute-start | bytes 307208 | tf_op jit(solution)/shard_map/ppermute | solution.py:31
  22.9 4.8 %collective-permute-start.8 = (f16[200,256]{1,0:T(8,128)(2,1)S(1)}, f16[200,256]{1,0:T(8,128)(2,1)S(1)}, u32[]{:S(2)}, u32[]{:S(2)}) collective-permute-start(f16[200,256]{1,0:T(8,128)(2,1)S(1)} %select_convert_fusion), channel_id=1, source_target_pairs={{0,8},{4,12},{8,0},{12,4},{16,24},{20,28},{24,16},{28,20},{1,9},{5... | collective-permute-start | bytes 307208 | tf_op jit(solution)/shard_map/ppermute | solution.py:31
  23.1 4.7 %collective-permute-start.9 = (f16[200,256]{1,0:T(8,128)(2,1)S(1)}, f16[200,256]{1,0:T(8,128)(2,1)S(1)}, u32[]{:S(2)}, u32[]{:S(2)}) collective-permute-start(f16[200,256]{1,0:T(8,128)(2,1)S(1)} %select_convert_fusion), channel_id=1, source_target_pairs={{0,4},{4,0},{8,12},{12,8},{16,20},{20,16},{24,28},{28,24},{1,5},{5... | collective-permute-start | bytes 307208 | tf_op jit(solution)/shard_map/ppermute | solution.py:31
  23.7 4.2 %collective-permute-start.11 = (f32[128,256]{1,0:T(8,128)S(1)}, f32[128,256]{1,0:T(8,128)S(1)}, u32[]{:S(2)}, u32[]{:S(2)}) collective-permute-start(f32[128,256]{1,0:T(8,128)S(1)} %add.33.pa_ref), channel_id=1, source_target_pairs={{0,1},{1,0},{2,3},{3,2},{4,5},{5,4},{6,7},{7,6},{8,9},{9,8},{10,11... | collective-permute-start | bytes 393224 | tf_op jit(solution)/shard_map/ppermute | solution.py:31

commit v9 on v7

--- a/solution.py
+++ b/solution.py
@@ -154,9 +154,13 @@
     m_ref[at:] = jnp.broadcast_to(e, (m_ref.shape[0] - at, e.shape[1]))
 
 
-def meet(to_height, g_ref, in_ref, c2_ref, hi_ref, lo_ref, keep_ref, m_ref):
+def partner_terms(c2_ref, hi_ref, lo_ref, out_ref):
+    out_ref[...] = through(c2_ref, hi_ref, lo_ref)
+
+
+def meet(to_height, g_ref, in_ref, gram_ref, keep_ref, m_ref):
     h_own = keep_ref.shape[0]
-    write_message(m_ref, (through(c2_ref, hi_ref, lo_ref) - (g_ref[h_own:] + in_ref[h_own:])) * to_height)
+    write_message(m_ref, (gram_ref[...] - (g_ref[h_own:] + in_ref[h_own:])) * to_height)
     keep_ref[...] = g_ref[0:h_own] + in_ref[0:h_own]
 
 
@@ -215,10 +219,11 @@
         (slab, after(a, g_away), b, b1, ga),
         4 * work,
     )
+    (gram_part,) = call(partner_terms, block, (c2, hi, lo), work // 32)
     slab_part, away = call(
         functools.partial(meet, scales[1]),
         block + [((h_own + TAIL, rank), F32)],
-        (g_keep, g_in, c2, hi, lo),
+        (g_keep, g_in, gram_part),
         work // 32,
     )
     away = away.astype(F16)

time: 28.9 us -> 28.9 us (level)
    pallas_call x8 -> x9, Pallas kernels: 6.23 us -> 6.25 us  [call(): pl.pallas_call(body, in_specs=[WHOLE] * len(args), out_specs=[WHOLE] * le...]
  transfers between devices with their start and end apart: 12 -> 12, of which waited for: 3 -> 4; matrix products, arithmetic and copies ran while one was open for 1% -> 1% of each run, Pallas kernels for 22% -> 21%
where the time goes in v9:
time: 28.9 us; the launch traced here: 28.8 us
  starting transfers between devices  15.5 us (54%)
  Pallas kernels  6.99 us (24%)
  waiting for transfers between devices  5.16 us (18%)
  between operations  0.81 us (3%)
    ppermute x12, starting transfers between devices, swap(): lax.ppermute(x, axis, [(i, i ^ bit) for i in range(lax.axis_size(axis))])  15.5 us
    pallas_call x9, Pallas kernels, call(): pl.pallas_call(body, in_specs=[WHOLE] * len(args), out_specs=[WHOLE] * le...  6.25 us
    ppermute x12, waiting for transfers between devices, swap(): lax.ppermute(x, axis, [(i, i ^ bit) for i in range(lax.axis_size(axis))])  5.16 us
    pallas_call x1, Pallas kernels, per_device(): pl.pallas_call(finish, in_specs=[WHOLE] * 3, out_specs=[WHOLE] * 3, out_s...  0.74 us
  transfers between devices with their start and end apart: 12, of which 4 were waited for; matrix products, arithmetic and copies ran while one was open for 1% of the time, Pallas kernels for 21%

profile of v9, /device:TPU:0, one launch (start us, length us, event | category | flops | bytes accessed | tf_op | source)
XLA Modules:
  0.0 28.8 jit_solution(15627415091467048764)
XLA Ops:
  0.7 3.0 %collective-permute-start.2 = (bf16[128,256]{1,0:T(8,128)(2,1)}, bf16[128,256]{1,0:T(8,128)(2,1)S(1)}, u32[]{:S(2)}, u32[]{:S(2)}) collective-permute-start(bf16[128,256]{1,0:T(8,128)(2,1)} %c0.1), channel_id=1, source_target_pairs={{0,2},{1,3},{2,0},{3,1},{4,6},{5,7},{6,4},{7,5},{8,10},{9,11},{10,... | collective-permute-start | bytes 196616 | tf_op jit(solution)/shard_map/ppermute | solution.py:31
  3.7 0.0 collective-permute-start.3
  3.7 0.2 collective-permute-start.4
  3.9 0.3 %collective-permute-start = (bf16[64,256]{1,0:T(8,128)(2,1)}, bf16[64,256]{1,0:T(8,128)(2,1)S(1)}, u32[]{:S(2)}, u32[]{:S(2)}) collective-permute-start(bf16[64,256]{1,0:T(8,128)(2,1)} %b_in.1), channel_id=1, source_target_pairs={{0,1},{1,0},{2,3},{3,2},{4,5},{5,4},{6,7},{7,6},{8,9},{9,8},{10,11... | collective-permute-start | bytes 98312 | tf_op jit(solution)/shard_map/ppermute | solution.py:31
  4.2 0.2 shard_map.68
  4.4 1.3 %shard_map.69 = f32[256,256]{1,0:T(8,128)S(1)} custom-call(bf16[128,64,512]{2,1,0:T(8,128)(2,1)S(1)} %copy-done, bf16[128,256]{1,0:T(8,128)(2,1)S(1)} %get-tuple-element.28.a_ref, bf16[64,256]{1,0:T(8,128)(2,1)S(1)} %get-tuple-element.21.b_ref), custom_call_target="tpu_custom_call" | custom-call | flops 4294967296 | tf_op jit(solution)/shard_map/pallas_call | solution.py:35
  5.8 0.3 collective-permute-start.1
  6.0 0.0 collective-permute-done.b1_ref
  6.0 1.4 %shard_map.70 = (f32[256,256]{1,0:T(8,128)S(1)}, bf16[256,256]{1,0:T(8,128)(2,1)S(1)}, bf16[256,256]{1,0:T(8,128)(2,1)S(1)}) custom-call(bf16[128,64,512]{2,1,0:T(8,128)(2,1)S(1)} %copy-done, bf16[128,256]{1,0:T(8,128)(2,1)S(1)} %get-tuple-element.28.a_ref, bf16[64,256]{1,0:T(8,128)(2,1)S(1)} %get-tuple-element.21.b_ref, ...), custom_call_target="tpu_custom_call" | custom-call | flops 8589934592 | tf_op jit(solution)/shard_map/pallas_call | solution.py:35
  7.4 0.0 collective-permute-done.2.c2_ref.c2
  7.4 0.2 shard_map.71.gram_ref
  7.6 0.0 collective-permute-done.1.in_ref
  7.6 0.1 shard_map.72
  7.7 2.5 %collective-permute-start.5 = (f16[136,256]{1,0:T(8,128)(2,1)S(1)}, f16[136,256]{1,0:T(8,128)(2,1)S(1)}, u32[]{:S(2)}, u32[]{:S(2)}) collective-permute-start(f16[136,256]{1,0:T(8,128)(2,1)S(1)} %convert_element_type.48), channel_id=1, source_target_pairs={{0,2},{1,3},{2,0},{3,1},{4,6},{5,7},{6,4},{7,5},{8,10},{9,11},{10,... | collective-permute-start | bytes 208904 | tf_op jit(solution)/shard_map/ppermute | solution.py:31
  10.2 0.0 collective-permute-done.3.c1
  10.2 2.7 %shard_map.73 = (f32[128,256]{1,0:T(8,128)S(1)}, f32[64,256]{1,0:T(8,128)S(1)}, f32[256,256]{1,0:T(8,128)S(1)}, f32[128,256]{1,0:T(8,128)S(1)}) custom-call(bf16[128,64,512]{2,1,0:T(8,128)(2,1)S(1)} %copy-done, bf16[128,256]{1,0:T(8,128)(2,1)S(1)} %get-tuple-element.28.a_ref, bf16[64,256]{1,0:T(8,128)(2,1)S(1)} %get-tuple-element.21.b_ref, ...), custom_call_target="tpu_custom_call" | custom-call | flops 2147483648 | tf_op jit(solution)/shard_map/pallas_call | solution.py:35
  12.9 0.2 collective-permute-done.5
  13.0 0.1 shard_map.74
  13.1 2.8 %collective-permute-start.6 = (f16[200,256]{1,0:T(8,128)(2,1)S(1)}, f16[200,256]{1,0:T(8,128)(2,1)S(1)}, u32[]{:S(2)}, u32[]{:S(2)}) collective-permute-start(f16[200,256]{1,0:T(8,128)(2,1)S(1)} %convert_element_type.50), channel_id=1, source_target_pairs={{0,12},{4,8},{8,4},{12,0},{16,28},{20,24},{24,20},{28,16},{1,13},{... | collective-permute-start | bytes 307208 | tf_op jit(solution)/shard_map/ppermute | solution.py:31
  15.9 0.4 %collective-permute-start.7 = (f16[200,256]{1,0:T(8,128)(2,1)S(1)}, f16[200,256]{1,0:T(8,128)(2,1)S(1)}, u32[]{:S(2)}, u32[]{:S(2)}) collective-permute-start(f16[200,256]{1,0:T(8,128)(2,1)S(1)} %convert_element_type.50), channel_id=1, source_target_pairs={{0,8},{4,12},{8,0},{12,4},{16,24},{20,28},{24,16},{28,20},{1,9},{5... | collective-permute-start | bytes 307208 | tf_op jit(solution)/shard_map/ppermute | solution.py:31
  16.4 0.3 %collective-permute-start.8 = (f16[200,256]{1,0:T(8,128)(2,1)S(1)}, f16[200,256]{1,0:T(8,128)(2,1)S(1)}, u32[]{:S(2)}, u32[]{:S(2)}) collective-permute-start(f16[200,256]{1,0:T(8,128)(2,1)S(1)} %convert_element_type.50), channel_id=1, source_target_pairs={{0,4},{4,0},{8,12},{12,8},{16,20},{20,16},{24,28},{28,24},{1,5},{5... | collective-permute-start | bytes 307208 | tf_op jit(solution)/shard_map/ppermute | solution.py:31
  16.7 0.4 %shard_map.75 = f32[128,256]{1,0:T(8,128)S(1)} custom-call(bf16[128,256]{1,0:T(8,128)(2,1)S(1)} %get-tuple-element.28.a_ref, bf16[64,256]{1,0:T(8,128)(2,1)S(1)} %get-tuple-element.21.b_ref, f32[256,256]{1,0:T(8,128)S(1)} %get-tuple-element.32.gc_ref, f32[128,256]{1,0:T(8,128)S(1)} %get-tuple-element.34.slab_ref), custom_call_target="tpu_custom_call" | custom-call | flops 67108864 | tf_op jit(solution)/shard_map/pallas_call | solution.py:35
  17.1 1.8 %collective-permute-start.10 = (f32[128,256]{1,0:T(8,128)S(1)}, f32[128,256]{1,0:T(8,128)S(1)}, u32[]{:S(2)}, u32[]{:S(2)}) collective-permute-start(f32[128,256]{1,0:T(8,128)S(1)} %shard_map.75), channel_id=1, source_target_pairs={{0,2},{1,3},{2,0},{3,1},{4,6},{5,7},{6,4},{7,5},{8,10},{9,11},{10,... | collective-permute-start | bytes 393224 | tf_op jit(solution)/shard_map/ppermute | solution.py:31
  18.9 0.9 %collective-permute-done.6 = f16[200,256]{1,0:T(8,128)(2,1)S(1)} collective-permute-done((f16[200,256]{1,0:T(8,128)(2,1)S(1)}, f16[200,256]{1,0:T(8,128)(2,1)S(1)}, u32[]{:S(2)}, u32[]{:S(2)}) %collective-permute-start.6) | collective-permute-done | bytes 102432 | tf_op jit(solution)/shard_map/ppermute | solution.py:31
  19.8 1.4 %collective-permute-done.7 = f16[200,256]{1,0:T(8,128)(2,1)S(1)} collective-permute-done((f16[200,256]{1,0:T(8,128)(2,1)S(1)}, f16[200,256]{1,0:T(8,128)(2,1)S(1)}, u32[]{:S(2)}, u32[]{:S(2)}) %collective-permute-start.7) | collective-permute-done | bytes 102432 | tf_op jit(solution)/shard_map/ppermute | solution.py:31
  21.2 0.0 collective-permute-done.8
  21.3 0.1 select_convert_fusion
  21.4 3.8 %collective-permute-start.9 = (f16[200,256]{1,0:T(8,128)(2,1)S(1)}, f16[200,256]{1,0:T(8,128)(2,1)S(1)}, u32[]{:S(2)}, u32[]{:S(2)}) collective-permute-start(f16[200,256]{1,0:T(8,128)(2,1)S(1)} %select_convert_fusion), channel_id=1, source_target_pairs={{0,24},{4,28},{8,16},{12,20},{16,8},{20,12},{24,0},{28,4},{1,25},{... | collective-permute-start | bytes 307208 | tf_op jit(solution)/shard_map/ppermute | solution.py:31
  25.2 0.1 collective-permute-start.11
  25.3 2.7 %collective-permute-done.9 = f16[200,256]{1,0:T(8,128)(2,1)S(1)} collective-permute-done((f16[200,256]{1,0:T(8,128)(2,1)S(1)}, f16[200,256]{1,0:T(8,128)(2,1)S(1)}, u32[]{:S(2)}, u32[]{:S(2)}) %collective-permute-start.9) | collective-permute-done | bytes 102432 | tf_op jit(solution)/shard_map/ppermute | solution.py:31
  28.0 0.0 collective-permute-done.11.in_ref
  28.0 0.7 %shard_map.76 = (f32[128,256]{1,0:T(8,128)}, f32[128,256]{1,0:T(8,128)}, f32[64,256]{1,0:T(8,128)}) custom-call(f32[200,256]{1,0:T(8,128)S(1)} %multiply_add_fusion.v_ref, f32[128,256]{1,0:T(8,128)S(1)} %add.33.pa_ref, f32[128,256]{1,0:T(8,128)S(1)} %collective-permute-done.11.in_ref), custom_call_target="tpu_custom_call" | custom-call | tf_op jit(solution)/shard_map/pallas_call | solution.py:375
  (20 shorter events, 0.2 us)
Async XLA Ops:
  0.6 3.6 %copy-start.3 = (bf16[64,256]{1,0:T(8,128)(2,1)S(1)}, bf16[64,256]{1,0:T(8,128)(2,1)}, u32[]{:S(2)}) copy-start(bf16[64,256]{1,0:T(8,128)(2,1)} %b_in.1) | copy-start | bytes 98308
  0.6 3.6 %copy-start.2 = (bf16[128,256]{1,0:T(8,128)(2,1)S(1)}, bf16[128,256]{1,0:T(8,128)(2,1)}, u32[]{:S(2)}) copy-start(bf16[128,256]{1,0:T(8,128)(2,1)} %a_in.1) | copy-start | bytes 196612
  0.7 3.8 %copy-start = (bf16[128,64,512]{2,1,0:T(8,128)(2,1)S(1)}, bf16[128,64,512]{2,1,0:T(8,128)(2,1)}, u32[]{:S(2)}) copy-start(bf16[128,64,512]{2,1,0:T(8,128)(2,1)} %x_ref.5) | copy-start | bytes 25165828
  0.7 6.7 %collective-permute-start.2 = (bf16[128,256]{1,0:T(8,128)(2,1)}, bf16[128,256]{1,0:T(8,128)(2,1)S(1)}, u32[]{:S(2)}, u32[]{:S(2)}) collective-permute-start(bf16[128,256]{1,0:T(8,128)(2,1)} %c0.1), channel_id=1, source_target_pairs={{0,2},{1,3},{2,0},{3,1},{4,6},{5,7},{6,4},{7,5},{8,10},{9,11},{10,... | collective-permute-start | bytes 196616 | tf_op jit(solution)/shard_map/ppermute | solution.py:31
  3.7 6.5 %collective-permute-start.3 = (bf16[128,256]{1,0:T(8,128)(2,1)}, bf16[128,256]{1,0:T(8,128)(2,1)S(1)}, u32[]{:S(2)}, u32[]{:S(2)}) collective-permute-start(bf16[128,256]{1,0:T(8,128)(2,1)} %c0.1), channel_id=1, source_target_pairs={{0,1},{1,0},{2,3},{3,2},{4,5},{5,4},{6,7},{7,6},{8,9},{9,8},{10,11... | collective-permute-start | bytes 196616 | tf_op jit(solution)/shard_map/ppermute | solution.py:31
  3.7 6.5 %collective-permute-start.4 = (bf16[128,256]{1,0:T(8,128)(2,1)}, bf16[128,256]{1,0:T(8,128)(2,1)S(1)}, u32[]{:S(2)}, u32[]{:S(2)}) collective-permute-start(bf16[128,256]{1,0:T(8,128)(2,1)} %c0.1), channel_id=1, source_target_pairs={{0,3},{1,2},{2,1},{3,0},{4,7},{5,6},{6,5},{7,4},{8,11},{9,10},{10,... | collective-permute-start | bytes 196616 | tf_op jit(solution)/shard_map/ppermute | solution.py:31
  3.9 2.1 %collective-permute-start = (bf16[64,256]{1,0:T(8,128)(2,1)}, bf16[64,256]{1,0:T(8,128)(2,1)S(1)}, u32[]{:S(2)}, u32[]{:S(2)}) collective-permute-start(bf16[64,256]{1,0:T(8,128)(2,1)} %b_in.1), channel_id=1, source_target_pairs={{0,1},{1,0},{2,3},{3,2},{4,5},{5,4},{6,7},{7,6},{8,9},{9,8},{10,11... | collective-permute-start | bytes 98312 | tf_op jit(solution)/shard_map/ppermute | solution.py:31
  5.8 1.8 %collective-permute-start.1 = (f32[256,256]{1,0:T(8,128)S(1)}, f32[256,256]{1,0:T(8,128)S(1)}, u32[]{:S(2)}, u32[]{:S(2)}) collective-permute-start(f32[256,256]{1,0:T(8,128)S(1)} %shard_map.69), channel_id=1, source_target_pairs={{0,1},{1,0},{2,3},{3,2},{4,5},{5,4},{6,7},{7,6},{8,9},{9,8},{10,11... | collective-permute-start | bytes 786440 | tf_op jit(solution)/shard_map/ppermute | solution.py:31
  6.0 4.2 %copy-start.1 = (bf16[128,256]{1,0:T(8,128)(2,1)S(1)}, bf16[128,256]{1,0:T(8,128)(2,1)}, u32[]{:S(2)}) copy-start(bf16[128,256]{1,0:T(8,128)(2,1)} %c0.1) | copy-start | bytes 196612
  7.7 5.3 %collective-permute-start.5 = (f16[136,256]{1,0:T(8,128)(2,1)S(1)}, f16[136,256]{1,0:T(8,128)(2,1)S(1)}, u32[]{:S(2)}, u32[]{:S(2)}) collective-permute-start(f16[136,256]{1,0:T(8,128)(2,1)S(1)} %convert_element_type.48), channel_id=1, source_target_pairs={{0,2},{1,3},{2,0},{3,1},{4,6},{5,7},{6,4},{7,5},{8,10},{9,11},{10,... | collective-permute-start | bytes 208904 | tf_op jit(solution)/shard_map/ppermute | solution.py:31
  13.1 6.7 %collective-permute-start.6 = (f16[200,256]{1,0:T(8,128)(2,1)S(1)}, f16[200,256]{1,0:T(8,128)(2,1)S(1)}, u32[]{:S(2)}, u32[]{:S(2)}) collective-permute-start(f16[200,256]{1,0:T(8,128)(2,1)S(1)} %convert_element_type.50), channel_id=1, source_target_pairs={{0,12},{4,8},{8,4},{12,0},{16,28},{20,24},{24,20},{28,16},{1,13},{... | collective-permute-start | bytes 307208 | tf_op jit(solution)/shard_map/ppermute | solution.py:31
  15.9 5.3 %collective-permute-start.7 = (f16[200,256]{1,0:T(8,128)(2,1)S(1)}, f16[200,256]{1,0:T(8,128)(2,1)S(1)}, u32[]{:S(2)}, u32[]{:S(2)}) collective-permute-start(f16[200,256]{1,0:T(8,128)(2,1)S(1)} %convert_element_type.50), channel_id=1, source_target_pairs={{0,8},{4,12},{8,0},{12,4},{16,24},{20,28},{24,16},{28,20},{1,9},{5... | collective-permute-start | bytes 307208 | tf_op jit(solution)/shard_map/ppermute | solution.py:31
  16.4 4.9 %collective-permute-start.8 = (f16[200,256]{1,0:T(8,128)(2,1)S(1)}, f16[200,256]{1,0:T(8,128)(2,1)S(1)}, u32[]{:S(2)}, u32[]{:S(2)}) collective-permute-start(f16[200,256]{1,0:T(8,128)(2,1)S(1)} %convert_element_type.50), channel_id=1, source_target_pairs={{0,4},{4,0},{8,12},{12,8},{16,20},{20,16},{24,28},{28,24},{1,5},{5... | collective-permute-start | bytes 307208 | tf_op jit(solution)/shard_map/ppermute | solution.py:31
  17.1 8.1 %collective-permute-start.10 = (f32[128,256]{1,0:T(8,128)S(1)}, f32[128,256]{1,0:T(8,128)S(1)}, u32[]{:S(2)}, u32[]{:S(2)}) collective-permute-start(f32[128,256]{1,0:T(8,128)S(1)} %shard_map.75), channel_id=1, source_target_pairs={{0,2},{1,3},{2,0},{3,1},{4,6},{5,7},{6,4},{7,5},{8,10},{9,11},{10,... | collective-permute-start | bytes 393224 | tf_op jit(solution)/shard_map/ppermute | solution.py:31
  21.4 6.6 %collective-permute-start.9 = (f16[200,256]{1,0:T(8,128)(2,1)S(1)}, f16[200,256]{1,0:T(8,128)(2,1)S(1)}, u32[]{:S(2)}, u32[]{:S(2)}) collective-permute-start(f16[200,256]{1,0:T(8,128)(2,1)S(1)} %select_convert_fusion), channel_id=1, source_target_pairs={{0,24},{4,28},{8,16},{12,20},{16,8},{20,12},{24,0},{28,4},{1,25},{... | collective-permute-start | bytes 307208 | tf_op jit(solution)/shard_map/ppermute | solution.py:31
  25.2 2.8 %collective-permute-start.11 = (f32[128,256]{1,0:T(8,128)S(1)}, f32[128,256]{1,0:T(8,128)S(1)}, u32[]{:S(2)}, u32[]{:S(2)}) collective-permute-start(f32[128,256]{1,0:T(8,128)S(1)} %add.33.pa_ref), channel_id=1, source_target_pairs={{0,1},{1,0},{2,3},{3,2},{4,5},{5,4},{6,7},{7,6},{8,9},{9,8},{10,11... | collective-permute-start | bytes 393224 | tf_op jit(solution)/shard_map/ppermute | solution.py:31

commit v10 on v7

--- a/solution.py
+++ b/solution.py
@@ -178,7 +178,7 @@
     r_rows = a_ref.shape[0]
     h_own = c0.shape[0]
     me = lax.axis_index("src")
-    for o, part in enumerate((c0, c1, c2, c3)):
+    for o, part in zip((0, 3, 2, 1), (c0, c1, c2, c3)):
         heights[pl.ds(pl.multiple_of((me ^ o) * h_own, h_own), h_own)] = part[...]
     x = x_ref[...].reshape(r_rows * s_rows, x_ref.shape[2])
     proj = jnp.dot(x, heights[...], preferred_element_type=F32).reshape(r_rows, s_rows, rank)
@@ -226,7 +226,7 @@
     pa, ps, gc, keep = call(
         functools.partial(project_four, scales[1], scales[2]),
         [((r_rows, rank), F32), ((s_rows, rank), F32), ((rank, rank), F32)] + block,
-        (slab, after(a, away), b, ga, slab_part, hi, lo, height_factor, c1, c2, c3),
+        (slab, after(a, away), b, ga, slab_part, hi, lo, height_factor, c3, c2, c1),
         work,
         scratch=[pltpu.VMEM((width, rank), BF16)],
     )

time: 28.9 us -> 28.9 us (level)
  no operation moved by 1% of the time
where the time goes in v10:
time: 28.9 us; the launch traced here: 28.7 us
  starting transfers between devices  15.7 us (54%)
  Pallas kernels  6.97 us (24%)
  waiting for transfers between devices  5.03 us (17%)
  between operations  0.8 us (3%)
    ppermute x12, starting transfers between devices, swap(): lax.ppermute(x, axis, [(i, i ^ bit) for i in range(lax.axis_size(axis))])  15.7 us
    pallas_call x8, Pallas kernels, call(): pl.pallas_call(body, in_specs=[WHOLE] * len(args), out_specs=[WHOLE] * le...  6.23 us
    ppermute x12, waiting for transfers between devices, swap(): lax.ppermute(x, axis, [(i, i ^ bit) for i in range(lax.axis_size(axis))])  5.03 us
    pallas_call x1, Pallas kernels, per_device(): pl.pallas_call(finish, in_specs=[WHOLE] * 3, out_specs=[WHOLE] * 3, out_s...  0.74 us
  transfers between devices with their start and end apart: 12, of which 3 were waited for; matrix products, arithmetic and copies ran while one was open for 1% of the time, Pallas kernels for 22%

profile of v10, /device:TPU:0, one launch (start us, length us, event | category | flops | bytes accessed | tf_op | source)
XLA Modules:
  0.0 28.7 jit_solution(12472046385485713557)
XLA Ops:
  0.7 3.0 %collective-permute-start.2 = (bf16[128,256]{1,0:T(8,128)(2,1)}, bf16[128,256]{1,0:T(8,128)(2,1)S(1)}, u32[]{:S(2)}, u32[]{:S(2)}) collective-permute-start(bf16[128,256]{1,0:T(8,128)(2,1)} %c0.1), channel_id=1, source_target_pairs={{0,2},{1,3},{2,0},{3,1},{4,6},{5,7},{6,4},{7,5},{8,10},{9,11},{10,... | collective-permute-start | bytes 196616 | tf_op jit(solution)/shard_map/ppermute | solution.py:31
  3.7 0.0 collective-permute-start.3
  3.7 0.2 collective-permute-start.4
  3.9 0.3 %collective-permute-start = (bf16[64,256]{1,0:T(8,128)(2,1)}, bf16[64,256]{1,0:T(8,128)(2,1)S(1)}, u32[]{:S(2)}, u32[]{:S(2)}) collective-permute-start(bf16[64,256]{1,0:T(8,128)(2,1)} %b_in.1), channel_id=1, source_target_pairs={{0,1},{1,0},{2,3},{3,2},{4,5},{5,4},{6,7},{7,6},{8,9},{9,8},{10,11... | collective-permute-start | bytes 98312 | tf_op jit(solution)/shard_map/ppermute | solution.py:31
  4.2 0.2 shard_map.68
  4.4 1.3 %shard_map.69 = f32[256,256]{1,0:T(8,128)S(1)} custom-call(bf16[128,64,512]{2,1,0:T(8,128)(2,1)S(1)} %copy-done, bf16[128,256]{1,0:T(8,128)(2,1)S(1)} %get-tuple-element.28.a_ref, bf16[64,256]{1,0:T(8,128)(2,1)S(1)} %get-tuple-element.21.b_ref), custom_call_target="tpu_custom_call" | custom-call | flops 4294967296 | tf_op jit(solution)/shard_map/pallas_call | solution.py:35
  5.8 0.2 collective-permute-start.1
  6.0 0.0 collective-permute-done.b1_ref
  6.0 1.3 %shard_map.70 = (f32[256,256]{1,0:T(8,128)S(1)}, bf16[256,256]{1,0:T(8,128)(2,1)S(1)}, bf16[256,256]{1,0:T(8,128)(2,1)S(1)}) custom-call(bf16[128,64,512]{2,1,0:T(8,128)(2,1)S(1)} %copy-done, bf16[128,256]{1,0:T(8,128)(2,1)S(1)} %get-tuple-element.28.a_ref, bf16[64,256]{1,0:T(8,128)(2,1)S(1)} %get-tuple-element.21.b_ref, ...), custom_call_target="tpu_custom_call" | custom-call | flops 8589934592 | tf_op jit(solution)/shard_map/pallas_call | solution.py:35
  7.4 0.0 collective-permute-done.2.c2_ref.c2
  7.4 0.0 collective-permute-done.1.in_ref
  7.4 0.2 shard_map.71
  7.6 2.6 %collective-permute-start.5 = (f16[136,256]{1,0:T(8,128)(2,1)S(1)}, f16[136,256]{1,0:T(8,128)(2,1)S(1)}, u32[]{:S(2)}, u32[]{:S(2)}) collective-permute-start(f16[136,256]{1,0:T(8,128)(2,1)S(1)} %convert_element_type.48), channel_id=1, source_target_pairs={{0,2},{1,3},{2,0},{3,1},{4,6},{5,7},{6,4},{7,5},{8,10},{9,11},{10,... | collective-permute-start | bytes 208904 | tf_op jit(solution)/shard_map/ppermute | solution.py:31
  10.3 0.0 collective-permute-done.3.c1
  10.3 0.0 collective-permute-done.4.c3
  10.3 2.7 %shard_map.72 = (f32[128,256]{1,0:T(8,128)S(1)}, f32[64,256]{1,0:T(8,128)S(1)}, f32[256,256]{1,0:T(8,128)S(1)}, f32[128,256]{1,0:T(8,128)S(1)}) custom-call(bf16[128,64,512]{2,1,0:T(8,128)(2,1)S(1)} %copy-done, bf16[128,256]{1,0:T(8,128)(2,1)S(1)} %get-tuple-element.28.a_ref, bf16[64,256]{1,0:T(8,128)(2,1)S(1)} %get-tuple-element.21.b_ref, ...), custom_call_target="tpu_custom_call" | custom-call | flops 2147483648 | tf_op jit(solution)/shard_map/pallas_call | solution.py:35
  13.0 0.0 collective-permute-done.5
  13.0 0.1 shard_map.73
  13.1 2.8 %collective-permute-start.6 = (f16[200,256]{1,0:T(8,128)(2,1)S(1)}, f16[200,256]{1,0:T(8,128)(2,1)S(1)}, u32[]{:S(2)}, u32[]{:S(2)}) collective-permute-start(f16[200,256]{1,0:T(8,128)(2,1)S(1)} %convert_element_type.50), channel_id=1, source_target_pairs={{0,12},{4,8},{8,4},{12,0},{16,28},{20,24},{24,20},{28,16},{1,13},{... | collective-permute-start | bytes 307208 | tf_op jit(solution)/shard_map/ppermute | solution.py:31
  15.9 0.4 %collective-permute-start.7 = (f16[200,256]{1,0:T(8,128)(2,1)S(1)}, f16[200,256]{1,0:T(8,128)(2,1)S(1)}, u32[]{:S(2)}, u32[]{:S(2)}) collective-permute-start(f16[200,256]{1,0:T(8,128)(2,1)S(1)} %convert_element_type.50), channel_id=1, source_target_pairs={{0,8},{4,12},{8,0},{12,4},{16,24},{20,28},{24,16},{28,20},{1,9},{5... | collective-permute-start | bytes 307208 | tf_op jit(solution)/shard_map/ppermute | solution.py:31
  16.3 0.3 %collective-permute-start.8 = (f16[200,256]{1,0:T(8,128)(2,1)S(1)}, f16[200,256]{1,0:T(8,128)(2,1)S(1)}, u32[]{:S(2)}, u32[]{:S(2)}) collective-permute-start(f16[200,256]{1,0:T(8,128)(2,1)S(1)} %convert_element_type.50), channel_id=1, source_target_pairs={{0,4},{4,0},{8,12},{12,8},{16,20},{20,16},{24,28},{28,24},{1,5},{5... | collective-permute-start | bytes 307208 | tf_op jit(solution)/shard_map/ppermute | solution.py:31
  16.7 0.4 %shard_map.74 = f32[128,256]{1,0:T(8,128)S(1)} custom-call(bf16[128,256]{1,0:T(8,128)(2,1)S(1)} %get-tuple-element.28.a_ref, bf16[64,256]{1,0:T(8,128)(2,1)S(1)} %get-tuple-element.21.b_ref, f32[256,256]{1,0:T(8,128)S(1)} %get-tuple-element.32.gc_ref, f32[128,256]{1,0:T(8,128)S(1)} %get-tuple-element.34.slab_ref), custom_call_target="tpu_custom_call" | custom-call | flops 67108864 | tf_op jit(solution)/shard_map/pallas_call | solution.py:35
  17.1 1.8 %collective-permute-start.10 = (f32[128,256]{1,0:T(8,128)S(1)}, f32[128,256]{1,0:T(8,128)S(1)}, u32[]{:S(2)}, u32[]{:S(2)}) collective-permute-start(f32[128,256]{1,0:T(8,128)S(1)} %shard_map.74), channel_id=1, source_target_pairs={{0,2},{1,3},{2,0},{3,1},{4,6},{5,7},{6,4},{7,5},{8,10},{9,11},{10,... | collective-permute-start | bytes 393224 | tf_op jit(solution)/shard_map/ppermute | solution.py:31
  18.9 0.9 %collective-permute-done.6 = f16[200,256]{1,0:T(8,128)(2,1)S(1)} collective-permute-done((f16[200,256]{1,0:T(8,128)(2,1)S(1)}, f16[200,256]{1,0:T(8,128)(2,1)S(1)}, u32[]{:S(2)}, u32[]{:S(2)}) %collective-permute-start.6) | collective-permute-done | bytes 102432 | tf_op jit(solution)/shard_map/ppermute | solution.py:31
  19.8 1.4 %collective-permute-done.7 = f16[200,256]{1,0:T(8,128)(2,1)S(1)} collective-permute-done((f16[200,256]{1,0:T(8,128)(2,1)S(1)}, f16[200,256]{1,0:T(8,128)(2,1)S(1)}, u32[]{:S(2)}, u32[]{:S(2)}) %collective-permute-start.7) | collective-permute-done | bytes 102432 | tf_op jit(solution)/shard_map/ppermute | solution.py:31
  21.2 0.0 collective-permute-done.8
  21.2 0.1 select_convert_fusion
  21.3 3.8 %collective-permute-start.9 = (f16[200,256]{1,0:T(8,128)(2,1)S(1)}, f16[200,256]{1,0:T(8,128)(2,1)S(1)}, u32[]{:S(2)}, u32[]{:S(2)}) collective-permute-start(f16[200,256]{1,0:T(8,128)(2,1)S(1)} %select_convert_fusion), channel_id=1, source_target_pairs={{0,24},{4,28},{8,16},{12,20},{16,8},{20,12},{24,0},{28,4},{1,25},{... | collective-permute-start | bytes 307208 | tf_op jit(solution)/shard_map/ppermute | solution.py:31
  25.1 0.0 collective-permute-done.10
  25.2 0.1 collective-permute-start.11
  25.3 2.7 %collective-permute-done.9 = f16[200,256]{1,0:T(8,128)(2,1)S(1)} collective-permute-done((f16[200,256]{1,0:T(8,128)(2,1)S(1)}, f16[200,256]{1,0:T(8,128)(2,1)S(1)}, u32[]{:S(2)}, u32[]{:S(2)}) %collective-permute-start.9) | collective-permute-done | bytes 102432 | tf_op jit(solution)/shard_map/ppermute | solution.py:31
  28.0 0.7 %shard_map.75 = (f32[128,256]{1,0:T(8,128)}, f32[128,256]{1,0:T(8,128)}, f32[64,256]{1,0:T(8,128)}) custom-call(f32[200,256]{1,0:T(8,128)S(1)} %multiply_add_fusion.v_ref, f32[128,256]{1,0:T(8,128)S(1)} %add.33.pa_ref, f32[128,256]{1,0:T(8,128)S(1)} %collective-permute-done.11.in_ref), custom_call_target="tpu_custom_call" | custom-call | tf_op jit(solution)/shard_map/pallas_call | solution.py:370
  (19 shorter events, 0.2 us)
Async XLA Ops:
  0.6 3.6 %copy-start.3 = (bf16[64,256]{1,0:T(8,128)(2,1)S(1)}, bf16[64,256]{1,0:T(8,128)(2,1)}, u32[]{:S(2)}) copy-start(bf16[64,256]{1,0:T(8,128)(2,1)} %b_in.1) | copy-start | bytes 98308
  0.6 3.6 %copy-start.2 = (bf16[128,256]{1,0:T(8,128)(2,1)S(1)}, bf16[128,256]{1,0:T(8,128)(2,1)}, u32[]{:S(2)}) copy-start(bf16[128,256]{1,0:T(8,128)(2,1)} %a_in.1) | copy-start | bytes 196612
  0.7 3.8 %copy-start = (bf16[128,64,512]{2,1,0:T(8,128)(2,1)S(1)}, bf16[128,64,512]{2,1,0:T(8,128)(2,1)}, u32[]{:S(2)}) copy-start(bf16[128,64,512]{2,1,0:T(8,128)(2,1)} %x_ref.5) | copy-start | bytes 25165828
  0.7 6.7 %collective-permute-start.2 = (bf16[128,256]{1,0:T(8,128)(2,1)}, bf16[128,256]{1,0:T(8,128)(2,1)S(1)}, u32[]{:S(2)}, u32[]{:S(2)}) collective-permute-start(bf16[128,256]{1,0:T(8,128)(2,1)} %c0.1), channel_id=1, source_target_pairs={{0,2},{1,3},{2,0},{3,1},{4,6},{5,7},{6,4},{7,5},{8,10},{9,11},{10,... | collective-permute-start | bytes 196616 | tf_op jit(solution)/shard_map/ppermute | solution.py:31
  3.7 6.6 %collective-permute-start.3 = (bf16[128,256]{1,0:T(8,128)(2,1)}, bf16[128,256]{1,0:T(8,128)(2,1)S(1)}, u32[]{:S(2)}, u32[]{:S(2)}) collective-permute-start(bf16[128,256]{1,0:T(8,128)(2,1)} %c0.1), channel_id=1, source_target_pairs={{0,3},{1,2},{2,1},{3,0},{4,7},{5,6},{6,5},{7,4},{8,11},{9,10},{10,... | collective-permute-start | bytes 196616 | tf_op jit(solution)/shard_map/ppermute | solution.py:31
  3.7 6.6 %collective-permute-start.4 = (bf16[128,256]{1,0:T(8,128)(2,1)}, bf16[128,256]{1,0:T(8,128)(2,1)S(1)}, u32[]{:S(2)}, u32[]{:S(2)}) collective-permute-start(bf16[128,256]{1,0:T(8,128)(2,1)} %c0.1), channel_id=1, source_target_pairs={{0,1},{1,0},{2,3},{3,2},{4,5},{5,4},{6,7},{7,6},{8,9},{9,8},{10,11... | collective-permute-start | bytes 196616 | tf_op jit(solution)/shard_map/ppermute | solution.py:31
  3.9 2.1 %collective-permute-start = (bf16[64,256]{1,0:T(8,128)(2,1)}, bf16[64,256]{1,0:T(8,128)(2,1)S(1)}, u32[]{:S(2)}, u32[]{:S(2)}) collective-permute-start(bf16[64,256]{1,0:T(8,128)(2,1)} %b_in.1), channel_id=1, source_target_pairs={{0,1},{1,0},{2,3},{3,2},{4,5},{5,4},{6,7},{7,6},{8,9},{9,8},{10,11... | collective-permute-start | bytes 98312 | tf_op jit(solution)/shard_map/ppermute | solution.py:31
  5.8 1.6 %collective-permute-start.1 = (f32[256,256]{1,0:T(8,128)S(1)}, f32[256,256]{1,0:T(8,128)S(1)}, u32[]{:S(2)}, u32[]{:S(2)}) collective-permute-start(f32[256,256]{1,0:T(8,128)S(1)} %shard_map.69), channel_id=1, source_target_pairs={{0,1},{1,0},{2,3},{3,2},{4,5},{5,4},{6,7},{7,6},{8,9},{9,8},{10,11... | collective-permute-start | bytes 786440 | tf_op jit(solution)/shard_map/ppermute | solution.py:31
  6.0 4.3 %copy-start.1 = (bf16[128,256]{1,0:T(8,128)(2,1)S(1)}, bf16[128,256]{1,0:T(8,128)(2,1)}, u32[]{:S(2)}) copy-start(bf16[128,256]{1,0:T(8,128)(2,1)} %c0.1) | copy-start | bytes 196612
  7.6 5.4 %collective-permute-start.5 = (f16[136,256]{1,0:T(8,128)(2,1)S(1)}, f16[136,256]{1,0:T(8,128)(2,1)S(1)}, u32[]{:S(2)}, u32[]{:S(2)}) collective-permute-start(f16[136,256]{1,0:T(8,128)(2,1)S(1)} %convert_element_type.48), channel_id=1, source_target_pairs={{0,2},{1,3},{2,0},{3,1},{4,6},{5,7},{6,4},{7,5},{8,10},{9,11},{10,... | collective-permute-start | bytes 208904 | tf_op jit(solution)/shard_map/ppermute | solution.py:31
  13.1 6.7 %collective-permute-start.6 = (f16[200,256]{1,0:T(8,128)(2,1)S(1)}, f16[200,256]{1,0:T(8,128)(2,1)S(1)}, u32[]{:S(2)}, u32[]{:S(2)}) collective-permute-start(f16[200,256]{1,0:T(8,128)(2,1)S(1)} %convert_element_type.50), channel_id=1, source_target_pairs={{0,12},{4,8},{8,4},{12,0},{16,28},{20,24},{24,20},{28,16},{1,13},{... | collective-permute-start | bytes 307208 | tf_op jit(solution)/shard_map/ppermute | solution.py:31
  15.9 5.3 %collective-permute-start.7 = (f16[200,256]{1,0:T(8,128)(2,1)S(1)}, f16[200,256]{1,0:T(8,128)(2,1)S(1)}, u32[]{:S(2)}, u32[]{:S(2)}) collective-permute-start(f16[200,256]{1,0:T(8,128)(2,1)S(1)} %convert_element_type.50), channel_id=1, source_target_pairs={{0,8},{4,12},{8,0},{12,4},{16,24},{20,28},{24,16},{28,20},{1,9},{5... | collective-permute-start | bytes 307208 | tf_op jit(solution)/shard_map/ppermute | solution.py:31
  16.3 4.9 %collective-permute-start.8 = (f16[200,256]{1,0:T(8,128)(2,1)S(1)}, f16[200,256]{1,0:T(8,128)(2,1)S(1)}, u32[]{:S(2)}, u32[]{:S(2)}) collective-permute-start(f16[200,256]{1,0:T(8,128)(2,1)S(1)} %convert_element_type.50), channel_id=1, source_target_pairs={{0,4},{4,0},{8,12},{12,8},{16,20},{20,16},{24,28},{28,24},{1,5},{5... | collective-permute-start | bytes 307208 | tf_op jit(solution)/shard_map/ppermute | solution.py:31
  17.1 8.1 %collective-permute-start.10 = (f32[128,256]{1,0:T(8,128)S(1)}, f32[128,256]{1,0:T(8,128)S(1)}, u32[]{:S(2)}, u32[]{:S(2)}) collective-permute-start(f32[128,256]{1,0:T(8,128)S(1)} %shard_map.74), channel_id=1, source_target_pairs={{0,2},{1,3},{2,0},{3,1},{4,6},{5,7},{6,4},{7,5},{8,10},{9,11},{10,... | collective-permute-start | bytes 393224 | tf_op jit(solution)/shard_map/ppermute | solution.py:31
  21.3 6.6 %collective-permute-start.9 = (f16[200,256]{1,0:T(8,128)(2,1)S(1)}, f16[200,256]{1,0:T(8,128)(2,1)S(1)}, u32[]{:S(2)}, u32[]{:S(2)}) collective-permute-start(f16[200,256]{1,0:T(8,128)(2,1)S(1)} %select_convert_fusion), channel_id=1, source_target_pairs={{0,24},{4,28},{8,16},{12,20},{16,8},{20,12},{24,0},{28,4},{1,25},{... | collective-permute-start | bytes 307208 | tf_op jit(solution)/shard_map/ppermute | solution.py:31
  25.2 2.8 %collective-permute-start.11 = (f32[128,256]{1,0:T(8,128)S(1)}, f32[128,256]{1,0:T(8,128)S(1)}, u32[]{:S(2)}, u32[]{:S(2)}) collective-permute-start(f32[128,256]{1,0:T(8,128)S(1)} %add.33.pa_ref), channel_id=1, source_target_pairs={{0,1},{1,0},{2,3},{3,2},{4,5},{5,4},{6,7},{7,6},{8,9},{9,8},{10,11... | collective-permute-start | bytes 393224 | tf_op jit(solution)/shard_map/ppermute | solution.py:31
